TPU v7x, 32 devices: a whole 2x2x4 slice. The times are simulated.
32 devices in a mesh: groups: 2 (over y), leaf: 4 (over z), chan: 4 (over x, core).
Axes of the slice: x: 2, y: 2, z: 4, core: 2. Of those that a mesh axis runs over, the one named last changes fastest.
Arguments:
- currents: bfloat16 [64, 32, 256], P(('groups', 'chan'), 'leaf'), parts along dimension 0, may hold values from -6 to 6
- counts: int32 [64], P(('groups', 'leaf')), parts along dimension 0, may hold values from 64 to 256
- near_list: int32 [64, 6], P(('groups', 'leaf')), parts along dimension 0, may hold values from 0 to 31, as said below
- m2l_list: int32 [8, 16], P(('groups', 'leaf')), parts along dimension 0, may hold values from 0 to 3
- m2l_type: int32 [8, 16], P(('groups', 'leaf')), parts along dimension 0, may hold values from 0 to 63
- interp: bfloat16 [64, 256, 216], P(('groups', 'leaf')), parts along dimension 0, may hold values from -0.375 to 0.375
- compress: bfloat16 [4, 216, 64], replicated, may hold values from -0.4375 to 0.4375
- m2m: bfloat16 [4, 8, 64, 64], replicated, may hold values from -0.25 to 0.25
- m2l: bfloat16 [4, 64, 64, 64], replicated, may hold values from -0.1875 to 0.1875
- near_tiles: bfloat16 [64, 6, 256, 256], P(('groups', 'leaf')), parts along dimension 0, may hold values from -0.15625 to 0.15625
- jacobi: bfloat16 [64, 256, 256], P(('groups', 'leaf')), parts along dimension 0
Outputs:
- applied: float32 [64, 32, 256], P(('groups', 'chan'), 'leaf'), parts along dimension 0
There are 2 independent parts, one for each index of `groups`. A program takes and returns all parts, laid end to end along the dimension named above; an argument that names none is the same for every part. Nothing has to cross between parts.
Inputs may be any that keep to these rules, and one draw needn't show every extreme that they name: near_list[l, 0] = l, and every entry lies within 8 leaves of l.
All inputs are finite; a program needn't handle non-finite values.
Results may differ from a plain program's by a relative error of at most 0.0035.
Values may be sent and summed in bfloat16 or wider, within the bound.
No kernel may reach another device: no remote copies, remote signals or barrier semaphores. Data moves between devices by JAX's collectives and lax.ppermute only.
A program may use at most 64 MiB of HBM per device.

v0:
```python
import jax
import jax.numpy as jnp
from jax import lax
from jax.sharding import PartitionSpec as P

INC = 8


def extended(block, sides, width):
    for axis, dim in sides:
        count = lax.axis_size(axis)
        forward = [(i, i + 1) for i in range(count - 1)]
        backward = [(target, source) for source, target in forward]
        low = lax.ppermute(
            lax.slice_in_dim(block, block.shape[dim] - width, None, axis=dim), axis, forward
        )
        high = lax.ppermute(lax.slice_in_dim(block, 0, width, axis=dim), axis, backward)
        block = jnp.concatenate([low, block, high], axis=dim)
    return block


def body(
    currents, counts, near_list, m2l_list, m2l_type, interp, compress, m2m, m2l, near_tiles, jacobi
):
    combos_here = currents.shape[0]
    per_dev = currents.shape[1]
    position = lax.axis_index("leaf")
    channel = lax.axis_index("chan") * combos_here // INC
    comp = lax.dynamic_index_in_dim(compress, channel, 0, keepdims=False)
    trans = lax.dynamic_index_in_dim(m2m, channel, 0, keepdims=False)
    table = lax.dynamic_index_in_dim(m2l, channel, 0, keepdims=False)
    slots = jnp.arange(currents.shape[2], dtype=jnp.int32)
    live = slots[None, :] < counts[:, None]
    masked = jnp.where(live[None], currents, jnp.zeros_like(currents))
    padded = extended(masked, (("leaf", 1),), per_dev)
    local_ids = near_list - (position * per_dev - per_dev)
    beside = jnp.take(padded, local_ids, axis=1)
    near = jnp.einsum("lkvu,qlku->qlv", near_tiles, beside, preferred_element_type=jnp.float32)
    nodes = jnp.einsum("qlu,lun->qln", masked, interp, preferred_element_type=jnp.float32).astype(
        jnp.bfloat16
    )
    moments = jnp.einsum("qln,nr->qlr", nodes, comp, preferred_element_type=jnp.float32).astype(
        jnp.bfloat16
    )
    every_leaf = lax.all_gather(moments, "leaf", axis=1, tiled=True)
    grouped = every_leaf.reshape(combos_here, every_leaf.shape[1] // 8, 8, every_leaf.shape[2])
    boxes = jnp.einsum("qpsr,srt->qpt", grouped, trans, preferred_element_type=jnp.float32).astype(
        jnp.bfloat16
    )
    sources = jnp.take(boxes, m2l_list, axis=1)
    mats = jnp.take(table, m2l_type, axis=0)
    local = jnp.einsum("qpkr,pkrt->qpt", sources, mats, preferred_element_type=jnp.float32).astype(
        jnp.bfloat16
    )
    leaf_local = jnp.einsum("qpt,srt->qpsr", local, trans, preferred_element_type=jnp.float32)
    leaf_local = leaf_local.reshape(combos_here, per_dev, leaf_local.shape[3]).astype(jnp.bfloat16)
    far_nodes = jnp.einsum(
        "qlr,nr->qln", leaf_local, comp, preferred_element_type=jnp.float32
    ).astype(jnp.bfloat16)
    far = jnp.einsum("qln,lun->qlu", far_nodes, interp, preferred_element_type=jnp.float32)
    total = (near + far).astype(jnp.bfloat16)
    applied = jnp.einsum("lvu,qlu->qlv", jacobi, total, preferred_element_type=jnp.float32)
    return jnp.where(live[None], applied, jnp.zeros_like(applied))


def solution(mesh):
    placed = (
        P(("groups", "chan"), "leaf", None),
        P(("groups", "leaf")),
        P(("groups", "leaf"), None),
        P(("groups", "leaf"), None),
        P(("groups", "leaf"), None),
        P(("groups", "leaf"), None, None),
        P(),
        P(),
        P(),
        P(("groups", "leaf"), None, None, None),
        P(("groups", "leaf"), None, None),
    )
    return jax.shard_map(
        body,
        mesh=mesh,
        in_specs=placed,
        out_specs=P(("groups", "chan"), "leaf", None),
        check_vma=False,
    )
```

profile of v0, /device:TPU:0, one launch (start us, length us, event | category | flops | bytes accessed | tf_op | source)
XLA Modules:
  0.0 38.6 jit_solution(2345306908190223081)
XLA Ops:
  0.0 0.0 copy-start
  0.0 0.0 copy-start.1
  0.0 0.9 %iota_compare_fusion = pred[8,256]{1,0:T(8,128)(4,1)S(1)} fusion(s32[8]{0:T(128)} %param.12), kind=kLoop, calls=%fused_computation.46 | loop fusion | flops 2048 | bytes 2080 | tf_op jit(solution)/shard_map/lt | solution.py:33
  0.9 0.8 %copy_select_fusion = bf16[8,8,256]{2,0,1:T(8,128)(2,1)S(1)} fusion(bf16[8,8,256]{2,1,0:T(8,128)(2,1)} %param.11, pred[8,256]{1,0:T(8,128)(4,1)S(1)} %iota_compare_fusion), kind=kLoop, calls=%fused_computation.40 | loop fusion | flops 16384 | bytes 67584 | tf_op jit(solution)/shard_map/jit(_where)/select_n | solution.py:34
  1.6 4.9 %collective-permute-start = (bf16[8,8,256]{2,0,1:T(8,128)(2,1)S(1)}, bf16[8,8,256]{2,0,1:T(8,128)(2,1)S(1)}, u32[]{:S(2)}, u32[]{:S(2)}) collective-permute-start(bf16[8,8,256]{2,0,1:T(8,128)(2,1)S(1)} %copy_select_fusion), channel_id=1, source_target_pairs={{0,4},{4,8},{8,12},{1,5},{5,9},{9,13},{2,6},{6,10},{10,14},{3,7},{... | collective-permute-start | bytes 98312 | tf_op jit(solution)/shard_map/ppermute | solution.py:14
  6.6 1.3 %collective-permute-start.1 = (bf16[8,8,256]{2,0,1:T(8,128)(2,1)S(1)}, bf16[8,8,256]{2,0,1:T(8,128)(2,1)S(1)}, u32[]{:S(2)}, u32[]{:S(2)}) collective-permute-start(bf16[8,8,256]{2,0,1:T(8,128)(2,1)S(1)} %copy_select_fusion), channel_id=1, source_target_pairs={{4,0},{8,4},{12,8},{5,1},{9,5},{13,9},{6,2},{10,6},{14,10},{7,3},{... | collective-permute-start | bytes 98312 | tf_op jit(solution)/shard_map/ppermute | solution.py:17
  7.9 0.7 %fusion.44 = s32[16]{0:T(128)S(1)} fusion(s32[1,16]{1,0:T(1,128)} %param.15), kind=kLoop, calls=%fused_computation.61 | loop fusion | flops 48 | bytes 128 | tf_op jit(solution)/shard_map/jit(_take)/broadcast_in_dim | solution.py:51
  8.6 0.7 %fusion.45 = s32[16]{0:T(128)S(1)} fusion(s32[1,16]{1,0:T(1,128)} %param.14), kind=kLoop, calls=%fused_computation.62 | loop fusion | flops 48 | bytes 128 | tf_op jit(solution)/shard_map/jit(_take)/broadcast_in_dim | solution.py:50
  9.2 0.7 %and_bitcast_fusion = (pred[16]{0:T(512)(128)(4,1)S(1)}, pred[16]{0:T(512)(128)(4,1)S(1)}) fusion(s32[1,16]{1,0:T(1,128)} %param.14, s32[1,16]{1,0:T(1,128)} %param.15), kind=kLoop, calls=%fused_computation.53 | loop fusion | flops 192 | bytes 160 | tf_op jit(solution)/shard_map/jit(_take)/reduce_and | solution.py:50
  9.9 1.5 %fusion.46 = bf16[8,8,216]{2,1,0:T(8,128)(2,1)S(1)} fusion(bf16[8,8,256]{2,0,1:T(8,128)(2,1)S(1)} %copy_select_fusion, bf16[8,256,216]{1,2,0:T(8,128)(2,1)} %param.16), kind=kOutput, calls=%fused_computation.63 | convolution fusion | flops 7077888 | bytes 945152 | tf_op jit(solution)/shard_map/qlu,lun->qln/dot_general | solution.py:39
  11.4 1.3 %dynamic-slice_bitcast_fusion = bf16[64,64,64]{2,1,0:T(8,128)(2,1)S(1)} fusion(bf16[4,64,64,64]{3,2,1,0:T(8,128)(2,1)} %param.19, s32[]{:T(128)S(6)} %select_n.91), kind=kLoop, calls=%fused_computation.16 | loop fusion | bytes 1048580 | tf_op jit(solution)/shard_map/jit(dynamic_index_in_dim)/squeeze | solution.py:31
  12.7 0.9 %convolution_convert_fusion.1 = bf16[8,8,64]{2,1,0:T(8,128)(2,1)S(1)} fusion(bf16[8,8,216]{2,1,0:T(8,128)(2,1)S(1)} %fusion.46, bf16[4,216,64]{1,2,0:T(8,128)(2,1)} %param.17, s32[]{:T(128)S(6)} %select_n.91), kind=kOutput, calls=%fused_computation.10 | convolution fusion | flops 1773568 | bytes 68612 | tf_op jit(solution)/shard_map/qln,nr->qlr/dot_general | solution.py:42
  13.6 13.3 %all_gather.3 = bf16[8,32,64]{2,1,0:T(8,128)(2,1)S(1)} all-gather(bf16[8,8,64]{2,1,0:T(8,128)(2,1)S(1)} %convolution_convert_fusion.1), channel_id=1, replica_groups=mesh['groups'=2,'leaf'=4,'chan'=4] {'leaf'}, dimensions={1}, use_global_device_ids=true | all-gather | bytes 40960 | tf_op jit(solution)/shard_map/all_gather | solution.py:45
  26.9 0.6 %gather_fusion.1 = bf16[16,64,64]{2,1,0:T(8,128)(2,1)S(1)} fusion(bf16[64,64,64]{2,1,0:T(8,128)(2,1)S(1)} %dynamic-slice_bitcast_fusion, s32[1024]{0:T(1024)S(1)} %pad_clamp_fusion.1), kind=kCustom, calls=%fused_computation.1 | custom fusion | bytes 262208 | tf_op jit(solution)/shard_map/jit(_take)/gather | solution.py:51
  27.5 1.1 %fusion.3 = bf16[8,4,64]{2,0,1:T(8,128)(2,1)S(1)} fusion(bf16[4,8,64,64]{3,2,1,0:T(8,128)(2,1)} %param.18, s32[]{:T(128)S(6)} %select_n.91, bf16[8,4,8,64]{3,2,1,0:T(8,128)(2,1)S(1)} %bitcast.90), kind=kOutput, calls=%fused_computation.12 | convolution fusion | flops 2099200 | bytes 167940 | tf_op jit(solution)/shard_map/qpsr,srt->qpt/dot_general | solution.py:47
  28.6 0.6 %gather_fusion.2 = bf16[16,8,64]{2,1,0:T(8,128)(2,1)S(1)} fusion(bf16[8,4,64]{2,0,1:T(8,128)(2,1)S(1)} %fusion.3, s32[1024]{0:T(1024)S(1)} %pad_clamp_fusion), kind=kCustom, calls=%fused_computation.2 | custom fusion | bytes 32832 | tf_op jit(solution)/shard_map/jit(_take)/gather | solution.py:50
  29.2 1.3 %fusion.6 = bf16[8,8,64]{2,0,1:T(8,128)(2,1)S(1)} fusion(bf16[16,64,64]{2,1,0:T(8,128)(2,1)S(1)} %gather_fusion.1, pred[16]{0:T(512)(128)(4,1)S(1)} %get-tuple-element.8, bf16[4,8,64,64]{3,2,1,0:T(8,128)(2,1)} %param.18, s32[]{:T(128)S(6)} %select_n.91, bf16[16,8,64]{2,1,0:T(8,128)(2,1)S(1)} %gather_fusion.2, pred[16]{0:T(512)(128)(4,1)S(1)} %get-tuple-element.7), kind=kOutput, calls=%fused_computation.17 | convolution fusion | flops 1647104 | bytes 286756 | tf_op jit(solution)/shard_map/qpt,srt->qpsr/dot_general | solution.py:55
  30.5 0.9 %convolution_convert_fusion = bf16[8,8,216]{2,1,0:T(8,128)(2,1)S(1)} fusion(bf16[4,216,64]{1,2,0:T(8,128)(2,1)} %param.17, s32[]{:T(128)S(6)} %select_n.91, bf16[8,8,64]{2,0,1:T(8,128)(2,1)S(1)} %fusion.6), kind=kOutput, calls=%fused_computation.8 | convolution fusion | flops 1783296 | bytes 68612 | tf_op jit(solution)/shard_map/qlr,nr->qln/dot_general | solution.py:57
  31.4 0.7 %compare_and_fusion = (pred[8,6]{1,0:T(8,128)(4,1)S(1)}, s32[8,6]{1,0:T(8,128)S(1)}) fusion(s32[8,6]{1,0:T(8,128)} %param.13, s32[]{:T(128)S(6)} %sub.13), kind=kLoop, calls=%fused_computation.50 | loop fusion | flops 336 | bytes 436 | tf_op jit(solution)/shard_map/jit(_take)/and | solution.py:37
  32.1 0.1 reshape.91
  32.2 0.0 collective-permute-done
  32.2 0.0 collective-permute-done.1
  32.3 0.6 %gather_fusion = bf16[48,8,256]{2,1,0:T(8,128)(2,1)S(1)} fusion(bf16[8,24,256]{2,0,1:T(8,128)(2,1)S(1)} %pad_maximum_fusion, s32[1024]{0:T(1024)S(1)} %pad_clamp_fusion.2), kind=kCustom, calls=%fused_computation | custom fusion | bytes 393408 | tf_op jit(solution)/shard_map/jit(_take)/gather | solution.py:37
  32.9 4.5 %convolution_bitcast_fusion = f32[8,8,256]{2,1,0:T(8,128)S(1)} fusion(bf16[8,6,256,256]{3,2,1,0:T(8,128)(2,1)} %param.20, bf16[8,6,8,256]{3,2,1,0:T(8,128)(2,1)S(1)} %bitcast.89, pred[8,6]{1,0:T(8,128)(4,1)S(1)} %get-tuple-element.5), kind=kOutput, calls=%fused_computation.6 | convolution fusion | flops 50429952 | bytes 6553648 | tf_op jit(solution)/shard_map/lkvu,qlku->qlv/dot_general | solution.py:38
  37.4 0.0 copy-done
  37.4 0.0 copy-done.1
  37.4 0.5 %fusion = f32[8,8,256]{2,0,1:T(8,128)S(1)} fusion(bf16[8,256,256]{2,1,0:T(8,128)(2,1)S(1)} %copy-done, f32[8,8,256]{2,1,0:T(8,128)S(1)} %convolution_bitcast_fusion, bf16[8,256,216]{1,2,0:T(8,128)(2,1)S(1)} %copy-done.1, bf16[8,8,216]{2,1,0:T(8,128)(2,1)S(1)} %convolution_convert_fusion, pred[8,256]{1,0:T(8,128)(4,1)S(1)} %iota_compare_fusion), kind=kOutput, calls=%fused_computation.4 | convolution fusion | flops 15515648 | bytes 2094080 | tf_op jit(solution)/shard_map/lvu,qlu->qlv/dot_general | solution.py:62
  37.9 0.7 %copy.16 = f32[8,8,256]{2,1,0:T(8,128)} copy(f32[8,8,256]{2,0,1:T(8,128)S(1)} %fusion) | data formatting | bytes 131072 | tf_op jit(solution)/shard_map/jit(_where)/select_n | solution.py:63
  (4 shorter events, 0.0 us)
Async XLA Ops:
  0.0 37.4 %copy-start = (bf16[8,256,256]{2,1,0:T(8,128)(2,1)S(1)}, bf16[8,256,256]{2,1,0:T(8,128)(2,1)}, u32[]{:S(2)}) copy-start(bf16[8,256,256]{2,1,0:T(8,128)(2,1)} %param.21) | copy-start | bytes 3145732
  0.0 37.4 %copy-start.1 = (bf16[8,256,216]{1,2,0:T(8,128)(2,1)S(1)}, bf16[8,256,216]{1,2,0:T(8,128)(2,1)}, u32[]{:S(2)}) copy-start(bf16[8,256,216]{1,2,0:T(8,128)(2,1)} %param.16) | copy-start | bytes 2654212
  1.6 30.6 %collective-permute-start = (bf16[8,8,256]{2,0,1:T(8,128)(2,1)S(1)}, bf16[8,8,256]{2,0,1:T(8,128)(2,1)S(1)}, u32[]{:S(2)}, u32[]{:S(2)}) collective-permute-start(bf16[8,8,256]{2,0,1:T(8,128)(2,1)S(1)} %copy_select_fusion), channel_id=1, source_target_pairs={{0,4},{4,8},{8,12},{1,5},{5,9},{9,13},{2,6},{6,10},{10,14},{3,7},{... | collective-permute-start | bytes 98312 | tf_op jit(solution)/shard_map/ppermute | solution.py:14
  6.6 25.6 %collective-permute-start.1 = (bf16[8,8,256]{2,0,1:T(8,128)(2,1)S(1)}, bf16[8,8,256]{2,0,1:T(8,128)(2,1)S(1)}, u32[]{:S(2)}, u32[]{:S(2)}) collective-permute-start(bf16[8,8,256]{2,0,1:T(8,128)(2,1)S(1)} %copy_select_fusion), channel_id=1, source_target_pairs={{4,0},{8,4},{12,8},{5,1},{9,5},{13,9},{6,2},{10,6},{14,10},{7,3},{... | collective-permute-start | bytes 98312 | tf_op jit(solution)/shard_map/ppermute | solution.py:17
where the time goes:
time: 39.1 us; the launch traced here: 38.6 us
  blocking collectives  13.3 us (34%)
  matrix products  10.8 us (28%)
  starting transfers between devices  6.22 us (16%)
  other arithmetic  4.37 us (11%)
  local copies, waits for them, and re-layouts  3.82 us (10%)
    all_gather x1, blocking collectives, body(): every_leaf = lax.all_gather(moments, 'leaf', axis=1, tiled=True)  13.3 us
    ppermute x1, starting transfers between devices, extended(): lax.ppermute(lax.slice_in_dim(block, block.shape[dim] - width, None, axis...  4.93 us
    dot_general x1, matrix products, body(): jnp.einsum('lkvu,qlku->qlv', near_tiles, beside, preferred_element_type=j...  4.51 us
    dot_general x1, matrix products, body(): jnp.einsum('qlu,lun->qln', masked, interp, preferred_element_type=jnp.flo...  1.5 us
    dot_general x1, matrix products, body(): jnp.einsum('qpt,srt->qpsr', local, trans, preferred_element_type=jnp.floa...  1.32 us
    squeeze x1, local copies, waits for them, and re-layouts, body(): table = lax.dynamic_index_in_dim(m2l, channel, 0, keepdims=False)  1.31 us
    ppermute x1, starting transfers between devices, extended(): lax.ppermute(lax.slice_in_dim(block, 0, width, axis=dim), axis, backward)  1.29 us
    dot_general x1, matrix products, body(): jnp.einsum('qpsr,srt->qpt', grouped, trans, preferred_element_type=jnp.fl...  1.12 us
  transfers between devices with their start and end apart: 2, of which 0 were waited for; matrix products, arithmetic and copies ran while one was open for 29% of the time, Pallas kernels for 0%

commit v1 on v0

v1 whole, which is shorter than its diff:
```python
import jax
import jax.numpy as jnp
from jax import lax
from jax.experimental import pallas as pl
from jax.experimental.pallas import tpu as pltpu
from jax.sharding import PartitionSpec as P

F32 = jnp.float32
BF16 = jnp.bfloat16
NT = (((1,), (1,)), ((), ()))
VMEM = pl.BlockSpec(memory_space=pltpu.VMEM)
SMEM = pl.BlockSpec(memory_space=pltpu.SMEM)
HBM = pl.BlockSpec(memory_space=pltpu.HBM)
COST = 2 * 10**9


def call(kernel, out_shape, in_specs, scratch=()):
    return pl.pallas_call(
        kernel,
        out_shape=out_shape,
        in_specs=in_specs,
        out_specs=jax.tree.map(lambda _: VMEM, out_shape),
        scratch_shapes=list(scratch),
        compiler_params=pltpu.CompilerParams(vmem_limit_bytes=16 << 20),
        cost_estimate=pl.CostEstimate(flops=COST, bytes_accessed=0, transcendentals=0),
    )


def in_hbm(*arrays):
    return [pltpu.with_memory_space_constraint(array, pltpu.HBM) for array in arrays]


def core_index():
    return lax.rem(lax.axis_index("chan"), 2)


def nt(a, b):
    return lax.dot_general(a, b, NT, preferred_element_type=F32)


def nn(a, b):
    return jnp.dot(a, b, preferred_element_type=F32)


def load_kernel(
    counts, own, interp_t, comp_t, m2m, interp_out, comp_out, m2m_out, mine, live, counts_s, own_s, sems
):
    base = lax.div(lax.axis_index("chan"), 2) * 2
    copies = [
        pltpu.make_async_copy(counts, counts_s, sems.at[0]),
        pltpu.make_async_copy(own, own_s, sems.at[1]),
        pltpu.make_async_copy(interp_t, interp_out, sems.at[2]),
        pltpu.make_async_copy(comp_t.at[pl.ds(base, 2)], comp_out, sems.at[3]),
        pltpu.make_async_copy(m2m.at[pl.ds(base, 2)], m2m_out, sems.at[4]),
    ]
    for copy in copies:
        copy.start()
    leaves, unknowns = live.shape
    slots = lax.broadcasted_iota(jnp.int32, (1, unknowns), 1)
    copies[0].wait()
    for leaf in range(leaves):
        live[leaf : leaf + 1] = jnp.where(slots < counts_s[leaf], 1.0, 0.0)
    copies[1].wait()
    mine[...] = jnp.swapaxes(own_s[...].astype(F32), 0, 1) * live[...][:, None, :]
    for copy in copies[2:]:
        copy.wait()


def box_kernel(mine, live, recv, interp_t, comp_t, m2m, packed, boxes):
    leaves, combos, unknowns = mine.shape
    rows = 2 * combos
    rank = m2m.shape[2]
    core = core_index()
    own = mine[...]
    other = jnp.swapaxes(recv[...].astype(F32), 0, 1) * live[...][:, None, :]
    both = jnp.concatenate([jnp.where(core == 1, other, own), own], axis=1).astype(BF16)
    packed[0:leaves] = both

    @pl.when(core == 0)
    def _():
        packed[leaves] = jnp.zeros((rows, unknowns), BF16)
        boxes[...] = jnp.zeros_like(boxes)

    @pl.when(core == 1)
    def _():
        nodes = jnp.concatenate(
            [nt(both[leaf], interp_t[leaf]).astype(BF16) for leaf in range(leaves)], axis=0
        )
        comp = comp_t[...].reshape(2 * rank, comp_t.shape[2])
        moments = nt(nodes, comp)
        row = lax.broadcasted_iota(jnp.int32, moments.shape, 0)
        lane = lax.broadcasted_iota(jnp.int32, moments.shape, 1)
        same = (lax.rem(row, rows) >= combos) == (lane >= rank)
        moments = jnp.where(same, moments, 0.0).astype(BF16)
        total = None
        for leaf in range(leaves):
            trans = jnp.concatenate([m2m[0, leaf], m2m[1, leaf]], axis=0)
            part = nn(moments[leaf * rows : (leaf + 1) * rows], trans)
            total = part if total is None else total + part
        wide = jnp.concatenate([total, jnp.zeros((rows, unknowns - rank), F32)], axis=1).astype(BF16)
        packed[leaves] = wide
        boxes[0] = wide


def local_kernel(near_list, m2l_type, mine, tiles, table, near, mats, own, sems):
    chan = lax.axis_index("chan")
    me = lax.axis_index("leaf")
    entries = mats.shape[0]
    leaves, neighbours = near_list.shape
    copies = [
        pltpu.make_async_copy(table.at[chan, m2l_type[0, k]], mats.at[k], sems.at[k])
        for k in range(entries)
    ]
    for copy in copies:
        copy.start()
    own[0:leaves] = mine[...]
    own[leaves] = jnp.zeros(own.shape[1:], F32)
    for leaf in range(leaves):
        total = None
        for k in range(neighbours):
            place = near_list[leaf, k] - me * leaves
            place = jnp.where(jnp.logical_and(place >= 0, place < leaves), place, leaves)
            part = nt(own[place].astype(BF16), tiles[leaf, k])
            total = part if total is None else total + part
        near[leaf] = total
    for copy in copies:
        copy.wait()


def final_kernel(
    near_list, m2l_list, live, here, swapped, boxes_own, mats, near, tiles, interp_t, comp_t, m2m, jacobi,
    out, beside, sources,
):
    core = core_index()
    me = lax.axis_index("leaf")
    count = sources.shape[0]
    entries = mats.shape[0]
    leaves, neighbours = near_list.shape
    combos, unknowns = near.shape[1:]
    rank = mats.shape[1]
    first = core == 0
    wide = leaves + 1

    def mine(block):
        block = block.astype(F32)
        return jnp.where(first, block[..., :combos, :], block[..., combos:, :])

    def received(start, size):
        return mine(jnp.where(first, here[start : start + size], swapped[start : start + size]))

    odd = lax.rem(me, 2) == 1
    box_a, box_b = received(leaves, 1)[0], received(wide + leaves, 1)[0]
    sources[0] = mine(jnp.where(first, swapped[2 * wide + count - 3], boxes_own[0]))
    sources[1] = jnp.where(odd, box_a, box_b)
    sources[count - 1] = jnp.where(odd, box_b, box_a)
    for s in range(2, count - 1):
        sources[s] = received(2 * wide + s - 2, 1)[0]

    low = received(0, leaves)
    high = received(wide, leaves)
    beside[0:leaves] = jnp.where(odd, low, high)
    beside[leaves : 2 * leaves] = jnp.where(odd, high, low)
    beside[2 * leaves] = jnp.zeros((combos, unknowns), F32)

    local = None
    for k in range(entries):
        step = lax.rem(me - m2l_list[0, k] + count, count)
        part = nn(sources[step][:, :rank].astype(BF16), mats[k])
        local = part if local is None else local + part
    local = local.astype(BF16)

    def near_of(leaf):
        total = near[leaf]
        for k in range(neighbours):
            place = near_list[leaf, k] - me * leaves
            place = jnp.where(
                place < 0, place + leaves, jnp.where(place >= leaves, place, 2 * leaves)
            )
            total = total + nt(beside[place].astype(BF16), tiles[leaf, k])
        return total

    half = leaves // 2
    sums = [near_of(leaf) for leaf in range(half)]
    leaf_local = jnp.concatenate(
        [nt(local, m2m[core, leaf]).astype(BF16) for leaf in range(leaves)], axis=0
    )
    sums += [near_of(leaf) for leaf in range(half, leaves)]
    far_nodes = nn(leaf_local, comp_t[core]).astype(BF16)
    for leaf in range(leaves):
        far = nn(far_nodes[leaf * combos : (leaf + 1) * combos], interp_t[leaf])
        applied = nt((sums[leaf] + far).astype(BF16), jacobi[leaf])
        out[:, leaf, :] = applied * live[leaf : leaf + 1]


def body(
    currents, counts, near_list, m2l_list, m2l_type, interp, compress, m2m, m2l, near_tiles, jacobi
):
    combos, leaves, unknowns = currents.shape
    nodes, rank = compress.shape[1:]
    entries = m2l_list.shape[1]
    n = lax.axis_size("leaf")
    chans = lax.axis_size("chan")
    axes = ("leaf", "chan")
    shape = jax.ShapeDtypeStruct

    def permute(value, target):
        moves = []
        for leaf in range(n):
            for c in range(0, chans, 2):
                for core in (0, 1):
                    to_leaf, to_core = target(leaf, core)
                    moves.append((leaf * chans + c + core, (to_leaf % n) * chans + c + to_core))
        return lax.ppermute(value, axes, moves)

    def swap(value):
        return permute(value, lambda leaf, core: (leaf, 1 - core))

    def gather(value, to_leaf):
        return permute(value, lambda leaf, core: (to_leaf(leaf), 0) if core else (leaf, 1))

    recv = swap(currents)
    interp_v, comp_v, m2m_v, mine, live = call(
        load_kernel,
        (
            shape((leaves, nodes, unknowns), BF16),
            shape((2, rank, nodes), BF16),
            shape((2, leaves, rank, rank), BF16),
            shape((leaves, combos, unknowns), F32),
            shape((leaves, unknowns), F32),
        ),
        [HBM] * 5,
        [
            pltpu.SMEM((leaves,), jnp.int32),
            pltpu.VMEM(currents.shape, BF16),
            pltpu.SemaphoreType.DMA((5,)),
        ],
    )(*in_hbm(counts, currents, jnp.swapaxes(interp, 1, 2), jnp.swapaxes(compress, 1, 2), m2m))
    packed, boxes = call(
        box_kernel,
        (
            shape((leaves + 1, 2 * combos, unknowns), BF16),
            shape((1, 2 * combos, unknowns), BF16),
        ),
        [VMEM] * 6,
    )(mine, live, recv, interp_v, comp_v, m2m_v)
    even_a = gather(packed, lambda leaf: leaf ^ 1)
    even_b = gather(packed, lambda leaf: leaf + 1 if leaf % 2 else leaf - 1)
    rest = [gather(boxes, lambda leaf, s=s: leaf + s) for s in range(2, n - 1)]
    near, mats = call(
        local_kernel,
        (shape((leaves, combos, unknowns), F32), shape((entries, rank, rank), BF16)),
        [SMEM, SMEM, VMEM, VMEM, HBM],
        [
            pltpu.VMEM((leaves + 1, combos, unknowns), F32),
            pltpu.SemaphoreType.DMA((entries,)),
        ],
    )(near_list, m2l_type, mine, near_tiles, *in_hbm(m2l))
    here = jnp.concatenate([even_a, even_b, *rest, boxes], axis=0)
    here, near = lax.optimization_barrier((here, near))
    swapped = swap(here)
    return call(
        final_kernel,
        shape(currents.shape, F32),
        [SMEM, SMEM] + [VMEM] * 11,
        [
            pltpu.VMEM((2 * leaves + 1, combos, unknowns), F32),
            pltpu.VMEM((n, combos, unknowns), F32),
        ],
    )(
        near_list, m2l_list, live, here, swapped, boxes, mats, near, near_tiles, interp_v, comp_v, m2m_v, jacobi,
    )


def solution(mesh):
    placed = (
        P(("groups", "chan"), "leaf", None),
        P(("groups", "leaf")),
        P(("groups", "leaf"), None),
        P(("groups", "leaf"), None),
        P(("groups", "leaf"), None),
        P(("groups", "leaf"), None, None),
        P(),
        P(),
        P(),
        P(("groups", "leaf"), None, None, None),
        P(("groups", "leaf"), None, None),
    )
    return jax.shard_map(
        body,
        mesh=mesh,
        in_specs=placed,
        out_specs=P(("groups", "chan"), "leaf", None),
        check_vma=False,
    )
```

time: 39.1 us -> 16.8 us (0.43)
  blocking collectives: 13.3 us -> 0 us
  matrix products: 10.8 us -> 0 us
  Pallas kernels: 0 us -> 8.95 us
  other arithmetic: 4.37 us -> 0.03 us
  local copies, waits for them, and re-layouts: 3.82 us -> 0.02 us
  waiting for transfers between devices: 0.01 us -> 2.19 us
  starting transfers between devices: 6.22 us -> 5.31 us
    all_gather x1 -> x0, blocking collectives: 13.3 us -> none  [body(): every_leaf = lax.all_gather(moments, 'leaf', axis=1, tiled=True)]
    dot_general x7 -> x0, matrix products: 10.8 us -> none  [the longest x1 4.51 us: body(): jnp.einsum('lkvu,qlku->qlv', near_tiles, beside, preferred_element_type=j...]
    pallas_call x0 -> x4, Pallas kernels: none -> 8.95 us  [the longest x1 4.32 us: body(): call(final_kernel, shape(currents.shape, F32), [SMEM, SMEM] + [VMEM] * 11...]
    ppermute x2 -> x5, waiting for transfers between devices: 0.01 us -> 2.19 us  [permute(): return lax.ppermute(value, axes, moves)]
    gather x3 -> x0, local copies, waits for them, and re-layouts: 1.75 us -> none  [the longest x1 0.6 us: body(): mats = jnp.take(table, m2l_type, axis=0)]
    broadcast_in_dim x2 -> x0, other arithmetic: 1.32 us -> none  [the longest x1 0.66 us: body(): mats = jnp.take(table, m2l_type, axis=0)]
    squeeze x1 -> x0, local copies, waits for them, and re-layouts: 1.31 us -> none  [body(): table = lax.dynamic_index_in_dim(m2l, channel, 0, keepdims=False)]
    ppermute x2 -> x5, starting transfers between devices: 6.22 us -> 5.31 us  [permute(): return lax.ppermute(value, axes, moves)]
  transfers between devices with their start and end apart: 2 -> 5, of which waited for: 0 -> 2; matrix products, arithmetic and copies ran while one was open for 29% -> 0% of each run, Pallas kernels for 0% -> 28%
where the time goes in v1:
time: 16.8 us; the launch traced here: 16.6 us
  Pallas kernels  8.95 us (53%)
  starting transfers between devices  5.31 us (32%)
  waiting for transfers between devices  2.19 us (13%)
    ppermute x5, starting transfers between devices, permute(): return lax.ppermute(value, axes, moves)  5.31 us
    pallas_call x1, Pallas kernels, body(): call(final_kernel, shape(currents.shape, F32), [SMEM, SMEM] + [VMEM] * 11...  4.32 us
    pallas_call x1, Pallas kernels, body(): call(local_kernel, (shape((leaves, combos, unknowns), F32), shape((entrie...  3.14 us
    ppermute x5, waiting for transfers between devices, permute(): return lax.ppermute(value, axes, moves)  2.19 us
    pallas_call x1, Pallas kernels, body(): call(load_kernel, (shape((leaves, nodes, unknowns), BF16), shape((2, rank...  1.45 us
  transfers between devices with their start and end apart: 5, of which 2 were waited for; matrix products, arithmetic and copies ran while one was open for 0% of the time, Pallas kernels for 28%

profile of v1, /device:TPU:0, one launch (start us, length us, event | category | flops | bytes accessed | tf_op | source)
XLA Modules:
  0.0 16.6 jit_solution(2367272968310182694)
XLA Ops:
  0.0 0.5 %collective-permute-start = (bf16[8,8,256]{2,1,0:T(8,128)(2,1)}, bf16[8,8,256]{2,1,0:T(8,128)(2,1)S(1)}, u32[]{:S(2)}, u32[]{:S(2)}) collective-permute-start(bf16[8,8,256]{2,1,0:T(8,128)(2,1)} %own.1), channel_id=1, source_target_pairs={{0,1},{1,0},{2,3},{3,2},{4,5},{5,4},{6,7},{7,6},{8,9},{9,8},{10,11... | collective-permute-start | bytes 98312 | tf_op jit(solution)/shard_map/ppermute | solution.py:213
  0.5 0.0 copy-start
  0.5 0.0 copy-start.2
  0.5 0.0 copy-start.3
  0.5 1.4 %shard_map.109 = (bf16[8,216,256]{2,1,0:T(8,128)(2,1)S(1)}, bf16[2,64,216]{2,1,0:T(8,128)(2,1)S(1)}, bf16[2,8,64,64]{3,2,1,0:T(8,128)(2,1)S(1)}, f32[8,8,256]{2,1,0:T(8,128)S(1)}, f32[8,256]{1,0:T(8,128)S(1)}) custom-call(s32[8]{0:T(128)} %counts.1, bf16[8,8,256]{2,1,0:T(8,128)(2,1)} %own.1, bf16[8,216,256]{2,1,0:T(8,128)(2,1)} %bitcast.2, ...), custom_call_target="tpu_custom_call" | custom-call | flops 2000000000 | tf_op jit(solution)/shard_map/pallas_call | solution.py:222
  1.9 0.0 collective-permute-done.recv
  2.0 0.0 copy-start.1
  2.0 0.0 copy-start.4
  2.0 0.7 %collective-permute-start.2 = (bf16[9,16,256]{2,1,0:T(8,128)(2,1)S(1)}, bf16[9,16,256]{2,1,0:T(8,128)(2,1)S(1)}, u32[]{:S(2)}, u32[]{:S(2)}) collective-permute-start(bf16[9,16,256]{2,1,0:T(8,128)(2,1)S(1)} %get-tuple-element.21), channel_id=1, source_target_pairs={{0,1},{1,12},{2,3},{3,14},{4,5},{5,8},{6,7},{7,10},{8,9},{9,4},{10... | collective-permute-start | bytes 221192 | tf_op jit(solution)/shard_map/ppermute | solution.py:213
  2.7 4.1 %collective-permute-start.1 = (bf16[9,16,256]{2,1,0:T(8,128)(2,1)S(1)}, bf16[9,16,256]{2,1,0:T(8,128)(2,1)S(1)}, u32[]{:S(2)}, u32[]{:S(2)}) collective-permute-start(bf16[9,16,256]{2,1,0:T(8,128)(2,1)S(1)} %get-tuple-element.21), channel_id=1, source_target_pairs={{0,1},{1,4},{2,3},{3,6},{4,5},{5,0},{6,7},{7,2},{8,9},{9,12},{10,1... | collective-permute-start | bytes 221192 | tf_op jit(solution)/shard_map/ppermute | solution.py:213
  6.8 0.0 collective-permute-start.3
  6.8 0.0 copy-done
  6.8 0.0 copy-done.2
  6.8 0.0 copy-done.3
  6.8 3.1 %shard_map.111 = (f32[8,8,256]{2,1,0:T(8,128)S(1)}, bf16[16,64,64]{2,1,0:T(8,128)(2,1)S(1)}) custom-call(s32[8,6]{1,0:T(8,128)S(1)} %copy-done.2, s32[1,16]{1,0:T(1,128)S(1)} %copy-done.3, f32[8,8,256]{2,1,0:T(8,128)S(1)} %get-tuple-element.17.mine, bf16[8,6,256,256]{3,2,1,0:T(8,128)(2,1)S(1)} %copy-done, bf16[4,64,64,64]{3,2,1,0:T(8,128)(2,1)} %table.1), custom_call_target="tpu_custom_call" | custom-call | flops 2000000000 | tf_op jit(solution)/shard_map/pallas_call | solution.py:249
  9.9 0.8 %collective-permute-done.3 = bf16[1,16,256]{2,1,0:T(8,128)(2,1)S(1)} collective-permute-done((bf16[1,16,256]{2,1,0:T(8,128)(2,1)S(1)}, bf16[1,16,256]{2,1,0:T(8,128)(2,1)S(1)}, u32[]{:S(2)}, u32[]{:S(2)}) %collective-permute-start.3) | collective-permute-done | bytes 8224 | tf_op jit(solution)/shard_map/ppermute | solution.py:213
  10.8 0.0 collective-permute-done.2
  10.8 0.0 collective-permute-done.1
  10.8 0.1 collective-permute-start.4
  10.9 1.4 %collective-permute-done.4.swapped = bf16[20,16,256]{2,1,0:T(8,128)(2,1)S(1)} collective-permute-done((bf16[20,16,256]{2,1,0:T(8,128)(2,1)S(1)}, bf16[20,16,256]{2,1,0:T(8,128)(2,1)S(1)}, u32[]{:S(2)}, u32[]{:S(2)}) %collective-permute-start.4) | collective-permute-done | bytes 163872 | tf_op jit(solution)/shard_map/ppermute | solution.py:213
  12.3 0.0 copy-done.1
  12.3 0.0 copy-done.4
  12.3 4.3 %shard_map.112 = f32[8,8,256]{2,1,0:T(8,128)} custom-call(s32[8,6]{1,0:T(8,128)S(1)} %copy-done.2, s32[1,16]{1,0:T(1,128)S(1)} %copy-done.4, f32[8,256]{1,0:T(8,128)S(1)} %get-tuple-element.16.live, bf16[20,16,256]{2,1,0:T(8,128)(2,1)S(1)} %pad_maximum_fusion.here, bf16[20,16,256]{2,1,0:T(8,128)(2,1)S(1)} %collective-permute-done.4.swapped, ...), custom_call_target="tpu_custom_call" | custom-call | flops 2000000000 | tf_op jit(solution)/shard_map/pallas_call | solution.py:261
  (2 shorter events, 0.1 us)
Async XLA Ops:
  0.0 1.9 %collective-permute-start = (bf16[8,8,256]{2,1,0:T(8,128)(2,1)}, bf16[8,8,256]{2,1,0:T(8,128)(2,1)S(1)}, u32[]{:S(2)}, u32[]{:S(2)}) collective-permute-start(bf16[8,8,256]{2,1,0:T(8,128)(2,1)} %own.1), channel_id=1, source_target_pairs={{0,1},{1,0},{2,3},{3,2},{4,5},{5,4},{6,7},{7,6},{8,9},{9,8},{10,11... | collective-permute-start | bytes 98312 | tf_op jit(solution)/shard_map/ppermute | solution.py:213
  0.5 6.3 %copy-start = (bf16[8,6,256,256]{3,2,1,0:T(8,128)(2,1)S(1)}, bf16[8,6,256,256]{3,2,1,0:T(8,128)(2,1)}, u32[]{:S(2)}) copy-start(bf16[8,6,256,256]{3,2,1,0:T(8,128)(2,1)} %tiles.3) | copy-start | bytes 18874372
  0.5 6.3 %copy-start.2 = (s32[8,6]{1,0:T(8,128)S(1)}, s32[8,6]{1,0:T(8,128)}, u32[]{:S(2)}) copy-start(s32[8,6]{1,0:T(8,128)} %near_list.3) | copy-start | bytes 580
  0.5 6.3 %copy-start.3 = (s32[1,16]{1,0:T(1,128)S(1)}, s32[1,16]{1,0:T(1,128)}, u32[]{:S(2)}) copy-start(s32[1,16]{1,0:T(1,128)} %m2l_type.1) | copy-start | bytes 196
  2.0 10.3 %copy-start.1 = (bf16[8,256,256]{2,1,0:T(8,128)(2,1)S(1)}, bf16[8,256,256]{2,1,0:T(8,128)(2,1)}, u32[]{:S(2)}) copy-start(bf16[8,256,256]{2,1,0:T(8,128)(2,1)} %jacobi.1) | copy-start | bytes 3145732
  2.0 10.3 %copy-start.4 = (s32[1,16]{1,0:T(1,128)S(1)}, s32[1,16]{1,0:T(1,128)}, u32[]{:S(2)}) copy-start(s32[1,16]{1,0:T(1,128)} %m2l_list.1) | copy-start | bytes 196
  2.0 8.8 %collective-permute-start.2 = (bf16[9,16,256]{2,1,0:T(8,128)(2,1)S(1)}, bf16[9,16,256]{2,1,0:T(8,128)(2,1)S(1)}, u32[]{:S(2)}, u32[]{:S(2)}) collective-permute-start(bf16[9,16,256]{2,1,0:T(8,128)(2,1)S(1)} %get-tuple-element.21), channel_id=1, source_target_pairs={{0,1},{1,12},{2,3},{3,14},{4,5},{5,8},{6,7},{7,10},{8,9},{9,4},{10... | collective-permute-start | bytes 221192 | tf_op jit(solution)/shard_map/ppermute | solution.py:213
  2.7 8.1 %collective-permute-start.1 = (bf16[9,16,256]{2,1,0:T(8,128)(2,1)S(1)}, bf16[9,16,256]{2,1,0:T(8,128)(2,1)S(1)}, u32[]{:S(2)}, u32[]{:S(2)}) collective-permute-start(bf16[9,16,256]{2,1,0:T(8,128)(2,1)S(1)} %get-tuple-element.21), channel_id=1, source_target_pairs={{0,1},{1,4},{2,3},{3,6},{4,5},{5,0},{6,7},{7,2},{8,9},{9,12},{10,1... | collective-permute-start | bytes 221192 | tf_op jit(solution)/shard_map/ppermute | solution.py:213
  6.8 4.0 %collective-permute-start.3 = (bf16[1,16,256]{2,1,0:T(8,128)(2,1)S(1)}, bf16[1,16,256]{2,1,0:T(8,128)(2,1)S(1)}, u32[]{:S(2)}, u32[]{:S(2)}) collective-permute-start(bf16[1,16,256]{2,1,0:T(8,128)(2,1)S(1)} %get-tuple-element.22.boxes_own), channel_id=1, source_target_pairs={{0,1},{1,8},{2,3},{3,10},{4,5},{5,12},{6,7},{7,14},{8,9},{9,0},{10... | collective-permute-start | bytes 24584 | tf_op jit(solution)/shard_map/ppermute | solution.py:213
  10.8 1.5 %collective-permute-start.4 = (bf16[20,16,256]{2,1,0:T(8,128)(2,1)S(1)}, bf16[20,16,256]{2,1,0:T(8,128)(2,1)S(1)}, u32[]{:S(2)}, u32[]{:S(2)}) collective-permute-start(bf16[20,16,256]{2,1,0:T(8,128)(2,1)S(1)} %pad_maximum_fusion.here), channel_id=1, source_target_pairs={{0,1},{1,0},{2,3},{3,2},{4,5},{5,4},{6,7},{7,6},{8,9},{9,8},{10,11... | collective-permute-start | bytes 491528 | tf_op jit(solution)/shard_map/ppermute | solution.py:213

commit v2 on v1

v2 whole, which is shorter than its diff:
```python
import jax
import jax.numpy as jnp
from jax import lax
from jax.experimental import pallas as pl
from jax.experimental.pallas import tpu as pltpu
from jax.sharding import PartitionSpec as P

F32 = jnp.float32
BF16 = jnp.bfloat16
NT = (((1,), (1,)), ((), ()))
VMEM = pl.BlockSpec(memory_space=pltpu.VMEM)
SMEM = pl.BlockSpec(memory_space=pltpu.SMEM)
HBM = pl.BlockSpec(memory_space=pltpu.HBM)
COST = 2 * 10**9


def call(kernel, out_shape, in_specs, scratch=()):
    return pl.pallas_call(
        kernel,
        out_shape=out_shape,
        in_specs=in_specs,
        out_specs=jax.tree.map(lambda _: VMEM, out_shape),
        scratch_shapes=list(scratch),
        compiler_params=pltpu.CompilerParams(vmem_limit_bytes=16 << 20),
        cost_estimate=pl.CostEstimate(flops=COST, bytes_accessed=0, transcendentals=0),
    )


def in_hbm(*arrays):
    return [pltpu.with_memory_space_constraint(array, pltpu.HBM) for array in arrays]


def core_index():
    return lax.rem(lax.axis_index("chan"), 2)


def nt(a, b):
    return lax.dot_general(a, b, NT, preferred_element_type=F32)


def nn(a, b):
    return jnp.dot(a, b, preferred_element_type=F32)


def halves(value):
    high = value.astype(BF16)
    return jnp.concatenate([high, (value - high.astype(F32)).astype(BF16)], axis=0)


def halves_sum(value):
    half = value.shape[0] // 2
    return value[:half] + value[half:]


def load_kernel(
    counts, own, interp_t, comp_t, m2m, interp_out, comp_out, m2m_out, mine, live, counts_s, own_s, sems
):
    base = lax.div(lax.axis_index("chan"), 2) * 2
    far = core_index() == 1
    first = [
        pltpu.make_async_copy(counts, counts_s, sems.at[0]),
        pltpu.make_async_copy(own, own_s, sems.at[1]),
    ]
    tables = [
        pltpu.make_async_copy(interp_t, interp_out, sems.at[2]),
        pltpu.make_async_copy(comp_t.at[pl.ds(base, 2)], comp_out, sems.at[3]),
        pltpu.make_async_copy(m2m.at[pl.ds(base, 2)], m2m_out, sems.at[4]),
    ]
    for copy in first:
        copy.start()

    @pl.when(far)
    def _():
        for copy in tables:
            copy.start()

    leaves, unknowns = live.shape
    slots = lax.broadcasted_iota(jnp.int32, (1, unknowns), 1)
    first[0].wait()
    for leaf in range(leaves):
        live[leaf : leaf + 1] = jnp.where(slots < counts_s[leaf], 1.0, 0.0)
    first[1].wait()
    mine[...] = jnp.swapaxes(own_s[...].astype(F32), 0, 1) * live[...][:, None, :]

    @pl.when(far)
    def _():
        for copy in tables:
            copy.wait()


def by_channel(rows, combos, rank):
    row = lax.broadcasted_iota(jnp.int32, (rows, 2 * rank), 0)
    lane = lax.broadcasted_iota(jnp.int32, (rows, 2 * rank), 1)
    return (lax.rem(row, 2 * combos) >= combos) == (lane >= rank)


def box_kernel(mine, live, recv, interp_t, comp_t, m2m, packed, boxes):
    leaves, combos, unknowns = mine.shape
    rows = 2 * combos
    rank = m2m.shape[2]
    core = core_index()
    own = mine[...]
    other = jnp.swapaxes(recv[...].astype(F32), 0, 1) * live[...][:, None, :]
    both = jnp.concatenate(
        [jnp.where(core == 1, other, own), jnp.where(core == 1, own, other)], axis=1
    ).astype(BF16)
    packed[0:leaves] = both

    @pl.when(core == 0)
    def _():
        packed[leaves] = jnp.zeros((rows, unknowns), BF16)
        boxes[...] = jnp.zeros_like(boxes)

    @pl.when(core == 1)
    def _():
        nodes = jnp.concatenate(
            [nt(both[leaf], interp_t[leaf]).astype(BF16) for leaf in range(leaves)], axis=0
        )
        comp = comp_t[...].reshape(2 * rank, comp_t.shape[2])
        moments = nt(nodes, comp)
        moments = jnp.where(by_channel(leaves * rows, combos, rank), moments, 0.0).astype(BF16)
        total = None
        for leaf in range(leaves):
            trans = jnp.concatenate([m2m[0, leaf], m2m[1, leaf]], axis=0)
            part = nn(moments[leaf * rows : (leaf + 1) * rows], trans)
            total = part if total is None else total + part
        pair = jnp.concatenate([total, total], axis=1)
        pair = jnp.where(by_channel(rows, combos, rank), pair, 0.0).astype(BF16)
        boxes[0] = pair
        packed[leaves] = jnp.concatenate(
            [pair, jnp.zeros((rows, unknowns - 2 * rank), BF16)], axis=1
        )


def near_kernel(near_list, packed, by_pair, by_edge, tiles, jacobi, near, beside):
    me = lax.axis_index("leaf")
    leaves, neighbours = near_list.shape

    @pl.when(core_index() == 0)
    def _():
        odd = lax.rem(me, 2) == 1
        pair = by_pair[0:leaves].astype(F32)
        edge = by_edge[0:leaves].astype(F32)
        beside[0:leaves] = jnp.where(odd, pair, edge)
        beside[leaves : 2 * leaves] = packed[0:leaves].astype(F32)
        beside[2 * leaves : 3 * leaves] = jnp.where(odd, edge, pair)
        start = (me - 1) * leaves
        sums = []
        for leaf in range(leaves):
            total = None
            for k in range(neighbours):
                part = nt(beside[near_list[leaf, k] - start].astype(BF16), tiles[leaf, k])
                total = part if total is None else total + part
            sums.append(halves(total))
        for leaf in range(leaves):
            near[leaf] = halves_sum(nt(sums[leaf], jacobi[leaf]))


def expand_kernel(interp_t, comp_t, out):
    @pl.when(core_index() == 1)
    def _():
        comp = comp_t[...].reshape(-1, comp_t.shape[2])
        for leaf in range(out.shape[0]):
            out[leaf] = halves(nn(comp, interp_t[leaf]))


def apply_kernel(expand, jacobi, out):
    @pl.when(core_index() == 1)
    def _():
        for leaf in range(out.shape[0]):
            out[leaf] = halves(halves_sum(nt(expand[leaf], jacobi[leaf])))


def source_kernel(m2l_list, m2l_type, table, out, sums):
    me = lax.axis_index("leaf")
    base = lax.div(lax.axis_index("chan"), 2) * 2
    rank = table.shape[2]

    @pl.when(core_index() == 1)
    def _():
        sums[...] = jnp.zeros_like(sums)
        for k in range(m2l_list.shape[1]):
            slot = jnp.bitwise_xor(m2l_list[0, k], me)
            kind = m2l_type[0, k]
            sums[slot, :rank] += table[base, kind].astype(F32)
            sums[slot, rank:] += table[base + 1, kind].astype(F32)
        for slot in range(out.shape[0]):
            out[slot] = halves(sums[slot])


def far_kernel(boxes, sources, near, m2m, apply, keep, send):
    core = core_index()
    leaves, rows = near.shape[:2]
    combos = rows // 2
    rank = m2m.shape[2]

    @pl.when(core == 0)
    def _():
        keep[...] = near[:, :combos]
        send[...] = near[:, combos:]

    @pl.when(core == 1)
    def _():
        local = None
        for slot in range(boxes.shape[0]):
            box = boxes[slot]
            part = nn(jnp.concatenate([box, box], axis=1), sources[slot])
            local = part if local is None else local + part
        local = local.astype(BF16)
        mask = by_channel(rows, combos, rank)
        down = []
        for leaf in range(leaves):
            trans = jnp.concatenate([m2m[0, leaf], m2m[1, leaf]], axis=0)
            down.append(jnp.where(mask, nt(local, trans), 0.0).astype(BF16))
        for leaf in range(leaves):
            far = nn(jnp.concatenate([down[leaf], down[leaf]], axis=1), apply[leaf])
            keep[leaf] = far[combos:]
            send[leaf] = far[:combos]


def final_kernel(live, keep, recv, out):
    total = (keep[...] + recv[...]) * live[...][:, None, :]
    out[...] = jnp.swapaxes(total, 0, 1)


def body(
    currents, counts, near_list, m2l_list, m2l_type, interp, compress, m2m, m2l, near_tiles, jacobi
):
    combos, leaves, unknowns = currents.shape
    nodes, rank = compress.shape[1:]
    rows = 2 * combos
    entries = m2l_list.shape[1]
    n = lax.axis_size("leaf")
    chans = lax.axis_size("chan")
    shape = jax.ShapeDtypeStruct

    def permute(value, target):
        moves = []
        for leaf in range(n):
            for chan in range(chans):
                to_leaf, to_chan = target(leaf, chan)
                moves.append((leaf * chans + chan, to_leaf * chans + to_chan))
        return lax.ppermute(value, ("leaf", "chan"), moves)

    def swap(value):
        return permute(value, lambda leaf, chan: (leaf, chan ^ 1))

    def edge(leaf, chan):
        if leaf in (0, n - 1) or chan % 2:
            return leaf, chan ^ 2
        return (leaf + 1 if leaf % 2 else leaf - 1), chan

    recv = swap(currents)
    interp_v, comp_v, m2m_v, mine, live = call(
        load_kernel,
        (
            shape((leaves, nodes, unknowns), BF16),
            shape((2, rank, nodes), BF16),
            shape((2, leaves, rank, rank), BF16),
            shape((leaves, combos, unknowns), F32),
            shape((leaves, unknowns), F32),
        ),
        [HBM] * 5,
        [
            pltpu.SMEM((leaves,), jnp.int32),
            pltpu.VMEM(currents.shape, BF16),
            pltpu.SemaphoreType.DMA((5,)),
        ],
    )(*in_hbm(counts, currents, jnp.swapaxes(interp, 1, 2), jnp.swapaxes(compress, 1, 2), m2m))
    packed, boxes = call(
        box_kernel,
        (shape((leaves + 1, rows, unknowns), BF16), shape((1, rows, 2 * rank), BF16)),
        [VMEM] * 6,
    )(mine, live, recv, interp_v, comp_v, m2m_v)
    double = shape((leaves, 4 * rank, unknowns), BF16)
    by_pair = permute(packed, lambda leaf, chan: (leaf ^ 1, chan))
    comp_v, after = lax.optimization_barrier((comp_v, packed))
    expand = call(expand_kernel, double, [VMEM] * 2)(interp_v, comp_v)
    after, expand = lax.optimization_barrier((after, expand))
    by_edge = permute(after, edge)
    m2l, expand = lax.optimization_barrier((m2l, expand))
    sources = call(
        source_kernel,
        shape((n, 4 * rank, rank), BF16),
        [SMEM, SMEM, VMEM],
        [pltpu.VMEM((n, 2 * rank, rank), F32)],
    )(m2l_list, m2l_type, m2l)
    boxes = jnp.concatenate([boxes, by_pair[leaves:, :, : 2 * rank]], axis=0)
    boxes, expand, sources = lax.optimization_barrier((boxes, expand, sources))
    apply = call(apply_kernel, double, [VMEM] * 2)(expand, jacobi)
    step = 2
    while step < n:
        boxes = jnp.concatenate(
            [
                boxes,
                permute(
                    boxes,
                    lambda leaf, chan, step=step: (leaf ^ step, chan) if chan % 2 else (leaf, chan ^ 2),
                ),
            ],
            axis=0,
        )
        step *= 2
    near = call(
        near_kernel,
        shape((leaves, rows, unknowns), F32),
        [SMEM, VMEM, VMEM, VMEM, VMEM, VMEM],
        [pltpu.VMEM((3 * leaves, rows, unknowns), F32)],
    )(near_list, packed, by_pair, by_edge, near_tiles, jacobi)
    part = shape((leaves, combos, unknowns), F32)
    keep, send = call(far_kernel, (part, part), [VMEM] * 5)(boxes, sources, near, m2m_v, apply)
    return call(final_kernel, shape(currents.shape, F32), [VMEM] * 3)(live, keep, swap(send))


def solution(mesh):
    placed = (
        P(("groups", "chan"), "leaf", None),
        P(("groups", "leaf")),
        P(("groups", "leaf"), None),
        P(("groups", "leaf"), None),
        P(("groups", "leaf"), None),
        P(("groups", "leaf"), None, None),
        P(),
        P(),
        P(),
        P(("groups", "leaf"), None, None, None),
        P(("groups", "leaf"), None, None),
    )
    return jax.shard_map(
        body,
        mesh=mesh,
        in_specs=placed,
        out_specs=P(("groups", "chan"), "leaf", None),
        check_vma=False,
    )
```

time: 16.8 us -> 14.5 us (0.86)
  Pallas kernels: 8.95 us -> 4.75 us
  starting transfers between devices: 5.31 us -> 7.21 us
    pallas_call x3 -> x7, Pallas kernels: 7.51 us -> 3.92 us  [the longest x1 2.64 us: body(): call(near_kernel, shape((leaves, rows, unknowns), F32), [SMEM, VMEM, VMEM...]
    ppermute x5, starting transfers between devices: 5.31 us -> 7.21 us  [permute(): return lax.ppermute(value, ('leaf', 'chan'), moves)]
    pallas_call x1, Pallas kernels: 1.45 us -> 0.83 us  [body(): call(load_kernel, (shape((leaves, nodes, unknowns), BF16), shape((2, rank...]
  transfers between devices with their start and end apart: 5 -> 5, of which waited for: 2 -> 3; matrix products, arithmetic and copies ran while one was open for 0% -> 0% of each run, Pallas kernels for 28% -> 28%
where the time goes in v2:
time: 14.5 us; the launch traced here: 14.3 us
  starting transfers between devices  7.21 us (50%)
  Pallas kernels  4.75 us (33%)
  waiting for transfers between devices  2.19 us (15%)
    ppermute x5, starting transfers between devices, permute(): return lax.ppermute(value, ('leaf', 'chan'), moves)  7.21 us
    pallas_call x1, Pallas kernels, body(): call(near_kernel, shape((leaves, rows, unknowns), F32), [SMEM, VMEM, VMEM...  2.64 us
    ppermute x5, waiting for transfers between devices, permute(): return lax.ppermute(value, ('leaf', 'chan'), moves)  2.19 us
    pallas_call x1, Pallas kernels, body(): call(load_kernel, (shape((leaves, nodes, unknowns), BF16), shape((2, rank...  0.83 us
    pallas_call x1, Pallas kernels, body(): call(final_kernel, shape(currents.shape, F32), [VMEM] * 3)  0.66 us
    pallas_call x1, Pallas kernels, body(): call(source_kernel, shape((n, 4 * rank, rank), BF16), [SMEM, SMEM, VMEM],...  0.56 us
  transfers between devices with their start and end apart: 5, of which 3 were waited for; matrix products, arithmetic and copies ran while one was open for 0% of the time, Pallas kernels for 28%

profile of v2, /device:TPU:0, one launch (start us, length us, event | category | flops | bytes accessed | tf_op | source)
XLA Modules:
  0.0 14.3 jit_solution(13509482177078594979)
XLA Ops:
  0.0 0.5 %collective-permute-start = (bf16[8,8,256]{2,1,0:T(8,128)(2,1)}, bf16[8,8,256]{2,1,0:T(8,128)(2,1)S(1)}, u32[]{:S(2)}, u32[]{:S(2)}) collective-permute-start(bf16[8,8,256]{2,1,0:T(8,128)(2,1)} %own.1), channel_id=1, source_target_pairs={{0,1},{1,0},{2,3},{3,2},{4,5},{5,4},{6,7},{7,6},{8,9},{9,8},{10,11... | collective-permute-start | bytes 98312 | tf_op jit(solution)/shard_map/ppermute | solution.py:243
  0.5 0.8 %shard_map.109 = (bf16[8,216,256]{2,1,0:T(8,128)(2,1)S(1)}, bf16[2,64,216]{2,1,0:T(8,128)(2,1)S(1)}, bf16[2,8,64,64]{3,2,1,0:T(8,128)(2,1)S(1)}, f32[8,8,256]{2,1,0:T(8,128)S(1)}, f32[8,256]{1,0:T(8,128)S(1)}) custom-call(s32[8]{0:T(128)} %counts.1, bf16[8,8,256]{2,1,0:T(8,128)(2,1)} %own.1, bf16[8,216,256]{2,1,0:T(8,128)(2,1)} %bitcast.4, ...), custom_call_target="tpu_custom_call" | custom-call | flops 2000000000 | tf_op jit(solution)/shard_map/pallas_call | solution.py:254
  1.3 0.2 %collective-permute-done.recv = bf16[8,8,256]{2,1,0:T(8,128)(2,1)S(1)} collective-permute-done((bf16[8,8,256]{2,1,0:T(8,128)(2,1)}, bf16[8,8,256]{2,1,0:T(8,128)(2,1)S(1)}, u32[]{:S(2)}, u32[]{:S(2)}) %collective-permute-start) | collective-permute-done | bytes 32800 | tf_op jit(solution)/shard_map/ppermute | solution.py:243
  1.5 0.0 copy-start.2
  1.5 0.0 copy-start.3
  1.5 0.0 copy-start.4
  1.6 0.0 copy-start
  1.6 3.0 %collective-permute-start.1 = (bf16[9,16,256]{2,1,0:T(8,128)(2,1)S(1)}, bf16[9,16,256]{2,1,0:T(8,128)(2,1)S(1)}, u32[]{:S(2)}, u32[]{:S(2)}) collective-permute-start(bf16[9,16,256]{2,1,0:T(8,128)(2,1)S(1)} %get-tuple-element.37.packed), channel_id=1, source_target_pairs={{0,4},{1,5},{2,6},{3,7},{4,0},{5,1},{6,2},{7,3},{8,12},{9,13},{10,... | collective-permute-start | bytes 221192 | tf_op jit(solution)/shard_map/ppermute | solution.py:243
  4.6 0.0 slice-start
  4.6 0.0 slice-start.1
  4.6 0.0 copy-start.1
  4.6 1.5 %collective-permute-start.3 = (bf16[9,16,256]{2,1,0:T(8,128)(2,1)S(1)}, bf16[9,16,256]{2,1,0:T(8,128)(2,1)S(1)}, u32[]{:S(2)}, u32[]{:S(2)}) collective-permute-start(bf16[9,16,256]{2,1,0:T(8,128)(2,1)S(1)} %get-tuple-element.37.packed), channel_id=1, source_target_pairs={{0,2},{1,3},{2,0},{3,1},{4,8},{5,7},{6,10},{7,5},{8,4},{9,11},{10,... | collective-permute-start | bytes 221192 | tf_op jit(solution)/shard_map/ppermute | solution.py:243
  6.1 0.0 copy-done.2
  6.1 0.0 copy-done.3
  6.1 0.0 copy-done.4
  6.1 0.6 %shard_map.112.sources = bf16[4,256,64]{2,1,0:T(8,128)(2,1)S(1)} custom-call(s32[1,16]{1,0:T(1,128)S(1)} %copy-done.3, s32[1,16]{1,0:T(1,128)S(1)} %copy-done.4, bf16[4,64,64,64]{3,2,1,0:T(8,128)(2,1)S(1)} %copy-done.2), custom_call_target="tpu_custom_call" | custom-call | flops 2000000000 | tf_op jit(solution)/shard_map/pallas_call | solution.py:282
  6.6 0.7 %collective-permute-done.1.by_pair = bf16[9,16,256]{2,1,0:T(8,128)(2,1)S(1)} collective-permute-done((bf16[9,16,256]{2,1,0:T(8,128)(2,1)S(1)}, bf16[9,16,256]{2,1,0:T(8,128)(2,1)S(1)}, u32[]{:S(2)}, u32[]{:S(2)}) %collective-permute-start.1) | collective-permute-done | bytes 73760 | tf_op jit(solution)/shard_map/ppermute | solution.py:243
  7.4 2.2 %collective-permute-start.2 = (bf16[2,16,128]{2,1,0:T(8,128)(2,1)S(1)}, bf16[2,16,128]{2,1,0:T(8,128)(2,1)S(1)}, u32[]{:S(2)}, u32[]{:S(2)}) collective-permute-start(bf16[2,16,128]{2,1,0:T(8,128)(2,1)S(1)} %pad_maximum_fusion.1), channel_id=1, source_target_pairs={{0,2},{1,9},{2,0},{3,11},{4,6},{5,13},{6,4},{7,15},{8,10},{9,1},{1... | collective-permute-start | bytes 24584 | tf_op jit(solution)/shard_map/ppermute | solution.py:243
  9.6 0.0 copy-done
  9.6 0.0 collective-permute-done.3.by_edge
  9.6 0.0 slice-done
  9.6 0.0 slice-done.1
  9.6 0.0 copy-done.1
  9.6 2.6 %shard_map.113.near = f32[8,16,256]{2,1,0:T(8,128)S(1)} custom-call(s32[8,6]{1,0:T(8,128)S(1)} %copy-done.1, bf16[9,16,256]{2,1,0:T(8,128)(2,1)S(1)} %get-tuple-element.37.packed, bf16[9,16,256]{2,1,0:T(8,128)(2,1)S(1)} %collective-permute-done.1.by_pair, bf16[9,16,256]{2,1,0:T(8,128)(2,1)S(1)} %collective-permute-done.3.by_edge, ...), custom_call_target="tpu_custom_call" | custom-call | flops 2000000000 | tf_op jit(solution)/shard_map/pallas_call | solution.py:304
  12.3 0.0 collective-permute-done.2
  12.3 0.1 collective-permute-start.4
  12.4 1.2 %collective-permute-done.4.recv = f32[8,8,256]{2,1,0:T(8,128)S(1)} collective-permute-done((f32[8,8,256]{2,1,0:T(8,128)S(1)}, f32[8,8,256]{2,1,0:T(8,128)S(1)}, u32[]{:S(2)}, u32[]{:S(2)}) %collective-permute-start.4) | collective-permute-done | bytes 65568 | tf_op jit(solution)/shard_map/ppermute | solution.py:243
  13.6 0.7 %shard_map.116 = f32[8,8,256]{2,1,0:T(8,128)} custom-call(f32[8,256]{1,0:T(8,128)S(1)} %get-tuple-element.23.live, f32[8,8,256]{2,1,0:T(8,128)S(1)} %get-tuple-element.39.keep, f32[8,8,256]{2,1,0:T(8,128)S(1)} %collective-permute-done.4.recv), custom_call_target="tpu_custom_call" | custom-call | flops 2000000000 | tf_op jit(solution)/shard_map/pallas_call | solution.py:312
  (8 shorter events, 0.1 us)
Async XLA Ops:
  0.0 1.5 %collective-permute-start = (bf16[8,8,256]{2,1,0:T(8,128)(2,1)}, bf16[8,8,256]{2,1,0:T(8,128)(2,1)S(1)}, u32[]{:S(2)}, u32[]{:S(2)}) collective-permute-start(bf16[8,8,256]{2,1,0:T(8,128)(2,1)} %own.1), channel_id=1, source_target_pairs={{0,1},{1,0},{2,3},{3,2},{4,5},{5,4},{6,7},{7,6},{8,9},{9,8},{10,11... | collective-permute-start | bytes 98312 | tf_op jit(solution)/shard_map/ppermute | solution.py:243
  1.5 4.5 %copy-start.2 = (bf16[4,64,64,64]{3,2,1,0:T(8,128)(2,1)S(1)}, bf16[4,64,64,64]{3,2,1,0:T(8,128)(2,1)}, u32[]{:S(2)}) copy-start(bf16[4,64,64,64]{3,2,1,0:T(8,128)(2,1)} %table) | copy-start | bytes 6291460
  1.5 4.5 %copy-start.3 = (s32[1,16]{1,0:T(1,128)S(1)}, s32[1,16]{1,0:T(1,128)}, u32[]{:S(2)}) copy-start(s32[1,16]{1,0:T(1,128)} %m2l_list.1) | copy-start | bytes 196
  1.5 4.5 %copy-start.4 = (s32[1,16]{1,0:T(1,128)S(1)}, s32[1,16]{1,0:T(1,128)}, u32[]{:S(2)}) copy-start(s32[1,16]{1,0:T(1,128)} %m2l_type.1) | copy-start | bytes 196
  1.6 8.0 %copy-start = (bf16[8,256,256]{2,1,0:T(8,128)(2,1)S(1)}, bf16[8,256,256]{2,1,0:T(8,128)(2,1)}, u32[]{:S(2)}) copy-start(bf16[8,256,256]{2,1,0:T(8,128)(2,1)} %jacobi.3) | copy-start | bytes 3145732
  1.6 5.8 %collective-permute-start.1 = (bf16[9,16,256]{2,1,0:T(8,128)(2,1)S(1)}, bf16[9,16,256]{2,1,0:T(8,128)(2,1)S(1)}, u32[]{:S(2)}, u32[]{:S(2)}) collective-permute-start(bf16[9,16,256]{2,1,0:T(8,128)(2,1)S(1)} %get-tuple-element.37.packed), channel_id=1, source_target_pairs={{0,4},{1,5},{2,6},{3,7},{4,0},{5,1},{6,2},{7,3},{8,12},{9,13},{10,... | collective-permute-start | bytes 221192 | tf_op jit(solution)/shard_map/ppermute | solution.py:243
  4.6 5.0 %slice-start = ((s8[6291456]{0:T(1024)(128)(4,1)}), s8[4194304]{0:T(1024)(128)(4,1)S(1)}, s32[]{:S(2)}) async-start(s8[6291456]{0:T(1024)(128)(4,1)} %bitcast.2), calls=%async_computation | async-start | bytes 8388608
  4.6 5.0 %slice-start.1 = ((s8[6291456]{0:T(1024)(128)(4,1)}), s8[2097152]{0:T(1024)(128)(4,1)S(1)}, s32[]{:S(2)}) async-start(s8[6291456]{0:T(1024)(128)(4,1)} %bitcast.2), calls=%async_computation.1 | async-start | bytes 4194304
  4.6 5.0 %copy-start.1 = (s32[8,6]{1,0:T(8,128)S(1)}, s32[8,6]{1,0:T(8,128)}, u32[]{:S(2)}) copy-start(s32[8,6]{1,0:T(8,128)} %near_list.1) | copy-start | bytes 580
  4.6 5.0 %collective-permute-start.3 = (bf16[9,16,256]{2,1,0:T(8,128)(2,1)S(1)}, bf16[9,16,256]{2,1,0:T(8,128)(2,1)S(1)}, u32[]{:S(2)}, u32[]{:S(2)}) collective-permute-start(bf16[9,16,256]{2,1,0:T(8,128)(2,1)S(1)} %get-tuple-element.37.packed), channel_id=1, source_target_pairs={{0,2},{1,3},{2,0},{3,1},{4,8},{5,7},{6,10},{7,5},{8,4},{9,11},{10,... | collective-permute-start | bytes 221192 | tf_op jit(solution)/shard_map/ppermute | solution.py:243
  7.4 4.9 %collective-permute-start.2 = (bf16[2,16,128]{2,1,0:T(8,128)(2,1)S(1)}, bf16[2,16,128]{2,1,0:T(8,128)(2,1)S(1)}, u32[]{:S(2)}, u32[]{:S(2)}) collective-permute-start(bf16[2,16,128]{2,1,0:T(8,128)(2,1)S(1)} %pad_maximum_fusion.1), channel_id=1, source_target_pairs={{0,2},{1,9},{2,0},{3,11},{4,6},{5,13},{6,4},{7,15},{8,10},{9,1},{1... | collective-permute-start | bytes 24584 | tf_op jit(solution)/shard_map/ppermute | solution.py:243
  12.3 1.3 %collective-permute-start.4 = (f32[8,8,256]{2,1,0:T(8,128)S(1)}, f32[8,8,256]{2,1,0:T(8,128)S(1)}, u32[]{:S(2)}, u32[]{:S(2)}) collective-permute-start(f32[8,8,256]{2,1,0:T(8,128)S(1)} %get-tuple-element.40), channel_id=1, source_target_pairs={{0,1},{1,0},{2,3},{3,2},{4,5},{5,4},{6,7},{7,6},{8,9},{9,8},{10,11... | collective-permute-start | bytes 196616 | tf_op jit(solution)/shard_map/ppermute | solution.py:243

commit v3 on v2

--- a/solution.py
+++ b/solution.py
@@ -9,9 +9,9 @@
 BF16 = jnp.bfloat16
 NT = (((1,), (1,)), ((), ()))
 VMEM = pl.BlockSpec(memory_space=pltpu.VMEM)
-SMEM = pl.BlockSpec(memory_space=pltpu.SMEM)
 HBM = pl.BlockSpec(memory_space=pltpu.HBM)
 COST = 2 * 10**9
+AHEAD = 2
 
 
 def call(kernel, out_shape, in_specs, scratch=()):
@@ -52,40 +52,34 @@
     return value[:half] + value[half:]
 
 
-def load_kernel(
-    counts, own, interp_t, comp_t, m2m, interp_out, comp_out, m2m_out, mine, live, counts_s, own_s, sems
-):
-    base = lax.div(lax.axis_index("chan"), 2) * 2
-    far = core_index() == 1
-    first = [
+def load_kernel(counts, own, mine, live, counts_s, own_s, sems):
+    copies = [
         pltpu.make_async_copy(counts, counts_s, sems.at[0]),
         pltpu.make_async_copy(own, own_s, sems.at[1]),
     ]
-    tables = [
-        pltpu.make_async_copy(interp_t, interp_out, sems.at[2]),
-        pltpu.make_async_copy(comp_t.at[pl.ds(base, 2)], comp_out, sems.at[3]),
-        pltpu.make_async_copy(m2m.at[pl.ds(base, 2)], m2m_out, sems.at[4]),
-    ]
-    for copy in first:
+    for copy in copies:
         copy.start()
-
-    @pl.when(far)
-    def _():
-        for copy in tables:
-            copy.start()
-
     leaves, unknowns = live.shape
     slots = lax.broadcasted_iota(jnp.int32, (1, unknowns), 1)
-    first[0].wait()
+    copies[0].wait()
     for leaf in range(leaves):
         live[leaf : leaf + 1] = jnp.where(slots < counts_s[leaf], 1.0, 0.0)
-    first[1].wait()
+    copies[1].wait()
     mine[...] = jnp.swapaxes(own_s[...].astype(F32), 0, 1) * live[...][:, None, :]
 
-    @pl.when(far)
-    def _():
-        for copy in tables:
-            copy.wait()
+
+def chip_base():
+    return lax.div(lax.axis_index("chan"), 2) * 2
+
+
+def chip_pair(table):
+    pair = table[pl.ds(chip_base(), 2)]
+    return pair.reshape(-1, table.shape[2])
+
+
+def chip_m2m(m2m, leaf):
+    base = chip_base()
+    return jnp.concatenate([m2m[base, leaf], m2m[base + 1, leaf]], axis=0)
 
 
 def by_channel(rows, combos, rank):
@@ -116,12 +110,12 @@
         nodes = jnp.concatenate(
             [nt(both[leaf], interp_t[leaf]).astype(BF16) for leaf in range(leaves)], axis=0
         )
-        comp = comp_t[...].reshape(2 * rank, comp_t.shape[2])
+        comp = chip_pair(comp_t)
         moments = nt(nodes, comp)
         moments = jnp.where(by_channel(leaves * rows, combos, rank), moments, 0.0).astype(BF16)
         total = None
         for leaf in range(leaves):
-            trans = jnp.concatenate([m2m[0, leaf], m2m[1, leaf]], axis=0)
+            trans = chip_m2m(m2m, leaf)
             part = nn(moments[leaf * rows : (leaf + 1) * rows], trans)
             total = part if total is None else total + part
         pair = jnp.concatenate([total, total], axis=1)
@@ -132,25 +126,29 @@
         )
 
 
-def near_kernel(near_list, packed, by_pair, by_edge, tiles, jacobi, near, beside):
+def near_kernel(near_list, packed, by_pair, by_edge, tiles, turned, first, jacobi, near, beside):
     me = lax.axis_index("leaf")
     leaves, neighbours = near_list.shape
+    ahead = turned.shape[1]
 
     @pl.when(core_index() == 0)
     def _():
+        places = near_list[...] - (me - 1) * leaves
         odd = lax.rem(me, 2) == 1
         pair = by_pair[0:leaves].astype(F32)
         edge = by_edge[0:leaves].astype(F32)
         beside[0:leaves] = jnp.where(odd, pair, edge)
         beside[leaves : 2 * leaves] = packed[0:leaves].astype(F32)
         beside[2 * leaves : 3 * leaves] = jnp.where(odd, edge, pair)
-        start = (me - 1) * leaves
         sums = []
         for leaf in range(leaves):
-            total = None
-            for k in range(neighbours):
-                part = nt(beside[near_list[leaf, k] - start].astype(BF16), tiles[leaf, k])
-                total = part if total is None else total + part
+            total = first[leaf]
+            for k in range(1, neighbours):
+                x = beside[places[leaf, k]].astype(BF16)
+                if k <= ahead:
+                    total = total + nn(x, turned[leaf, k - 1])
+                else:
+                    total = total + nt(x, tiles[leaf, k])
             sums.append(halves(total))
         for leaf in range(leaves):
             near[leaf] = halves_sum(nt(sums[leaf], jacobi[leaf]))
@@ -159,7 +157,7 @@
 def expand_kernel(interp_t, comp_t, out):
     @pl.when(core_index() == 1)
     def _():
-        comp = comp_t[...].reshape(-1, comp_t.shape[2])
+        comp = chip_pair(comp_t)
         for leaf in range(out.shape[0]):
             out[leaf] = halves(nn(comp, interp_t[leaf]))
 
@@ -171,17 +169,26 @@
             out[leaf] = halves(halves_sum(nt(expand[leaf], jacobi[leaf])))
 
 
-def source_kernel(m2l_list, m2l_type, table, out, sums):
+def ahead_kernel(m2l_list, m2l_type, table, packed, tiles, out, turned, first, sums):
+    core = core_index()
     me = lax.axis_index("leaf")
-    base = lax.div(lax.axis_index("chan"), 2) * 2
+    base = chip_base()
     rank = table.shape[2]
 
-    @pl.when(core_index() == 1)
-    def _():
+    @pl.when(core == 0)
+    def _():
+        for leaf in range(first.shape[0]):
+            first[leaf] = nt(packed[leaf], tiles[leaf, 0])
+            for k in range(turned.shape[1]):
+                turned[leaf, k] = tiles[leaf, k + 1].T
+
+    @pl.when(core == 1)
+    def _():
+        slots = jnp.bitwise_xor(m2l_list[...], me)
+        kinds = m2l_type[...]
         sums[...] = jnp.zeros_like(sums)
         for k in range(m2l_list.shape[1]):
-            slot = jnp.bitwise_xor(m2l_list[0, k], me)
-            kind = m2l_type[0, k]
+            slot, kind = slots[0, k], kinds[0, k]
             sums[slot, :rank] += table[base, kind].astype(F32)
             sums[slot, rank:] += table[base + 1, kind].astype(F32)
         for slot in range(out.shape[0]):
@@ -210,7 +217,7 @@
         mask = by_channel(rows, combos, rank)
         down = []
         for leaf in range(leaves):
-            trans = jnp.concatenate([m2m[0, leaf], m2m[1, leaf]], axis=0)
+            trans = chip_m2m(m2m, leaf)
             down.append(jnp.where(mask, nt(local, trans), 0.0).astype(BF16))
         for leaf in range(leaves):
             far = nn(jnp.concatenate([down[leaf], down[leaf]], axis=1), apply[leaf])
@@ -245,47 +252,52 @@
     def swap(value):
         return permute(value, lambda leaf, chan: (leaf, chan ^ 1))
 
-    def edge(leaf, chan):
-        if leaf in (0, n - 1) or chan % 2:
+    def first(leaf, chan):
+        if chan % 2:
+            return leaf ^ 1, chan
+        if leaf in (0, n - 1):
             return leaf, chan ^ 2
         return (leaf + 1 if leaf % 2 else leaf - 1), chan
 
+    def second(leaf, chan):
+        return (leaf, chan ^ 2) if chan % 2 else (leaf ^ 1, chan)
+
     recv = swap(currents)
-    interp_v, comp_v, m2m_v, mine, live = call(
+    interp_t = jnp.swapaxes(interp, 1, 2)
+    comp_t = jnp.swapaxes(compress, 1, 2)
+    mine, live = call(
         load_kernel,
-        (
-            shape((leaves, nodes, unknowns), BF16),
-            shape((2, rank, nodes), BF16),
-            shape((2, leaves, rank, rank), BF16),
-            shape((leaves, combos, unknowns), F32),
-            shape((leaves, unknowns), F32),
-        ),
-        [HBM] * 5,
+        (shape((leaves, combos, unknowns), F32), shape((leaves, unknowns), F32)),
+        [HBM] * 2,
         [
             pltpu.SMEM((leaves,), jnp.int32),
             pltpu.VMEM(currents.shape, BF16),
-            pltpu.SemaphoreType.DMA((5,)),
+            pltpu.SemaphoreType.DMA((2,)),
         ],
-    )(*in_hbm(counts, currents, jnp.swapaxes(interp, 1, 2), jnp.swapaxes(compress, 1, 2), m2m))
+    )(*in_hbm(counts, currents))
     packed, boxes = call(
         box_kernel,
         (shape((leaves + 1, rows, unknowns), BF16), shape((1, rows, 2 * rank), BF16)),
         [VMEM] * 6,
-    )(mine, live, recv, interp_v, comp_v, m2m_v)
+    )(mine, live, recv, interp_t, comp_t, m2m)
     double = shape((leaves, 4 * rank, unknowns), BF16)
-    by_pair = permute(packed, lambda leaf, chan: (leaf ^ 1, chan))
-    comp_v, after = lax.optimization_barrier((comp_v, packed))
-    expand = call(expand_kernel, double, [VMEM] * 2)(interp_v, comp_v)
+    by_edge = permute(packed, first)
+    comp_t, after = lax.optimization_barrier((comp_t, packed))
+    expand = call(expand_kernel, double, [VMEM] * 2)(interp_t, comp_t)
     after, expand = lax.optimization_barrier((after, expand))
-    by_edge = permute(after, edge)
+    by_pair = permute(after, second)
     m2l, expand = lax.optimization_barrier((m2l, expand))
-    sources = call(
-        source_kernel,
-        shape((n, 4 * rank, rank), BF16),
-        [SMEM, SMEM, VMEM],
+    sources, turned, first_near = call(
+        ahead_kernel,
+        (
+            shape((n, 4 * rank, rank), BF16),
+            shape((leaves, AHEAD, unknowns, unknowns), BF16),
+            shape((leaves, rows, unknowns), F32),
+        ),
+        [VMEM] * 5,
         [pltpu.VMEM((n, 2 * rank, rank), F32)],
-    )(m2l_list, m2l_type, m2l)
-    boxes = jnp.concatenate([boxes, by_pair[leaves:, :, : 2 * rank]], axis=0)
+    )(m2l_list, m2l_type, m2l, packed, near_tiles)
+    boxes = jnp.concatenate([boxes, by_edge[leaves:, :, : 2 * rank]], axis=0)
     boxes, expand, sources = lax.optimization_barrier((boxes, expand, sources))
     apply = call(apply_kernel, double, [VMEM] * 2)(expand, jacobi)
     step = 2
@@ -304,11 +316,11 @@
     near = call(
         near_kernel,
         shape((leaves, rows, unknowns), F32),
-        [SMEM, VMEM, VMEM, VMEM, VMEM, VMEM],
+        [VMEM] * 8,
         [pltpu.VMEM((3 * leaves, rows, unknowns), F32)],
-    )(near_list, packed, by_pair, by_edge, near_tiles, jacobi)
+    )(near_list, packed, by_pair, by_edge, near_tiles, turned, first_near, jacobi)
     part = shape((leaves, combos, unknowns), F32)
-    keep, send = call(far_kernel, (part, part), [VMEM] * 5)(boxes, sources, near, m2m_v, apply)
+    keep, send = call(far_kernel, (part, part), [VMEM] * 5)(boxes, sources, near, m2m, apply)
     return call(final_kernel, shape(currents.shape, F32), [VMEM] * 3)(live, keep, swap(send))
 
 

time: 14.5 us -> 13 us (0.90)
  waiting for transfers between devices: 2.19 us -> 1.06 us
  Pallas kernels: 4.75 us -> 3.94 us
  starting transfers between devices: 7.21 us -> 7.66 us
    ppermute x5, waiting for transfers between devices: 2.19 us -> 1.06 us  [permute(): return lax.ppermute(value, ('leaf', 'chan'), moves)]
    pallas_call x5, Pallas kernels: 4.06 us -> 3.24 us  [the longest x1 1.67 us: body(): call(near_kernel, shape((leaves, rows, unknowns), F32), [VMEM] * 8, [pltp...]
    ppermute x5, starting transfers between devices: 7.21 us -> 7.66 us  [permute(): return lax.ppermute(value, ('leaf', 'chan'), moves)]
  transfers between devices with their start and end apart: 5 -> 5, of which waited for: 3 -> 2; matrix products, arithmetic and copies ran while one was open for 0% -> 0% of each run, Pallas kernels for 28% -> 25%
where the time goes in v3:
time: 13 us; the launch traced here: 12.8 us
  starting transfers between devices  7.66 us (59%)
  Pallas kernels  3.94 us (30%)
  waiting for transfers between devices  1.06 us (8%)
  between operations  0.13 us (1%)
    ppermute x5, starting transfers between devices, permute(): return lax.ppermute(value, ('leaf', 'chan'), moves)  7.66 us
    pallas_call x1, Pallas kernels, body(): call(near_kernel, shape((leaves, rows, unknowns), F32), [VMEM] * 8, [pltp...  1.67 us
    ppermute x5, waiting for transfers between devices, permute(): return lax.ppermute(value, ('leaf', 'chan'), moves)  1.06 us
    pallas_call x1, Pallas kernels, body(): call(load_kernel, (shape((leaves, combos, unknowns), F32), shape((leaves,...  0.95 us
    pallas_call x1, Pallas kernels, body(): call(final_kernel, shape(currents.shape, F32), [VMEM] * 3)  0.66 us
    pallas_call x1, Pallas kernels, body(): call(ahead_kernel, (shape((n, 4 * rank, rank), BF16), shape((leaves, AHEA...  0.61 us
  transfers between devices with their start and end apart: 5, of which 2 were waited for; matrix products, arithmetic and copies ran while one was open for 0% of the time, Pallas kernels for 25%

profile of v3, /device:TPU:0, one launch (start us, length us, event | category | flops | bytes accessed | tf_op | source)
XLA Modules:
  0.0 12.8 jit_solution(3967198001096511544)
XLA Ops:
  0.0 0.0 copy-start.6
  0.0 0.0 copy-start.7
  0.0 0.0 copy-start.5
  0.0 0.5 %collective-permute-start = (bf16[8,8,256]{2,1,0:T(8,128)(2,1)}, bf16[8,8,256]{2,1,0:T(8,128)(2,1)S(1)}, u32[]{:S(2)}, u32[]{:S(2)}) collective-permute-start(bf16[8,8,256]{2,1,0:T(8,128)(2,1)} %own.1), channel_id=1, source_target_pairs={{0,1},{1,0},{2,3},{3,2},{4,5},{5,4},{6,7},{7,6},{8,9},{9,8},{10,11... | collective-permute-start | bytes 98312 | tf_op jit(solution)/shard_map/ppermute | solution.py:250
  0.5 0.0 slice-start
  0.5 0.9 %shard_map.109 = (f32[8,8,256]{2,1,0:T(8,128)S(1)}, f32[8,256]{1,0:T(8,128)S(1)}) custom-call(s32[8]{0:T(128)} %counts.1, bf16[8,8,256]{2,1,0:T(8,128)(2,1)} %own.1), custom_call_target="tpu_custom_call" | custom-call | flops 2000000000 | tf_op jit(solution)/shard_map/pallas_call | solution.py:268
  1.5 0.1 collective-permute-done.recv
  1.6 0.0 copy-done.6
  1.6 0.0 copy-done.7
  1.6 0.0 copy-done.5
  1.6 0.0 slice-start.1
  1.7 0.0 copy-start
  1.7 0.0 copy-start.3
  1.7 0.0 copy-start.4
  1.7 2.9 %collective-permute-start.1 = (bf16[9,16,256]{2,1,0:T(8,128)(2,1)S(1)}, bf16[9,16,256]{2,1,0:T(8,128)(2,1)S(1)}, u32[]{:S(2)}, u32[]{:S(2)}) collective-permute-start(bf16[9,16,256]{2,1,0:T(8,128)(2,1)S(1)} %get-tuple-element.35.packed), channel_id=1, source_target_pairs={{0,2},{1,5},{2,0},{3,7},{4,8},{5,1},{6,10},{7,3},{8,4},{9,13},{10,... | collective-permute-start | bytes 221192 | tf_op jit(solution)/shard_map/ppermute | solution.py:250
  4.6 0.0 copy-start.1
  4.6 1.7 %collective-permute-start.3 = (bf16[9,16,256]{2,1,0:T(8,128)(2,1)S(1)}, bf16[9,16,256]{2,1,0:T(8,128)(2,1)S(1)}, u32[]{:S(2)}, u32[]{:S(2)}) collective-permute-start(bf16[9,16,256]{2,1,0:T(8,128)(2,1)S(1)} %get-tuple-element.35.packed), channel_id=1, source_target_pairs={{0,4},{1,3},{2,6},{3,1},{4,0},{5,7},{6,2},{7,5},{8,12},{9,11},{10,... | collective-permute-start | bytes 221192 | tf_op jit(solution)/shard_map/ppermute | solution.py:250
  6.3 0.0 slice-done
  6.3 0.0 slice-done.1
  6.3 0.0 copy-done
  6.3 0.0 copy-done.3
  6.3 0.0 copy-done.4
  6.3 0.6 %shard_map.112 = (bf16[4,256,64]{2,1,0:T(8,128)(2,1)S(1)}, bf16[8,2,256,256]{3,2,1,0:T(8,128)(2,1)S(1)}, f32[8,16,256]{2,1,0:T(8,128)S(1)}) custom-call(s32[1,16]{1,0:T(1,128)S(1)} %copy-done.3, s32[1,16]{1,0:T(1,128)S(1)} %copy-done.4, bf16[4,64,64,64]{3,2,1,0:T(8,128)(2,1)S(1)} %copy-done, bf16[9,16,256]{2,1,0:T(8,128)(2,1)S(1)} %get-tuple-element.35.packed, ...), custom_call_target="tpu_custom_call" | custom-call | flops 2000000000 | tf_op jit(solution)/shard_map/pallas_call | solution.py:290
  6.9 0.0 copy-start.2
  6.9 0.0 collective-permute-done.1.by_edge
  7.0 2.0 %collective-permute-start.2 = (bf16[2,16,128]{2,1,0:T(8,128)(2,1)S(1)}, bf16[2,16,128]{2,1,0:T(8,128)(2,1)S(1)}, u32[]{:S(2)}, u32[]{:S(2)}) collective-permute-start(bf16[2,16,128]{2,1,0:T(8,128)(2,1)S(1)} %pad_maximum_fusion.1), channel_id=1, source_target_pairs={{0,2},{1,9},{2,0},{3,11},{4,6},{5,13},{6,4},{7,15},{8,10},{9,1},{1... | collective-permute-start | bytes 24584 | tf_op jit(solution)/shard_map/ppermute | solution.py:250
  9.0 0.0 copy-done.1
  9.0 0.0 collective-permute-done.3.by_pair
  9.0 0.0 copy-done.2
  9.0 1.7 %shard_map.113.near = f32[8,16,256]{2,1,0:T(8,128)S(1)} custom-call(s32[8,6]{1,0:T(8,128)S(1)} %copy-done.2, bf16[9,16,256]{2,1,0:T(8,128)(2,1)S(1)} %get-tuple-element.35.packed, bf16[9,16,256]{2,1,0:T(8,128)(2,1)S(1)} %collective-permute-done.3.by_pair, bf16[9,16,256]{2,1,0:T(8,128)(2,1)S(1)} %collective-permute-done.1.by_edge, ...), custom_call_target="tpu_custom_call" | custom-call | flops 2000000000 | tf_op jit(solution)/shard_map/pallas_call | solution.py:316
  10.6 0.0 collective-permute-done.2
  10.7 0.6 %collective-permute-start.4 = (f32[8,8,256]{2,1,0:T(8,128)S(1)}, f32[8,8,256]{2,1,0:T(8,128)S(1)}, u32[]{:S(2)}, u32[]{:S(2)}) collective-permute-start(f32[8,8,256]{2,1,0:T(8,128)S(1)} %get-tuple-element.40), channel_id=1, source_target_pairs={{0,1},{1,0},{2,3},{3,2},{4,5},{5,4},{6,7},{7,6},{8,9},{9,8},{10,11... | collective-permute-start | bytes 196616 | tf_op jit(solution)/shard_map/ppermute | solution.py:250
  11.3 0.9 %collective-permute-done.4.recv = f32[8,8,256]{2,1,0:T(8,128)S(1)} collective-permute-done((f32[8,8,256]{2,1,0:T(8,128)S(1)}, f32[8,8,256]{2,1,0:T(8,128)S(1)}, u32[]{:S(2)}, u32[]{:S(2)}) %collective-permute-start.4) | collective-permute-done | bytes 65568 | tf_op jit(solution)/shard_map/ppermute | solution.py:250
  12.2 0.7 %shard_map.116 = f32[8,8,256]{2,1,0:T(8,128)} custom-call(f32[8,256]{1,0:T(8,128)S(1)} %get-tuple-element.23.live, f32[8,8,256]{2,1,0:T(8,128)S(1)} %get-tuple-element.39.keep, f32[8,8,256]{2,1,0:T(8,128)S(1)} %collective-permute-done.4.recv), custom_call_target="tpu_custom_call" | custom-call | flops 2000000000 | tf_op jit(solution)/shard_map/pallas_call | solution.py:324
  (8 shorter events, 0.1 us)
Async XLA Ops:
  0.0 1.6 %copy-start.6 = (bf16[4,8,64,64]{3,2,1,0:T(8,128)(2,1)S(1)}, bf16[4,8,64,64]{3,2,1,0:T(8,128)(2,1)}, u32[]{:S(2)}) copy-start(bf16[4,8,64,64]{3,2,1,0:T(8,128)(2,1)} %m2m.3) | copy-start | bytes 786436
  0.0 1.6 %copy-start.7 = (bf16[4,216,64]{1,2,0:T(8,128)(2,1)S(1)}, bf16[4,216,64]{1,2,0:T(8,128)(2,1)}, u32[]{:S(2)}) copy-start(bf16[4,216,64]{1,2,0:T(8,128)(2,1)} %param.17) | copy-start | bytes 331780
  0.0 1.6 %copy-start.5 = (bf16[8,256,216]{1,2,0:T(8,128)(2,1)S(1)}, bf16[8,256,216]{1,2,0:T(8,128)(2,1)}, u32[]{:S(2)}) copy-start(bf16[8,256,216]{1,2,0:T(8,128)(2,1)} %param.16) | copy-start | bytes 2654212
  0.0 1.6 %collective-permute-start = (bf16[8,8,256]{2,1,0:T(8,128)(2,1)}, bf16[8,8,256]{2,1,0:T(8,128)(2,1)S(1)}, u32[]{:S(2)}, u32[]{:S(2)}) collective-permute-start(bf16[8,8,256]{2,1,0:T(8,128)(2,1)} %own.1), channel_id=1, source_target_pairs={{0,1},{1,0},{2,3},{3,2},{4,5},{5,4},{6,7},{7,6},{8,9},{9,8},{10,11... | collective-permute-start | bytes 98312 | tf_op jit(solution)/shard_map/ppermute | solution.py:250
  0.5 5.7 %slice-start = ((s8[6291456]{0:T(1024)(128)(4,1)}), s8[4194304]{0:T(1024)(128)(4,1)S(1)}, s32[]{:S(2)}) async-start(s8[6291456]{0:T(1024)(128)(4,1)} %bitcast.2), calls=%async_computation | async-start | bytes 8388608
  1.6 4.7 %slice-start.1 = ((s8[6291456]{0:T(1024)(128)(4,1)}), s8[2097152]{0:T(1024)(128)(4,1)S(1)}, s32[]{:S(2)}) async-start(s8[6291456]{0:T(1024)(128)(4,1)} %bitcast.2), calls=%async_computation.1 | async-start | bytes 4194304
  1.7 4.6 %copy-start = (bf16[4,64,64,64]{3,2,1,0:T(8,128)(2,1)S(1)}, bf16[4,64,64,64]{3,2,1,0:T(8,128)(2,1)}, u32[]{:S(2)}) copy-start(bf16[4,64,64,64]{3,2,1,0:T(8,128)(2,1)} %table) | copy-start | bytes 6291460
  1.7 4.6 %copy-start.3 = (s32[1,16]{1,0:T(1,128)S(1)}, s32[1,16]{1,0:T(1,128)}, u32[]{:S(2)}) copy-start(s32[1,16]{1,0:T(1,128)} %m2l_list.1) | copy-start | bytes 196
  1.7 4.6 %copy-start.4 = (s32[1,16]{1,0:T(1,128)S(1)}, s32[1,16]{1,0:T(1,128)}, u32[]{:S(2)}) copy-start(s32[1,16]{1,0:T(1,128)} %m2l_type.1) | copy-start | bytes 196
  1.7 5.2 %collective-permute-start.1 = (bf16[9,16,256]{2,1,0:T(8,128)(2,1)S(1)}, bf16[9,16,256]{2,1,0:T(8,128)(2,1)S(1)}, u32[]{:S(2)}, u32[]{:S(2)}) collective-permute-start(bf16[9,16,256]{2,1,0:T(8,128)(2,1)S(1)} %get-tuple-element.35.packed), channel_id=1, source_target_pairs={{0,2},{1,5},{2,0},{3,7},{4,8},{5,1},{6,10},{7,3},{8,4},{9,13},{10,... | collective-permute-start | bytes 221192 | tf_op jit(solution)/shard_map/ppermute | solution.py:250
  4.6 4.4 %copy-start.1 = (bf16[8,256,256]{2,1,0:T(8,128)(2,1)S(1)}, bf16[8,256,256]{2,1,0:T(8,128)(2,1)}, u32[]{:S(2)}) copy-start(bf16[8,256,256]{2,1,0:T(8,128)(2,1)} %jacobi.3) | copy-start | bytes 3145732
  4.6 4.4 %collective-permute-start.3 = (bf16[9,16,256]{2,1,0:T(8,128)(2,1)S(1)}, bf16[9,16,256]{2,1,0:T(8,128)(2,1)S(1)}, u32[]{:S(2)}, u32[]{:S(2)}) collective-permute-start(bf16[9,16,256]{2,1,0:T(8,128)(2,1)S(1)} %get-tuple-element.35.packed), channel_id=1, source_target_pairs={{0,4},{1,3},{2,6},{3,1},{4,0},{5,7},{6,2},{7,5},{8,12},{9,11},{10,... | collective-permute-start | bytes 221192 | tf_op jit(solution)/shard_map/ppermute | solution.py:250
  6.9 2.1 %copy-start.2 = (s32[8,6]{1,0:T(8,128)S(1)}, s32[8,6]{1,0:T(8,128)}, u32[]{:S(2)}) copy-start(s32[8,6]{1,0:T(8,128)} %near_list.1) | copy-start | bytes 580
  7.0 3.7 %collective-permute-start.2 = (bf16[2,16,128]{2,1,0:T(8,128)(2,1)S(1)}, bf16[2,16,128]{2,1,0:T(8,128)(2,1)S(1)}, u32[]{:S(2)}, u32[]{:S(2)}) collective-permute-start(bf16[2,16,128]{2,1,0:T(8,128)(2,1)S(1)} %pad_maximum_fusion.1), channel_id=1, source_target_pairs={{0,2},{1,9},{2,0},{3,11},{4,6},{5,13},{6,4},{7,15},{8,10},{9,1},{1... | collective-permute-start | bytes 24584 | tf_op jit(solution)/shard_map/ppermute | solution.py:250
  10.7 1.5 %collective-permute-start.4 = (f32[8,8,256]{2,1,0:T(8,128)S(1)}, f32[8,8,256]{2,1,0:T(8,128)S(1)}, u32[]{:S(2)}, u32[]{:S(2)}) collective-permute-start(f32[8,8,256]{2,1,0:T(8,128)S(1)} %get-tuple-element.40), channel_id=1, source_target_pairs={{0,1},{1,0},{2,3},{3,2},{4,5},{5,4},{6,7},{7,6},{8,9},{9,8},{10,11... | collective-permute-start | bytes 196616 | tf_op jit(solution)/shard_map/ppermute | solution.py:250

commit v4 on v0

v4 whole, which is shorter than its diff:
```python
import jax
import jax.numpy as jnp
from jax import lax
from jax.experimental import pallas as pl
from jax.experimental.pallas import tpu as pltpu
from jax.sharding import PartitionSpec as P

F32 = jnp.float32
BF16 = jnp.bfloat16
NT = (((1,), (1,)), ((), ()))
VMEM = pl.BlockSpec(memory_space=pltpu.VMEM)
HBM = pl.BlockSpec(memory_space=pltpu.HBM)
INC = 8
COST = 2 * 10**9
AHEAD = 2
KCOST = 2000000000
PCOST = 2000000000
NCOST = 1000000


def call(kernel, out_shape, in_specs, scratch=(), cost=COST):
    return pl.pallas_call(
        kernel,
        out_shape=out_shape,
        in_specs=in_specs,
        out_specs=jax.tree.map(lambda _: VMEM, out_shape),
        scratch_shapes=list(scratch),
        compiler_params=pltpu.CompilerParams(vmem_limit_bytes=16 << 20),
        cost_estimate=pl.CostEstimate(flops=cost, bytes_accessed=0, transcendentals=0),
    )


def in_hbm(*arrays):
    return [pltpu.with_memory_space_constraint(array, pltpu.HBM) for array in arrays]


def nt(a, b):
    return lax.dot_general(a, b, NT, preferred_element_type=F32)


def nn(a, b):
    return jnp.dot(a, b, preferred_element_type=F32)


def tn(a, b):
    return lax.dot_general(a, b, (((0,), (0,)), ((), ())), preferred_element_type=F32)


def halves(value):
    high = value.astype(BF16)
    return jnp.concatenate([high, (value - high.astype(F32)).astype(BF16)], axis=0)


def halves_sum(value):
    half = value.shape[0] // 2
    return value[:half] + value[half:]


def twice(value):
    return jnp.concatenate([value, value], axis=1)


def load_kernel(counts, own, mine, live, counts_s, own_s, sems):
    copies = [
        pltpu.make_async_copy(counts, counts_s, sems.at[0]),
        pltpu.make_async_copy(own, own_s, sems.at[1]),
    ]
    for copy in copies:
        copy.start()
    leaves, unknowns = live.shape
    slots = lax.broadcasted_iota(jnp.int32, (1, unknowns), 1)
    copies[0].wait()
    for leaf in range(leaves):
        live[leaf : leaf + 1] = jnp.where(slots < counts_s[leaf], 1.0, 0.0)
    copies[1].wait()
    mine[...] = jnp.swapaxes(own_s[...].astype(F32), 0, 1) * live[...][:, None, :]


def box_kernel(
    channel, mine, interp_t, comp_t, m2m, near_list, m2l_list, m2l_type, packed, box, places, slots, kinds
):
    me = lax.axis_index("leaf")
    count = lax.axis_size("leaf")
    places[...] = near_list[...] - (me - 1) * mine.shape[0]
    slots[...] = lax.rem(me - m2l_list[...] + count, count)
    kinds[...] = m2l_type[...]
    leaves, combos, unknowns = mine.shape
    rank = m2m.shape[2]
    x = mine[...].astype(BF16)
    packed[0:leaves] = x
    chan = channel()
    nodes = jnp.concatenate(
        [nt(x[leaf], interp_t[leaf]).astype(BF16) for leaf in range(leaves)], axis=0
    )
    moments = nt(nodes, comp_t[chan]).astype(BF16)
    total = None
    for leaf in range(leaves):
        part = nn(moments[leaf * combos : (leaf + 1) * combos], m2m[chan, leaf])
        total = part if total is None else total + part
    pair = twice(total).astype(BF16)
    packed[leaves] = jnp.concatenate(
        [pair, jnp.zeros((combos, unknowns - 2 * rank), BF16)], axis=1
    )
    box[0] = pair


def prepare_kernel(
    channel, packed, tiles, interp_t, comp_t, m2m, slots, kinds, jacobi, table,
    turned, first, apply, sources, expand, mats, sums, mat_sems,
):
    leaves = first.shape[0]
    chan = channel()
    kind = kinds[...]
    copies = [
        pltpu.make_async_copy(table.at[chan, kind[0, k]], mats.at[k], mat_sems.at[k])
        for k in range(mats.shape[0])
    ]
    for copy in copies:
        copy.start()
    comp = comp_t[chan]
    for leaf in range(leaves):
        expand[leaf] = halves(nn(comp, interp_t[leaf]))
    for leaf in range(leaves):
        first[leaf] = nt(packed[leaf], tiles[leaf, 0])
        for k in range(turned.shape[1]):
            turned[leaf, k] = tiles[leaf, k + 1].T
    applied = [halves(halves_sum(nt(expand[leaf], jacobi[leaf]))) for leaf in range(leaves)]
    for leaf in range(leaves):
        child = m2m[chan, leaf]
        apply[leaf] = halves(tn(jnp.concatenate([child, child], axis=0), applied[leaf]))
    for copy in copies:
        copy.wait()
    slot = slots[...]
    sums[...] = jnp.zeros_like(sums)
    for k in range(mats.shape[0]):
        sums[slot[0, k]] += mats[k].astype(F32)
    for place in range(sources.shape[0]):
        sources[place] = halves(sums[place])


def near_kernel(places, packed, high, low, tiles, turned, first, jacobi, near, beside):
    leaves, neighbours = places.shape
    ahead = turned.shape[1]
    places = places[...]
    beside[0:leaves] = low[0:leaves].astype(F32)
    beside[leaves : 2 * leaves] = packed[0:leaves].astype(F32)
    beside[2 * leaves : 3 * leaves] = high[0:leaves].astype(F32)
    sums = []
    for leaf in range(leaves):
        total = first[leaf]
        for k in range(1, neighbours):
            x = beside[places[leaf, k]].astype(BF16)
            if k <= ahead:
                total = total + nn(x, turned[leaf, k - 1])
            else:
                total = total + nt(x, tiles[leaf, k])
        sums.append(halves(total))
    for leaf in range(leaves):
        near[leaf] = halves_sum(nt(sums[leaf], jacobi[leaf]))


def final_kernel(sources, near, live, apply, box, high, low, *refs):
    *further, out = refs
    leaves, lanes = near.shape[0], box.shape[2]
    boxes = [box[0], low[leaves, :, :lanes]] + [ref[0] for ref in further] + [high[leaves, :, :lanes]]
    local = None
    for slot in range(sources.shape[0]):
        part = nn(boxes[slot], sources[slot])
        local = part if local is None else local + part
    local = twice(local).astype(BF16)
    for leaf in range(near.shape[0]):
        far = nn(local, apply[leaf])
        out[:, leaf, :] = (near[leaf] + far) * live[leaf : leaf + 1]


def body(
    currents, counts, near_list, m2l_list, m2l_type, interp, compress, m2m, m2l, near_tiles, jacobi
):
    combos, leaves, unknowns = currents.shape
    rank = compress.shape[2]
    entries = m2l_list.shape[1]
    n = lax.axis_size("leaf")
    chans = lax.axis_size("chan")
    shape = jax.ShapeDtypeStruct

    def channel():
        return lax.div(lax.axis_index("chan") * combos, INC)

    def bound(kernel):
        return lambda *refs: kernel(channel, *refs)

    def permute(value, shift, cross):
        moves = []
        for leaf in range(n):
            for chan in range(chans):
                to = (leaf + shift) % n * chans + (chan ^ 1 if cross else chan)
                moves.append((leaf * chans + chan, to))
        return lax.ppermute(value, ("leaf", "chan"), moves)

    interp_t = jnp.swapaxes(interp, 1, 2)
    comp_t = jnp.swapaxes(compress, 1, 2)
    part = shape((leaves, combos, unknowns), F32)
    mine, live = call(
        load_kernel,
        (part, shape((leaves, unknowns), F32)),
        [HBM] * 2,
        [
            pltpu.SMEM((leaves,), jnp.int32),
            pltpu.VMEM(currents.shape, BF16),
            pltpu.SemaphoreType.DMA((2,)),
        ],
    )(*in_hbm(counts, currents))
    packed, box, places, slots, kinds = call(
        bound(box_kernel),
        (
            shape((leaves + 1, combos, unknowns), BF16),
            shape((1, combos, 2 * rank), BF16),
            shape(near_list.shape, jnp.int32),
            shape(m2l_list.shape, jnp.int32),
            shape(m2l_type.shape, jnp.int32),
        ),
        [VMEM] * 7,
        cost=KCOST,
    )(mine, interp_t, comp_t, m2m, near_list, m2l_list, m2l_type)
    other = permute(box, 0, True)
    low = permute(packed, 1, False)

    high = permute(packed, -1, False)
    further = [permute(other, shift, True) for shift in range(2, n - 1)]
    after, _ = lax.optimization_barrier((packed, other))
    turned, first, apply, sources = call(
        bound(prepare_kernel),
        (
            shape((leaves, AHEAD, unknowns, unknowns), BF16),
            part,
            shape((leaves, 2 * rank, unknowns), BF16),
            shape((n, 2 * rank, rank), BF16),
        ),
        [VMEM] * 8 + [HBM],
        [
            pltpu.VMEM((leaves, 2 * rank, unknowns), BF16),
            pltpu.VMEM((entries, rank, rank), BF16),
            pltpu.VMEM((n, rank, rank), F32),
            pltpu.SemaphoreType.DMA((entries,)),
        ],
        PCOST,
    )(after, near_tiles, interp_t, comp_t, m2m, slots, kinds, jacobi, *in_hbm(m2l))
    near = call(
        near_kernel, part, [VMEM] * 8, [pltpu.VMEM((3 * leaves, combos, unknowns), F32)], NCOST
    )(places, packed, high, low, near_tiles, turned, first, jacobi)
    return call(final_kernel, shape(currents.shape, F32), [VMEM] * (7 + len(further)))(
        sources, near, live, apply, box, high, low, *further
    )


def solution(mesh):
    placed = (
        P(("groups", "chan"), "leaf", None),
        P(("groups", "leaf")),
        P(("groups", "leaf"), None),
        P(("groups", "leaf"), None),
        P(("groups", "leaf"), None),
        P(("groups", "leaf"), None, None),
        P(),
        P(),
        P(),
        P(("groups", "leaf"), None, None, None),
        P(("groups", "leaf"), None, None),
    )
    return jax.shard_map(
        body,
        mesh=mesh,
        in_specs=placed,
        out_specs=P(("groups", "chan"), "leaf", None),
        check_vma=False,
    )
```

time: 39.1 us -> 12.6 us (0.32)
  blocking collectives: 13.3 us -> 0 us
  matrix products: 10.8 us -> 0 us
  Pallas kernels: 0 us -> 5.81 us
  other arithmetic: 4.37 us -> 0 us
  local copies, waits for them, and re-layouts: 3.82 us -> 0.45 us
  starting transfers between devices: 6.22 us -> 5.65 us
  waiting for transfers between devices: 0.01 us -> 0.44 us
    all_gather x1 -> x0, blocking collectives: 13.3 us -> none  [body(): every_leaf = lax.all_gather(moments, 'leaf', axis=1, tiled=True)]
    dot_general x7 -> x0, matrix products: 10.8 us -> none  [the longest x1 4.51 us: body(): jnp.einsum('lkvu,qlku->qlv', near_tiles, beside, preferred_element_type=j...]
    pallas_call x0 -> x5, Pallas kernels: none -> 5.81 us  [the longest x1 1.64 us: body(): call(near_kernel, part, [VMEM] * 8, [pltpu.VMEM((3 * leaves, combos, unkn...]
    gather x3 -> x0, local copies, waits for them, and re-layouts: 1.75 us -> none  [the longest x1 0.6 us: body(): mats = jnp.take(table, m2l_type, axis=0)]
    broadcast_in_dim x2 -> x0, other arithmetic: 1.32 us -> none  [the longest x1 0.66 us: body(): mats = jnp.take(table, m2l_type, axis=0)]
    squeeze x1 -> x0, local copies, waits for them, and re-layouts: 1.31 us -> none  [body(): table = lax.dynamic_index_in_dim(m2l, channel, 0, keepdims=False)]
    lt x1 -> x0, other arithmetic: 0.87 us -> none  [body(): live = slots[None, :] < counts[:, None]]
    select_n x1 -> x0, other arithmetic: 0.77 us -> none  [body(): masked = jnp.where(live[None], currents, jnp.zeros_like(currents))]
  transfers between devices with their start and end apart: 2 -> 4, of which waited for: 0 -> 2; matrix products, arithmetic and copies ran while one was open for 29% -> 0% of each run, Pallas kernels for 0% -> 26%
where the time goes in v4:
time: 12.6 us; the launch traced here: 12.4 us
  Pallas kernels  5.81 us (46%)
  starting transfers between devices  5.65 us (45%)
  local copies, waits for them, and re-layouts  0.45 us (4%)
  waiting for transfers between devices  0.44 us (3%)
    ppermute x4, starting transfers between devices, permute(): return lax.ppermute(value, ('leaf', 'chan'), moves)  5.65 us
    pallas_call x1, Pallas kernels, body(): call(near_kernel, part, [VMEM] * 8, [pltpu.VMEM((3 * leaves, combos, unkn...  1.64 us
    pallas_call x1, Pallas kernels, body(): call(bound(prepare_kernel), (shape((leaves, AHEAD, unknowns, unknowns), B...  1.54 us
    pallas_call x1, Pallas kernels, body(): call(final_kernel, shape(currents.shape, F32), [VMEM] * (7 + len(further)))  1.09 us
    pallas_call x1, Pallas kernels, body(): call(load_kernel, (part, shape((leaves, unknowns), F32)), [HBM] * 2, [plt...  0.91 us
    pallas_call x1, Pallas kernels, body(): call(bound(box_kernel), (shape((leaves + 1, combos, unknowns), BF16), sha...  0.63 us
    unnamed x16, local copies, waits for them, and re-layouts  0.45 us
    ppermute x4, waiting for transfers between devices, permute(): return lax.ppermute(value, ('leaf', 'chan'), moves)  0.44 us
  transfers between devices with their start and end apart: 4, of which 2 were waited for; matrix products, arithmetic and copies ran while one was open for 0% of the time, Pallas kernels for 26%

profile of v4, /device:TPU:0, one launch (start us, length us, event | category | flops | bytes accessed | tf_op | source)
XLA Modules:
  0.0 12.4 jit_solution(11164181325815770970)
XLA Ops:
  0.0 0.0 copy-start.3
  0.0 0.0 copy-start.4
  0.0 0.0 copy-start.2
  0.0 0.0 copy-start.7
  0.0 0.0 copy-start.6
  0.0 0.0 copy-start.5
  0.0 0.9 %shard_map.109 = (f32[8,8,256]{2,1,0:T(8,128)S(1)}, f32[8,256]{1,0:T(8,128)S(1)}) custom-call(s32[8]{0:T(128)} %counts.1, bf16[8,8,256]{2,1,0:T(8,128)(2,1)} %own.1), custom_call_target="tpu_custom_call" | custom-call | flops 2000000000 | tf_op jit(solution)/shard_map/pallas_call | solution.py:203
  0.9 0.0 copy-start
  1.0 0.0 copy-start.1
  1.0 0.1 copy-done.3
  1.1 0.0 copy-done.4
  1.1 0.3 %copy-done.2 = bf16[8,256,216]{1,2,0:T(8,128)(2,1)S(1)} copy-done((bf16[8,256,216]{1,2,0:T(8,128)(2,1)S(1)}, bf16[8,256,216]{1,2,0:T(8,128)(2,1)}, u32[]{:S(2)}) %copy-start.2) | copy-done | bytes 884760
  1.4 0.0 copy-done.7
  1.4 0.0 copy-done.6
  1.4 0.0 copy-done.5
  1.4 0.6 %shard_map.110 = (bf16[9,8,256]{2,1,0:T(8,128)(2,1)S(1)}, bf16[1,8,128]{2,1,0:T(8,128)(2,1)S(1)}, s32[8,6]{1,0:T(8,128)S(1)}, s32[1,16]{1,0:T(1,128)S(1)}, s32[1,16]{1,0:T(1,128)S(1)}) custom-call(f32[8,8,256]{2,1,0:T(8,128)S(1)} %get-tuple-element.17.refs_0_, bf16[8,216,256]{2,1,0:T(8,128)(2,1)S(1)} %bitcast.2, bf16[4,64,216]{2,1,0:T(8,128)(2,1)S(1)} %bitcast.4, ...), custom_call_target="tpu_custom_call" | custom-call | flops 2000000000 | tf_op jit(solution)/shard_map/pallas_call | solution.py:213
  2.0 0.5 %collective-permute-start = (bf16[1,8,128]{2,1,0:T(8,128)(2,1)S(1)}, bf16[1,8,128]{2,1,0:T(8,128)(2,1)S(1)}, u32[]{:S(2)}, u32[]{:S(2)}) collective-permute-start(bf16[1,8,128]{2,1,0:T(8,128)(2,1)S(1)} %get-tuple-element.19.box), channel_id=1, source_target_pairs={{0,1},{1,0},{2,3},{3,2},{4,5},{5,4},{6,7},{7,6},{8,9},{9,8},{10,11... | collective-permute-start | bytes 6152 | tf_op jit(solution)/shard_map/ppermute | solution.py:198
  2.5 2.6 %collective-permute-start.2 = (bf16[9,8,256]{2,1,0:T(8,128)(2,1)S(1)}, bf16[9,8,256]{2,1,0:T(8,128)(2,1)S(1)}, u32[]{:S(2)}, u32[]{:S(2)}) collective-permute-start(bf16[9,8,256]{2,1,0:T(8,128)(2,1)S(1)} %get-tuple-element.20.refs_0_.packed), channel_id=1, source_target_pairs={{0,4},{1,5},{2,6},{3,7},{4,8},{5,9},{6,10},{7,11},{8,12},{9,13},{1... | collective-permute-start | bytes 110600 | tf_op jit(solution)/shard_map/ppermute | solution.py:198
  5.1 2.1 %collective-permute-start.1 = (bf16[9,8,256]{2,1,0:T(8,128)(2,1)S(1)}, bf16[9,8,256]{2,1,0:T(8,128)(2,1)S(1)}, u32[]{:S(2)}, u32[]{:S(2)}) collective-permute-start(bf16[9,8,256]{2,1,0:T(8,128)(2,1)S(1)} %get-tuple-element.20.refs_0_.packed), channel_id=1, source_target_pairs={{0,12},{1,13},{2,14},{3,15},{4,0},{5,1},{6,2},{7,3},{8,4},{9,5},{1... | collective-permute-start | bytes 110600 | tf_op jit(solution)/shard_map/ppermute | solution.py:198
  7.2 0.0 collective-permute-done
  7.2 0.5 %collective-permute-start.3 = (bf16[1,8,128]{2,1,0:T(8,128)(2,1)S(1)}, bf16[1,8,128]{2,1,0:T(8,128)(2,1)S(1)}, u32[]{:S(2)}, u32[]{:S(2)}) collective-permute-start(bf16[1,8,128]{2,1,0:T(8,128)(2,1)S(1)} %collective-permute-done), channel_id=1, source_target_pairs={{0,9},{1,8},{2,11},{3,10},{4,13},{5,12},{6,15},{7,14},{8,1},{9,0},... | collective-permute-start | bytes 6152 | tf_op jit(solution)/shard_map/ppermute | solution.py:198
  7.7 0.0 copy-done
  7.7 0.0 copy-done.1
  7.7 1.5 %shard_map.111 = (bf16[8,2,256,256]{3,2,1,0:T(8,128)(2,1)S(1)}, f32[8,8,256]{2,1,0:T(8,128)S(1)}, bf16[8,128,256]{2,1,0:T(8,128)(2,1)S(1)}, bf16[4,128,64]{2,1,0:T(8,128)(2,1)S(1)}) custom-call(bf16[9,8,256]{2,1,0:T(8,128)(2,1)S(1)} %get-tuple-element.20.refs_0_.packed, bf16[8,6,256,256]{3,2,1,0:T(8,128)(2,1)S(1)} %copy-done, ...), custom_call_target="tpu_custom_call" | custom-call | flops 2000000000 | tf_op jit(solution)/shard_map/pallas_call | solution.py:231
  9.2 0.1 collective-permute-done.2.low
  9.3 0.3 %collective-permute-done.1.high = bf16[9,8,256]{2,1,0:T(8,128)(2,1)S(1)} collective-permute-done((bf16[9,8,256]{2,1,0:T(8,128)(2,1)S(1)}, bf16[9,8,256]{2,1,0:T(8,128)(2,1)S(1)}, u32[]{:S(2)}, u32[]{:S(2)}) %collective-permute-start.1) | collective-permute-done | bytes 36896 | tf_op jit(solution)/shard_map/ppermute | solution.py:198
  9.7 1.6 %shard_map.112.near = f32[8,8,256]{2,1,0:T(8,128)S(1)} custom-call(s32[8,6]{1,0:T(8,128)S(1)} %get-tuple-element.24.places, bf16[9,8,256]{2,1,0:T(8,128)(2,1)S(1)} %get-tuple-element.20.refs_0_.packed, bf16[9,8,256]{2,1,0:T(8,128)(2,1)S(1)} %collective-permute-done.1.high, bf16[9,8,256]{2,1,0:T(8,128)(2,1)S(1)} %collective-permute-done.2.low, ...), custom_call_target="tpu_custom_call" | custom-call | flops 1000000 | tf_op jit(solution)/shard_map/pallas_call | solution.py:248
  11.3 0.0 collective-permute-done.3.refs_0_
  11.3 1.1 %shard_map.113 = f32[8,8,256]{2,1,0:T(8,128)} custom-call(bf16[4,128,64]{2,1,0:T(8,128)(2,1)S(1)} %get-tuple-element.23.sources, f32[8,8,256]{2,1,0:T(8,128)S(1)} %shard_map.112.near, f32[8,256]{1,0:T(8,128)S(1)} %get-tuple-element.27.live, bf16[8,128,256]{2,1,0:T(8,128)(2,1)S(1)} %get-tuple-element.28.apply, bf16[1,8,128]{2,1,0:T(8,128)(2,1)S(1)} %get-tuple-element.19.box, ...), custom_call_target="tpu_custom_call" | custom-call | flops 2000000000 | tf_op jit(solution)/shard_map/pallas_call | solution.py:251
Async XLA Ops:
  0.0 1.1 %copy-start.3 = (bf16[4,8,64,64]{3,2,1,0:T(8,128)(2,1)S(1)}, bf16[4,8,64,64]{3,2,1,0:T(8,128)(2,1)}, u32[]{:S(2)}) copy-start(bf16[4,8,64,64]{3,2,1,0:T(8,128)(2,1)} %refs_4_.3) | copy-start | bytes 786436
  0.0 1.1 %copy-start.4 = (bf16[4,216,64]{1,2,0:T(8,128)(2,1)S(1)}, bf16[4,216,64]{1,2,0:T(8,128)(2,1)}, u32[]{:S(2)}) copy-start(bf16[4,216,64]{1,2,0:T(8,128)(2,1)} %param.17) | copy-start | bytes 331780
  0.0 1.4 %copy-start.2 = (bf16[8,256,216]{1,2,0:T(8,128)(2,1)S(1)}, bf16[8,256,216]{1,2,0:T(8,128)(2,1)}, u32[]{:S(2)}) copy-start(bf16[8,256,216]{1,2,0:T(8,128)(2,1)} %param.16) | copy-start | bytes 2654212
  0.0 1.4 %copy-start.7 = (s32[1,16]{1,0:T(1,128)S(1)}, s32[1,16]{1,0:T(1,128)}, u32[]{:S(2)}) copy-start(s32[1,16]{1,0:T(1,128)} %refs_6_.1) | copy-start | bytes 196
  0.0 1.4 %copy-start.6 = (s32[1,16]{1,0:T(1,128)S(1)}, s32[1,16]{1,0:T(1,128)}, u32[]{:S(2)}) copy-start(s32[1,16]{1,0:T(1,128)} %refs_5_.1) | copy-start | bytes 196
  0.0 1.4 %copy-start.5 = (s32[8,6]{1,0:T(8,128)S(1)}, s32[8,6]{1,0:T(8,128)}, u32[]{:S(2)}) copy-start(s32[8,6]{1,0:T(8,128)} %refs_4_.2) | copy-start | bytes 580
  0.9 6.7 %copy-start = (bf16[8,6,256,256]{3,2,1,0:T(8,128)(2,1)S(1)}, bf16[8,6,256,256]{3,2,1,0:T(8,128)(2,1)}, u32[]{:S(2)}) copy-start(bf16[8,6,256,256]{3,2,1,0:T(8,128)(2,1)} %tiles.1) | copy-start | bytes 18874372
  1.0 6.7 %copy-start.1 = (bf16[8,256,256]{2,1,0:T(8,128)(2,1)S(1)}, bf16[8,256,256]{2,1,0:T(8,128)(2,1)}, u32[]{:S(2)}) copy-start(bf16[8,256,256]{2,1,0:T(8,128)(2,1)} %jacobi.1) | copy-start | bytes 3145732
  2.0 5.1 %collective-permute-start = (bf16[1,8,128]{2,1,0:T(8,128)(2,1)S(1)}, bf16[1,8,128]{2,1,0:T(8,128)(2,1)S(1)}, u32[]{:S(2)}, u32[]{:S(2)}) collective-permute-start(bf16[1,8,128]{2,1,0:T(8,128)(2,1)S(1)} %get-tuple-element.19.box), channel_id=1, source_target_pairs={{0,1},{1,0},{2,3},{3,2},{4,5},{5,4},{6,7},{7,6},{8,9},{9,8},{10,11... | collective-permute-start | bytes 6152 | tf_op jit(solution)/shard_map/ppermute | solution.py:198
  2.5 6.8 %collective-permute-start.2 = (bf16[9,8,256]{2,1,0:T(8,128)(2,1)S(1)}, bf16[9,8,256]{2,1,0:T(8,128)(2,1)S(1)}, u32[]{:S(2)}, u32[]{:S(2)}) collective-permute-start(bf16[9,8,256]{2,1,0:T(8,128)(2,1)S(1)} %get-tuple-element.20.refs_0_.packed), channel_id=1, source_target_pairs={{0,4},{1,5},{2,6},{3,7},{4,8},{5,9},{6,10},{7,11},{8,12},{9,13},{1... | collective-permute-start | bytes 110600 | tf_op jit(solution)/shard_map/ppermute | solution.py:198
  5.1 4.6 %collective-permute-start.1 = (bf16[9,8,256]{2,1,0:T(8,128)(2,1)S(1)}, bf16[9,8,256]{2,1,0:T(8,128)(2,1)S(1)}, u32[]{:S(2)}, u32[]{:S(2)}) collective-permute-start(bf16[9,8,256]{2,1,0:T(8,128)(2,1)S(1)} %get-tuple-element.20.refs_0_.packed), channel_id=1, source_target_pairs={{0,12},{1,13},{2,14},{3,15},{4,0},{5,1},{6,2},{7,3},{8,4},{9,5},{1... | collective-permute-start | bytes 110600 | tf_op jit(solution)/shard_map/ppermute | solution.py:198
  7.2 4.2 %collective-permute-start.3 = (bf16[1,8,128]{2,1,0:T(8,128)(2,1)S(1)}, bf16[1,8,128]{2,1,0:T(8,128)(2,1)S(1)}, u32[]{:S(2)}, u32[]{:S(2)}) collective-permute-start(bf16[1,8,128]{2,1,0:T(8,128)(2,1)S(1)} %collective-permute-done), channel_id=1, source_target_pairs={{0,9},{1,8},{2,11},{3,10},{4,13},{5,12},{6,15},{7,14},{8,1},{9,0},... | collective-permute-start | bytes 6152 | tf_op jit(solution)/shard_map/ppermute | solution.py:198

commit v5 on v4

--- a/solution.py
+++ b/solution.py
@@ -12,7 +12,7 @@
 HBM = pl.BlockSpec(memory_space=pltpu.HBM)
 INC = 8
 COST = 2 * 10**9
-AHEAD = 2
+AHEAD = 4
 KCOST = 2000000000
 PCOST = 2000000000
 NCOST = 1000000
@@ -60,46 +60,53 @@
     return jnp.concatenate([value, value], axis=1)
 
 
-def load_kernel(counts, own, mine, live, counts_s, own_s, sems):
-    copies = [
-        pltpu.make_async_copy(counts, counts_s, sems.at[0]),
-        pltpu.make_async_copy(own, own_s, sems.at[1]),
-    ]
+def load_kernel(
+    channel, counts, own, comp_t, m2m, near_list, m2l_list, m2l_type,
+    mine, live, comp_out, m2m_out, places, slots, kinds, counts_s, own_s, near_s, list_s, sems,
+):
+    chan = channel()
+    me = lax.axis_index("leaf")
+    count = lax.axis_size("leaf")
+    pairs = (
+        (counts, counts_s),
+        (own, own_s),
+        (comp_t.at[chan], comp_out),
+        (m2m.at[chan], m2m_out),
+        (near_list, near_s),
+        (m2l_list, list_s),
+        (m2l_type, kinds),
+    )
+    copies = [pltpu.make_async_copy(a, b, sems.at[k]) for k, (a, b) in enumerate(pairs)]
     for copy in copies:
         copy.start()
     leaves, unknowns = live.shape
-    slots = lax.broadcasted_iota(jnp.int32, (1, unknowns), 1)
+    lanes = lax.broadcasted_iota(jnp.int32, (1, unknowns), 1)
     copies[0].wait()
     for leaf in range(leaves):
-        live[leaf : leaf + 1] = jnp.where(slots < counts_s[leaf], 1.0, 0.0)
+        live[leaf : leaf + 1] = jnp.where(lanes < counts_s[leaf], 1.0, 0.0)
     copies[1].wait()
     mine[...] = jnp.swapaxes(own_s[...].astype(F32), 0, 1) * live[...][:, None, :]
-
-
-def box_kernel(
-    channel, mine, interp_t, comp_t, m2m, near_list, m2l_list, m2l_type, packed, box, places, slots, kinds
-):
-    me = lax.axis_index("leaf")
-    count = lax.axis_size("leaf")
-    places[...] = near_list[...] - (me - 1) * mine.shape[0]
-    slots[...] = lax.rem(me - m2l_list[...] + count, count)
-    kinds[...] = m2l_type[...]
+    for copy in copies[2:]:
+        copy.wait()
+    places[...] = near_s[...] - (me - 1) * leaves
+    slots[...] = lax.rem(me - list_s[...] + count, count)
+
+
+def box_kernel(mine, interp_t, comp_t, m2m, packed, box):
     leaves, combos, unknowns = mine.shape
-    rank = m2m.shape[2]
     x = mine[...].astype(BF16)
     packed[0:leaves] = x
-    chan = channel()
     nodes = jnp.concatenate(
         [nt(x[leaf], interp_t[leaf]).astype(BF16) for leaf in range(leaves)], axis=0
     )
-    moments = nt(nodes, comp_t[chan]).astype(BF16)
+    moments = nt(nodes, comp_t[...]).astype(BF16)
     total = None
     for leaf in range(leaves):
-        part = nn(moments[leaf * combos : (leaf + 1) * combos], m2m[chan, leaf])
+        part = nn(moments[leaf * combos : (leaf + 1) * combos], m2m[leaf])
         total = part if total is None else total + part
     pair = twice(total).astype(BF16)
     packed[leaves] = jnp.concatenate(
-        [pair, jnp.zeros((combos, unknowns - 2 * rank), BF16)], axis=1
+        [pair, jnp.zeros((combos, unknowns - pair.shape[1]), BF16)], axis=1
     )
     box[0] = pair
 
@@ -117,7 +124,7 @@
     ]
     for copy in copies:
         copy.start()
-    comp = comp_t[chan]
+    comp = comp_t[...]
     for leaf in range(leaves):
         expand[leaf] = halves(nn(comp, interp_t[leaf]))
     for leaf in range(leaves):
@@ -126,7 +133,7 @@
             turned[leaf, k] = tiles[leaf, k + 1].T
     applied = [halves(halves_sum(nt(expand[leaf], jacobi[leaf]))) for leaf in range(leaves)]
     for leaf in range(leaves):
-        child = m2m[chan, leaf]
+        child = m2m[leaf]
         apply[leaf] = halves(tn(jnp.concatenate([child, child], axis=0), applied[leaf]))
     for copy in copies:
         copy.wait()
@@ -138,7 +145,7 @@
         sources[place] = halves(sums[place])
 
 
-def near_kernel(places, packed, high, low, tiles, turned, first, jacobi, near, beside):
+def near_kernel(places, packed, low, high, tiles, turned, first, jacobi, near, beside):
     leaves, neighbours = places.shape
     ahead = turned.shape[1]
     places = places[...]
@@ -159,7 +166,7 @@
         near[leaf] = halves_sum(nt(sums[leaf], jacobi[leaf]))
 
 
-def final_kernel(sources, near, live, apply, box, high, low, *refs):
+def final_kernel(sources, near, live, apply, box, low, high, *refs):
     *further, out = refs
     leaves, lanes = near.shape[0], box.shape[2]
     boxes = [box[0], low[leaves, :, :lanes]] + [ref[0] for ref in further] + [high[leaves, :, :lanes]]
@@ -200,28 +207,33 @@
     interp_t = jnp.swapaxes(interp, 1, 2)
     comp_t = jnp.swapaxes(compress, 1, 2)
     part = shape((leaves, combos, unknowns), F32)
-    mine, live = call(
-        load_kernel,
-        (part, shape((leaves, unknowns), F32)),
-        [HBM] * 2,
-        [
-            pltpu.SMEM((leaves,), jnp.int32),
-            pltpu.VMEM(currents.shape, BF16),
-            pltpu.SemaphoreType.DMA((2,)),
-        ],
-    )(*in_hbm(counts, currents))
-    packed, box, places, slots, kinds = call(
-        bound(box_kernel),
+    nodes = interp_t.shape[1]
+    mine, live, comp_v, m2m_v, places, slots, kinds = call(
+        bound(load_kernel),
         (
-            shape((leaves + 1, combos, unknowns), BF16),
-            shape((1, combos, 2 * rank), BF16),
+            part,
+            shape((leaves, unknowns), F32),
+            shape((rank, nodes), BF16),
+            shape((leaves, rank, rank), BF16),
             shape(near_list.shape, jnp.int32),
             shape(m2l_list.shape, jnp.int32),
             shape(m2l_type.shape, jnp.int32),
         ),
-        [VMEM] * 7,
+        [HBM] * 7,
+        [
+            pltpu.SMEM((leaves,), jnp.int32),
+            pltpu.VMEM(currents.shape, BF16),
+            pltpu.VMEM(near_list.shape, jnp.int32),
+            pltpu.VMEM(m2l_list.shape, jnp.int32),
+            pltpu.SemaphoreType.DMA((7,)),
+        ],
+    )(*in_hbm(counts, currents, comp_t, m2m, near_list, m2l_list, m2l_type))
+    packed, box = call(
+        box_kernel,
+        (shape((leaves + 1, combos, unknowns), BF16), shape((1, combos, 2 * rank), BF16)),
+        [VMEM] * 4,
         cost=KCOST,
-    )(mine, interp_t, comp_t, m2m, near_list, m2l_list, m2l_type)
+    )(mine, interp_t, comp_v, m2m_v)
     other = permute(box, 0, True)
     low = permute(packed, 1, False)
 
@@ -244,12 +256,12 @@
             pltpu.SemaphoreType.DMA((entries,)),
         ],
         PCOST,
-    )(after, near_tiles, interp_t, comp_t, m2m, slots, kinds, jacobi, *in_hbm(m2l))
+    )(after, near_tiles, interp_t, comp_v, m2m_v, slots, kinds, jacobi, *in_hbm(m2l))
     near = call(
         near_kernel, part, [VMEM] * 8, [pltpu.VMEM((3 * leaves, combos, unknowns), F32)], NCOST
-    )(places, packed, high, low, near_tiles, turned, first, jacobi)
+    )(places, packed, low, high, near_tiles, turned, first, jacobi)
     return call(final_kernel, shape(currents.shape, F32), [VMEM] * (7 + len(further)))(
-        sources, near, live, apply, box, high, low, *further
+        sources, near, live, apply, box, low, high, *further
     )
 
 

time: 12.6 us -> 12.2 us (0.968)
  local copies, waits for them, and re-layouts: 0.45 us -> 0.19 us
  waiting for transfers between devices: 0.44 us -> 0.22 us
  Pallas kernels: 5.81 us -> 5.96 us
    pallas_call x1, Pallas kernels: 1.64 us -> 1.34 us  [body(): call(near_kernel, part, [VMEM] * 8, [pltpu.VMEM((3 * leaves, combos, unkn...]
    pallas_call x1, Pallas kernels: 1.54 us -> 1.8 us  [body(): call(bound(prepare_kernel), (shape((leaves, AHEAD, unknowns, unknowns), B...]
    unnamed x16 -> x6, local copies, waits for them, and re-layouts: 0.45 us -> 0.19 us
    ppermute x4, waiting for transfers between devices: 0.44 us -> 0.22 us  [permute(): return lax.ppermute(value, ('leaf', 'chan'), moves)]
    pallas_call x2, Pallas kernels: 1.55 us -> 1.73 us  [the longest x1 1.1 us: body(): call(bound(load_kernel), (part, shape((leaves, unknowns), F32), shape((ra...]
where the time goes in v5:
time: 12.2 us; the launch traced here: 12.1 us
  Pallas kernels  5.96 us (49%)
  starting transfers between devices  5.65 us (46%)
  waiting for transfers between devices  0.22 us (2%)
  local copies, waits for them, and re-layouts  0.19 us (2%)
    ppermute x4, starting transfers between devices, permute(): return lax.ppermute(value, ('leaf', 'chan'), moves)  5.65 us
    pallas_call x1, Pallas kernels, body(): call(bound(prepare_kernel), (shape((leaves, AHEAD, unknowns, unknowns), B...  1.8 us
    pallas_call x1, Pallas kernels, body(): call(near_kernel, part, [VMEM] * 8, [pltpu.VMEM((3 * leaves, combos, unkn...  1.34 us
    pallas_call x1, Pallas kernels, body(): call(bound(load_kernel), (part, shape((leaves, unknowns), F32), shape((ra...  1.1 us
    pallas_call x1, Pallas kernels, body(): call(final_kernel, shape(currents.shape, F32), [VMEM] * (7 + len(further)))  1.08 us
    pallas_call x1, Pallas kernels, body(): call(box_kernel, (shape((leaves + 1, combos, unknowns), BF16), shape((1,...  0.63 us
  transfers between devices with their start and end apart: 4, of which 2 were waited for; matrix products, arithmetic and copies ran while one was open for 0% of the time, Pallas kernels for 26%

profile of v5, /device:TPU:0, one launch (start us, length us, event | category | flops | bytes accessed | tf_op | source)
XLA Modules:
  0.0 12.1 jit_solution(1288705462227294265)
XLA Ops:
  0.0 0.0 copy-start.2
  0.0 1.1 %shard_map.109 = (f32[8,8,256]{2,1,0:T(8,128)S(1)}, f32[8,256]{1,0:T(8,128)S(1)}, bf16[64,216]{1,0:T(8,128)(2,1)S(1)}, bf16[8,64,64]{2,1,0:T(8,128)(2,1)S(1)}, s...) custom-call(s32[8]{0:T(128)} %refs_0_.1, bf16[8,8,256]{2,1,0:T(8,128)(2,1)} %refs_1_.2, ...), custom_call_target="tpu_custom_call" | custom-call | flops 2000000000 | tf_op jit(solution)/shard_map/pallas_call | solution.py:211
  1.1 0.0 copy-start
  1.1 0.0 copy-start.1
  1.1 0.2 %copy-done.2 = bf16[8,256,216]{1,2,0:T(8,128)(2,1)S(1)} copy-done((bf16[8,256,216]{1,2,0:T(8,128)(2,1)S(1)}, bf16[8,256,216]{1,2,0:T(8,128)(2,1)}, u32[]{:S(2)}) %copy-start.2) | copy-done | bytes 884760
  1.3 0.6 %shard_map.110 = (bf16[9,8,256]{2,1,0:T(8,128)(2,1)S(1)}, bf16[1,8,128]{2,1,0:T(8,128)(2,1)S(1)}) custom-call(f32[8,8,256]{2,1,0:T(8,128)S(1)} %get-tuple-element.19.mine, bf16[8,216,256]{2,1,0:T(8,128)(2,1)S(1)} %bitcast.2, bf16[64,216]{1,0:T(8,128)(2,1)S(1)} %get-tuple-element.20.comp_t.refs_3_, bf16[8,64,64]{2,1,0:T(8,128)(2,1)S(1)} %get-tuple-element.21.m2m.refs_4_), custom_call_target="tpu_custom_call" | custom-call | flops 2000000000 | tf_op jit(solution)/shard_map/pallas_call | solution.py:231
  1.9 0.5 %collective-permute-start = (bf16[1,8,128]{2,1,0:T(8,128)(2,1)S(1)}, bf16[1,8,128]{2,1,0:T(8,128)(2,1)S(1)}, u32[]{:S(2)}, u32[]{:S(2)}) collective-permute-start(bf16[1,8,128]{2,1,0:T(8,128)(2,1)S(1)} %get-tuple-element.23.box), channel_id=1, source_target_pairs={{0,1},{1,0},{2,3},{3,2},{4,5},{5,4},{6,7},{7,6},{8,9},{9,8},{10,11... | collective-permute-start | bytes 6152 | tf_op jit(solution)/shard_map/ppermute | solution.py:205
  2.4 2.6 %collective-permute-start.1 = (bf16[9,8,256]{2,1,0:T(8,128)(2,1)S(1)}, bf16[9,8,256]{2,1,0:T(8,128)(2,1)S(1)}, u32[]{:S(2)}, u32[]{:S(2)}) collective-permute-start(bf16[9,8,256]{2,1,0:T(8,128)(2,1)S(1)} %get-tuple-element.24.refs_0_.packed), channel_id=1, source_target_pairs={{0,4},{1,5},{2,6},{3,7},{4,8},{5,9},{6,10},{7,11},{8,12},{9,13},{1... | collective-permute-start | bytes 110600 | tf_op jit(solution)/shard_map/ppermute | solution.py:205
  5.0 2.1 %collective-permute-start.2 = (bf16[9,8,256]{2,1,0:T(8,128)(2,1)S(1)}, bf16[9,8,256]{2,1,0:T(8,128)(2,1)S(1)}, u32[]{:S(2)}, u32[]{:S(2)}) collective-permute-start(bf16[9,8,256]{2,1,0:T(8,128)(2,1)S(1)} %get-tuple-element.24.refs_0_.packed), channel_id=1, source_target_pairs={{0,12},{1,13},{2,14},{3,15},{4,0},{5,1},{6,2},{7,3},{8,4},{9,5},{1... | collective-permute-start | bytes 110600 | tf_op jit(solution)/shard_map/ppermute | solution.py:205
  7.1 0.0 collective-permute-done
  7.1 0.5 %collective-permute-start.3 = (bf16[1,8,128]{2,1,0:T(8,128)(2,1)S(1)}, bf16[1,8,128]{2,1,0:T(8,128)(2,1)S(1)}, u32[]{:S(2)}, u32[]{:S(2)}) collective-permute-start(bf16[1,8,128]{2,1,0:T(8,128)(2,1)S(1)} %collective-permute-done), channel_id=1, source_target_pairs={{0,9},{1,8},{2,11},{3,10},{4,13},{5,12},{6,15},{7,14},{8,1},{9,0},... | collective-permute-start | bytes 6152 | tf_op jit(solution)/shard_map/ppermute | solution.py:205
  7.6 0.0 copy-done
  7.6 0.0 copy-done.1
  7.6 1.8 %shard_map.111 = (bf16[8,4,256,256]{3,2,1,0:T(8,128)(2,1)S(1)}, f32[8,8,256]{2,1,0:T(8,128)S(1)}, bf16[8,128,256]{2,1,0:T(8,128)(2,1)S(1)}, bf16[4,128,64]{2,1,0:T(8,128)(2,1)S(1)}) custom-call(bf16[9,8,256]{2,1,0:T(8,128)(2,1)S(1)} %get-tuple-element.24.refs_0_.packed, bf16[8,6,256,256]{3,2,1,0:T(8,128)(2,1)S(1)} %copy-done, ...), custom_call_target="tpu_custom_call" | custom-call | flops 2000000000 | tf_op jit(solution)/shard_map/pallas_call | solution.py:243
  9.4 0.0 collective-permute-done.1.low
  9.4 0.1 %collective-permute-done.2.high = bf16[9,8,256]{2,1,0:T(8,128)(2,1)S(1)} collective-permute-done((bf16[9,8,256]{2,1,0:T(8,128)(2,1)S(1)}, bf16[9,8,256]{2,1,0:T(8,128)(2,1)S(1)}, u32[]{:S(2)}, u32[]{:S(2)}) %collective-permute-start.2) | collective-permute-done | bytes 36896 | tf_op jit(solution)/shard_map/ppermute | solution.py:205
  9.6 1.3 %shard_map.112.near = f32[8,8,256]{2,1,0:T(8,128)S(1)} custom-call(s32[8,6]{1,0:T(8,128)S(1)} %get-tuple-element.28.places, bf16[9,8,256]{2,1,0:T(8,128)(2,1)S(1)} %get-tuple-element.24.refs_0_.packed, bf16[9,8,256]{2,1,0:T(8,128)(2,1)S(1)} %collective-permute-done.1.low, bf16[9,8,256]{2,1,0:T(8,128)(2,1)S(1)} %collective-permute-done.2.high, ...), custom_call_target="tpu_custom_call" | custom-call | flops 1000000 | tf_op jit(solution)/shard_map/pallas_call | solution.py:260
  10.9 0.1 collective-permute-done.3.refs_0_
  11.0 1.1 %shard_map.113 = f32[8,8,256]{2,1,0:T(8,128)} custom-call(bf16[4,128,64]{2,1,0:T(8,128)(2,1)S(1)} %get-tuple-element.27.sources, f32[8,8,256]{2,1,0:T(8,128)S(1)} %shard_map.112.near, f32[8,256]{1,0:T(8,128)S(1)} %get-tuple-element.31.live, bf16[8,128,256]{2,1,0:T(8,128)(2,1)S(1)} %get-tuple-element.32.apply, bf16[1,8,128]{2,1,0:T(8,128)(2,1)S(1)} %get-tuple-element.23.box, ...), custom_call_target="tpu_custom_call" | custom-call | flops 2000000000 | tf_op jit(solution)/shard_map/pallas_call | solution.py:263
Async XLA Ops:
  0.0 1.3 %copy-start.2 = (bf16[8,256,216]{1,2,0:T(8,128)(2,1)S(1)}, bf16[8,256,216]{1,2,0:T(8,128)(2,1)}, u32[]{:S(2)}) copy-start(bf16[8,256,216]{1,2,0:T(8,128)(2,1)} %param.16) | copy-start | bytes 2654212
  1.1 6.5 %copy-start = (bf16[8,6,256,256]{3,2,1,0:T(8,128)(2,1)S(1)}, bf16[8,6,256,256]{3,2,1,0:T(8,128)(2,1)}, u32[]{:S(2)}) copy-start(bf16[8,6,256,256]{3,2,1,0:T(8,128)(2,1)} %tiles.1) | copy-start | bytes 18874372
  1.1 6.5 %copy-start.1 = (bf16[8,256,256]{2,1,0:T(8,128)(2,1)S(1)}, bf16[8,256,256]{2,1,0:T(8,128)(2,1)}, u32[]{:S(2)}) copy-start(bf16[8,256,256]{2,1,0:T(8,128)(2,1)} %jacobi.1) | copy-start | bytes 3145732
  1.9 5.1 %collective-permute-start = (bf16[1,8,128]{2,1,0:T(8,128)(2,1)S(1)}, bf16[1,8,128]{2,1,0:T(8,128)(2,1)S(1)}, u32[]{:S(2)}, u32[]{:S(2)}) collective-permute-start(bf16[1,8,128]{2,1,0:T(8,128)(2,1)S(1)} %get-tuple-element.23.box), channel_id=1, source_target_pairs={{0,1},{1,0},{2,3},{3,2},{4,5},{5,4},{6,7},{7,6},{8,9},{9,8},{10,11... | collective-permute-start | bytes 6152 | tf_op jit(solution)/shard_map/ppermute | solution.py:205
  2.4 7.0 %collective-permute-start.1 = (bf16[9,8,256]{2,1,0:T(8,128)(2,1)S(1)}, bf16[9,8,256]{2,1,0:T(8,128)(2,1)S(1)}, u32[]{:S(2)}, u32[]{:S(2)}) collective-permute-start(bf16[9,8,256]{2,1,0:T(8,128)(2,1)S(1)} %get-tuple-element.24.refs_0_.packed), channel_id=1, source_target_pairs={{0,4},{1,5},{2,6},{3,7},{4,8},{5,9},{6,10},{7,11},{8,12},{9,13},{1... | collective-permute-start | bytes 110600 | tf_op jit(solution)/shard_map/ppermute | solution.py:205
  5.0 4.6 %collective-permute-start.2 = (bf16[9,8,256]{2,1,0:T(8,128)(2,1)S(1)}, bf16[9,8,256]{2,1,0:T(8,128)(2,1)S(1)}, u32[]{:S(2)}, u32[]{:S(2)}) collective-permute-start(bf16[9,8,256]{2,1,0:T(8,128)(2,1)S(1)} %get-tuple-element.24.refs_0_.packed), channel_id=1, source_target_pairs={{0,12},{1,13},{2,14},{3,15},{4,0},{5,1},{6,2},{7,3},{8,4},{9,5},{1... | collective-permute-start | bytes 110600 | tf_op jit(solution)/shard_map/ppermute | solution.py:205
  7.1 3.9 %collective-permute-start.3 = (bf16[1,8,128]{2,1,0:T(8,128)(2,1)S(1)}, bf16[1,8,128]{2,1,0:T(8,128)(2,1)S(1)}, u32[]{:S(2)}, u32[]{:S(2)}) collective-permute-start(bf16[1,8,128]{2,1,0:T(8,128)(2,1)S(1)} %collective-permute-done), channel_id=1, source_target_pairs={{0,9},{1,8},{2,11},{3,10},{4,13},{5,12},{6,15},{7,14},{8,1},{9,0},... | collective-permute-start | bytes 6152 | tf_op jit(solution)/shard_map/ppermute | solution.py:205

commit v6 on v5

--- a/solution.py
+++ b/solution.py
@@ -170,14 +170,10 @@
     *further, out = refs
     leaves, lanes = near.shape[0], box.shape[2]
     boxes = [box[0], low[leaves, :, :lanes]] + [ref[0] for ref in further] + [high[leaves, :, :lanes]]
-    local = None
-    for slot in range(sources.shape[0]):
-        part = nn(boxes[slot], sources[slot])
-        local = part if local is None else local + part
+    local = nn(jnp.concatenate(boxes, axis=1), sources[...].reshape(-1, sources.shape[2]))
     local = twice(local).astype(BF16)
-    for leaf in range(near.shape[0]):
-        far = nn(local, apply[leaf])
-        out[:, leaf, :] = (near[leaf] + far) * live[leaf : leaf + 1]
+    done = [(near[leaf] + nn(local, apply[leaf])) * live[leaf : leaf + 1] for leaf in range(near.shape[0])]
+    out[...] = jnp.swapaxes(jnp.stack(done), 0, 1)
 
 
 def body(

time: 12.2 us -> 12.1 us (level)
  no operation moved by 1% of the time
where the time goes in v6:
time: 12.1 us; the launch traced here: 12 us
  Pallas kernels  5.88 us (49%)
  starting transfers between devices  5.65 us (47%)
  waiting for transfers between devices  0.22 us (2%)
  local copies, waits for them, and re-layouts  0.19 us (2%)
    ppermute x4, starting transfers between devices, permute(): return lax.ppermute(value, ('leaf', 'chan'), moves)  5.65 us
    pallas_call x1, Pallas kernels, body(): call(bound(prepare_kernel), (shape((leaves, AHEAD, unknowns, unknowns), B...  1.8 us
    pallas_call x1, Pallas kernels, body(): call(near_kernel, part, [VMEM] * 8, [pltpu.VMEM((3 * leaves, combos, unkn...  1.35 us
    pallas_call x1, Pallas kernels, body(): call(bound(load_kernel), (part, shape((leaves, unknowns), F32), shape((ra...  1.1 us
    pallas_call x1, Pallas kernels, body(): call(final_kernel, shape(currents.shape, F32), [VMEM] * (7 + len(further)))  1.01 us
    pallas_call x1, Pallas kernels, body(): call(box_kernel, (shape((leaves + 1, combos, unknowns), BF16), shape((1,...  0.63 us
  transfers between devices with their start and end apart: 4, of which 2 were waited for; matrix products, arithmetic and copies ran while one was open for 0% of the time, Pallas kernels for 26%

profile of v6, /device:TPU:0, one launch (start us, length us, event | category | flops | bytes accessed | tf_op | source)
XLA Modules:
  0.0 12.0 jit_solution(3074426300899956604)
XLA Ops:
  0.0 0.0 copy-start.2
  0.0 1.1 %shard_map.109 = (f32[8,8,256]{2,1,0:T(8,128)S(1)}, f32[8,256]{1,0:T(8,128)S(1)}, bf16[64,216]{1,0:T(8,128)(2,1)S(1)}, bf16[8,64,64]{2,1,0:T(8,128)(2,1)S(1)}, s...) custom-call(s32[8]{0:T(128)} %refs_0_.1, bf16[8,8,256]{2,1,0:T(8,128)(2,1)} %refs_1_.2, ...), custom_call_target="tpu_custom_call" | custom-call | flops 2000000000 | tf_op jit(solution)/shard_map/pallas_call | solution.py:207
  1.1 0.0 copy-start
  1.1 0.0 copy-start.1
  1.1 0.2 %copy-done.2 = bf16[8,256,216]{1,2,0:T(8,128)(2,1)S(1)} copy-done((bf16[8,256,216]{1,2,0:T(8,128)(2,1)S(1)}, bf16[8,256,216]{1,2,0:T(8,128)(2,1)}, u32[]{:S(2)}) %copy-start.2) | copy-done | bytes 884760
  1.3 0.6 %shard_map.110 = (bf16[9,8,256]{2,1,0:T(8,128)(2,1)S(1)}, bf16[1,8,128]{2,1,0:T(8,128)(2,1)S(1)}) custom-call(f32[8,8,256]{2,1,0:T(8,128)S(1)} %get-tuple-element.19.mine, bf16[8,216,256]{2,1,0:T(8,128)(2,1)S(1)} %bitcast.2, bf16[64,216]{1,0:T(8,128)(2,1)S(1)} %get-tuple-element.20.comp_t.refs_3_, bf16[8,64,64]{2,1,0:T(8,128)(2,1)S(1)} %get-tuple-element.21.m2m.refs_4_), custom_call_target="tpu_custom_call" | custom-call | flops 2000000000 | tf_op jit(solution)/shard_map/pallas_call | solution.py:227
  1.9 0.5 %collective-permute-start = (bf16[1,8,128]{2,1,0:T(8,128)(2,1)S(1)}, bf16[1,8,128]{2,1,0:T(8,128)(2,1)S(1)}, u32[]{:S(2)}, u32[]{:S(2)}) collective-permute-start(bf16[1,8,128]{2,1,0:T(8,128)(2,1)S(1)} %get-tuple-element.23.box), channel_id=1, source_target_pairs={{0,1},{1,0},{2,3},{3,2},{4,5},{5,4},{6,7},{7,6},{8,9},{9,8},{10,11... | collective-permute-start | bytes 6152 | tf_op jit(solution)/shard_map/ppermute | solution.py:201
  2.4 2.6 %collective-permute-start.1 = (bf16[9,8,256]{2,1,0:T(8,128)(2,1)S(1)}, bf16[9,8,256]{2,1,0:T(8,128)(2,1)S(1)}, u32[]{:S(2)}, u32[]{:S(2)}) collective-permute-start(bf16[9,8,256]{2,1,0:T(8,128)(2,1)S(1)} %get-tuple-element.24.refs_0_.packed), channel_id=1, source_target_pairs={{0,4},{1,5},{2,6},{3,7},{4,8},{5,9},{6,10},{7,11},{8,12},{9,13},{1... | collective-permute-start | bytes 110600 | tf_op jit(solution)/shard_map/ppermute | solution.py:201
  5.0 2.1 %collective-permute-start.2 = (bf16[9,8,256]{2,1,0:T(8,128)(2,1)S(1)}, bf16[9,8,256]{2,1,0:T(8,128)(2,1)S(1)}, u32[]{:S(2)}, u32[]{:S(2)}) collective-permute-start(bf16[9,8,256]{2,1,0:T(8,128)(2,1)S(1)} %get-tuple-element.24.refs_0_.packed), channel_id=1, source_target_pairs={{0,12},{1,13},{2,14},{3,15},{4,0},{5,1},{6,2},{7,3},{8,4},{9,5},{1... | collective-permute-start | bytes 110600 | tf_op jit(solution)/shard_map/ppermute | solution.py:201
  7.1 0.0 collective-permute-done
  7.1 0.5 %collective-permute-start.3 = (bf16[1,8,128]{2,1,0:T(8,128)(2,1)S(1)}, bf16[1,8,128]{2,1,0:T(8,128)(2,1)S(1)}, u32[]{:S(2)}, u32[]{:S(2)}) collective-permute-start(bf16[1,8,128]{2,1,0:T(8,128)(2,1)S(1)} %collective-permute-done), channel_id=1, source_target_pairs={{0,9},{1,8},{2,11},{3,10},{4,13},{5,12},{6,15},{7,14},{8,1},{9,0},... | collective-permute-start | bytes 6152 | tf_op jit(solution)/shard_map/ppermute | solution.py:201
  7.6 0.0 copy-done
  7.6 0.0 copy-done.1
  7.6 1.8 %shard_map.111 = (bf16[8,4,256,256]{3,2,1,0:T(8,128)(2,1)S(1)}, f32[8,8,256]{2,1,0:T(8,128)S(1)}, bf16[8,128,256]{2,1,0:T(8,128)(2,1)S(1)}, bf16[4,128,64]{2,1,0:T(8,128)(2,1)S(1)}) custom-call(bf16[9,8,256]{2,1,0:T(8,128)(2,1)S(1)} %get-tuple-element.24.refs_0_.packed, bf16[8,6,256,256]{3,2,1,0:T(8,128)(2,1)S(1)} %copy-done, ...), custom_call_target="tpu_custom_call" | custom-call | flops 2000000000 | tf_op jit(solution)/shard_map/pallas_call | solution.py:239
  9.4 0.0 collective-permute-done.1.low
  9.4 0.2 %collective-permute-done.2.high = bf16[9,8,256]{2,1,0:T(8,128)(2,1)S(1)} collective-permute-done((bf16[9,8,256]{2,1,0:T(8,128)(2,1)S(1)}, bf16[9,8,256]{2,1,0:T(8,128)(2,1)S(1)}, u32[]{:S(2)}, u32[]{:S(2)}) %collective-permute-start.2) | collective-permute-done | bytes 36896 | tf_op jit(solution)/shard_map/ppermute | solution.py:201
  9.6 1.3 %shard_map.112.near = f32[8,8,256]{2,1,0:T(8,128)S(1)} custom-call(s32[8,6]{1,0:T(8,128)S(1)} %get-tuple-element.28.places, bf16[9,8,256]{2,1,0:T(8,128)(2,1)S(1)} %get-tuple-element.24.refs_0_.packed, bf16[9,8,256]{2,1,0:T(8,128)(2,1)S(1)} %collective-permute-done.1.low, bf16[9,8,256]{2,1,0:T(8,128)(2,1)S(1)} %collective-permute-done.2.high, ...), custom_call_target="tpu_custom_call" | custom-call | flops 1000000 | tf_op jit(solution)/shard_map/pallas_call | solution.py:256
  10.9 0.1 collective-permute-done.3.refs_0_
  11.0 1.0 %shard_map.113 = f32[8,8,256]{2,1,0:T(8,128)} custom-call(bf16[4,128,64]{2,1,0:T(8,128)(2,1)S(1)} %get-tuple-element.27.sources, f32[8,8,256]{2,1,0:T(8,128)S(1)} %shard_map.112.near, f32[8,256]{1,0:T(8,128)S(1)} %get-tuple-element.31.live, bf16[8,128,256]{2,1,0:T(8,128)(2,1)S(1)} %get-tuple-element.32.apply, bf16[1,8,128]{2,1,0:T(8,128)(2,1)S(1)} %get-tuple-element.23.box, ...), custom_call_target="tpu_custom_call" | custom-call | flops 2000000000 | tf_op jit(solution)/shard_map/pallas_call | solution.py:259
Async XLA Ops:
  0.0 1.3 %copy-start.2 = (bf16[8,256,216]{1,2,0:T(8,128)(2,1)S(1)}, bf16[8,256,216]{1,2,0:T(8,128)(2,1)}, u32[]{:S(2)}) copy-start(bf16[8,256,216]{1,2,0:T(8,128)(2,1)} %param.16) | copy-start | bytes 2654212
  1.1 6.5 %copy-start = (bf16[8,6,256,256]{3,2,1,0:T(8,128)(2,1)S(1)}, bf16[8,6,256,256]{3,2,1,0:T(8,128)(2,1)}, u32[]{:S(2)}) copy-start(bf16[8,6,256,256]{3,2,1,0:T(8,128)(2,1)} %tiles.1) | copy-start | bytes 18874372
  1.1 6.5 %copy-start.1 = (bf16[8,256,256]{2,1,0:T(8,128)(2,1)S(1)}, bf16[8,256,256]{2,1,0:T(8,128)(2,1)}, u32[]{:S(2)}) copy-start(bf16[8,256,256]{2,1,0:T(8,128)(2,1)} %jacobi.1) | copy-start | bytes 3145732
  1.9 5.1 %collective-permute-start = (bf16[1,8,128]{2,1,0:T(8,128)(2,1)S(1)}, bf16[1,8,128]{2,1,0:T(8,128)(2,1)S(1)}, u32[]{:S(2)}, u32[]{:S(2)}) collective-permute-start(bf16[1,8,128]{2,1,0:T(8,128)(2,1)S(1)} %get-tuple-element.23.box), channel_id=1, source_target_pairs={{0,1},{1,0},{2,3},{3,2},{4,5},{5,4},{6,7},{7,6},{8,9},{9,8},{10,11... | collective-permute-start | bytes 6152 | tf_op jit(solution)/shard_map/ppermute | solution.py:201
  2.4 7.0 %collective-permute-start.1 = (bf16[9,8,256]{2,1,0:T(8,128)(2,1)S(1)}, bf16[9,8,256]{2,1,0:T(8,128)(2,1)S(1)}, u32[]{:S(2)}, u32[]{:S(2)}) collective-permute-start(bf16[9,8,256]{2,1,0:T(8,128)(2,1)S(1)} %get-tuple-element.24.refs_0_.packed), channel_id=1, source_target_pairs={{0,4},{1,5},{2,6},{3,7},{4,8},{5,9},{6,10},{7,11},{8,12},{9,13},{1... | collective-permute-start | bytes 110600 | tf_op jit(solution)/shard_map/ppermute | solution.py:201
  5.0 4.6 %collective-permute-start.2 = (bf16[9,8,256]{2,1,0:T(8,128)(2,1)S(1)}, bf16[9,8,256]{2,1,0:T(8,128)(2,1)S(1)}, u32[]{:S(2)}, u32[]{:S(2)}) collective-permute-start(bf16[9,8,256]{2,1,0:T(8,128)(2,1)S(1)} %get-tuple-element.24.refs_0_.packed), channel_id=1, source_target_pairs={{0,12},{1,13},{2,14},{3,15},{4,0},{5,1},{6,2},{7,3},{8,4},{9,5},{1... | collective-permute-start | bytes 110600 | tf_op jit(solution)/shard_map/ppermute | solution.py:201
  7.1 3.9 %collective-permute-start.3 = (bf16[1,8,128]{2,1,0:T(8,128)(2,1)S(1)}, bf16[1,8,128]{2,1,0:T(8,128)(2,1)S(1)}, u32[]{:S(2)}, u32[]{:S(2)}) collective-permute-start(bf16[1,8,128]{2,1,0:T(8,128)(2,1)S(1)} %collective-permute-done), channel_id=1, source_target_pairs={{0,9},{1,8},{2,11},{3,10},{4,13},{5,12},{6,15},{7,14},{8,1},{9,0},... | collective-permute-start | bytes 6152 | tf_op jit(solution)/shard_map/ppermute | solution.py:201

commit v7 on v6

--- a/solution.py
+++ b/solution.py
@@ -113,7 +113,7 @@
 
 def prepare_kernel(
     channel, packed, tiles, interp_t, comp_t, m2m, slots, kinds, jacobi, table,
-    turned, first, apply, sources, expand, mats, sums, mat_sems,
+    turned, first, apply, back, sources, expand, mats, sums, mat_sems,
 ):
     leaves = first.shape[0]
     chan = channel()
@@ -126,7 +126,10 @@
         copy.start()
     comp = comp_t[...]
     for leaf in range(leaves):
-        expand[leaf] = halves(nn(comp, interp_t[leaf]))
+        top = jnp.max(jnp.abs(jacobi[leaf]).astype(F32), axis=(0, 1), keepdims=True)
+        scale = jnp.where(top > 2.0**90, 2.0**-30, jnp.where(top < 2.0**-90, 2.0**30, 1.0))
+        back[leaf : leaf + 1] = jnp.broadcast_to(1.0 / scale, (1, back.shape[1]))
+        expand[leaf] = halves(nn(comp, interp_t[leaf]) * scale)
     for leaf in range(leaves):
         first[leaf] = nt(packed[leaf], tiles[leaf, 0])
         for k in range(turned.shape[1]):
@@ -166,13 +169,16 @@
         near[leaf] = halves_sum(nt(sums[leaf], jacobi[leaf]))
 
 
-def final_kernel(sources, near, live, apply, box, low, high, *refs):
+def final_kernel(sources, near, live, back, apply, box, low, high, *refs):
     *further, out = refs
     leaves, lanes = near.shape[0], box.shape[2]
     boxes = [box[0], low[leaves, :, :lanes]] + [ref[0] for ref in further] + [high[leaves, :, :lanes]]
     local = nn(jnp.concatenate(boxes, axis=1), sources[...].reshape(-1, sources.shape[2]))
     local = twice(local).astype(BF16)
-    done = [(near[leaf] + nn(local, apply[leaf])) * live[leaf : leaf + 1] for leaf in range(near.shape[0])]
+    done = []
+    for leaf in range(leaves):
+        row = slice(leaf, leaf + 1)
+        done.append((near[leaf] + nn(local, apply[leaf]) * back[row]) * live[row])
     out[...] = jnp.swapaxes(jnp.stack(done), 0, 1)
 
 
@@ -236,12 +242,13 @@
     high = permute(packed, -1, False)
     further = [permute(other, shift, True) for shift in range(2, n - 1)]
     after, _ = lax.optimization_barrier((packed, other))
-    turned, first, apply, sources = call(
+    turned, first, apply, back, sources = call(
         bound(prepare_kernel),
         (
             shape((leaves, AHEAD, unknowns, unknowns), BF16),
             part,
             shape((leaves, 2 * rank, unknowns), BF16),
+            shape((leaves, unknowns), F32),
             shape((n, 2 * rank, rank), BF16),
         ),
         [VMEM] * 8 + [HBM],
@@ -256,8 +263,8 @@
     near = call(
         near_kernel, part, [VMEM] * 8, [pltpu.VMEM((3 * leaves, combos, unknowns), F32)], NCOST
     )(places, packed, low, high, near_tiles, turned, first, jacobi)
-    return call(final_kernel, shape(currents.shape, F32), [VMEM] * (7 + len(further)))(
-        sources, near, live, apply, box, low, high, *further
+    return call(final_kernel, shape(currents.shape, F32), [VMEM] * (8 + len(further)))(
+        sources, near, live, back, apply, box, low, high, *further
     )
 
 

time: 12.1 us -> 12.3 us (1.017)
  the two profiles are of different devices: /device:TPU:0 before, /device:TPU:1 now
where the time goes in v7:
time: 12.3 us; the launch traced here: 12.1 us
  Pallas kernels  6.11 us (50%)
  starting transfers between devices  5.76 us (47%)
  local copies, waits for them, and re-layouts  0.19 us (2%)
    ppermute x4, starting transfers between devices, permute(): return lax.ppermute(value, ('leaf', 'chan'), moves)  5.76 us
    pallas_call x1, Pallas kernels, body(): call(bound(prepare_kernel), (shape((leaves, AHEAD, unknowns, unknowns), B...  2.02 us
    pallas_call x1, Pallas kernels, body(): call(near_kernel, part, [VMEM] * 8, [pltpu.VMEM((3 * leaves, combos, unkn...  1.35 us
    pallas_call x1, Pallas kernels, body(): call(bound(load_kernel), (part, shape((leaves, unknowns), F32), shape((ra...  1.1 us
    pallas_call x1, Pallas kernels, body(): call(final_kernel, shape(currents.shape, F32), [VMEM] * (8 + len(further)))  1.01 us
    pallas_call x1, Pallas kernels, body(): call(box_kernel, (shape((leaves + 1, combos, unknowns), BF16), shape((1,...  0.63 us
  transfers between devices with their start and end apart: 4, of which 0 were waited for; matrix products, arithmetic and copies ran while one was open for 0% of the time, Pallas kernels for 28%

profile of v7, /device:TPU:1, one launch (start us, length us, event | category | flops | bytes accessed | tf_op | source)
XLA Modules:
  0.0 12.1 jit_solution(18285804020753870593)
XLA Ops:
  0.0 0.0 copy-start.2
  0.0 1.1 %shard_map.109 = (f32[8,8,256]{2,1,0:T(8,128)S(1)}, f32[8,256]{1,0:T(8,128)S(1)}, bf16[64,216]{1,0:T(8,128)(2,1)S(1)}, bf16[8,64,64]{2,1,0:T(8,128)(2,1)S(1)}, s...) custom-call(s32[8]{0:T(128)} %refs_0_.1, bf16[8,8,256]{2,1,0:T(8,128)(2,1)} %refs_1_.2, ...), custom_call_target="tpu_custom_call" | custom-call | flops 2000000000 | tf_op jit(solution)/shard_map/pallas_call | solution.py:213
  1.1 0.0 copy-start
  1.1 0.0 copy-start.1
  1.1 0.2 %copy-done.2 = bf16[8,256,216]{1,2,0:T(8,128)(2,1)S(1)} copy-done((bf16[8,256,216]{1,2,0:T(8,128)(2,1)S(1)}, bf16[8,256,216]{1,2,0:T(8,128)(2,1)}, u32[]{:S(2)}) %copy-start.2) | copy-done | bytes 884760
  1.3 0.6 %shard_map.110 = (bf16[9,8,256]{2,1,0:T(8,128)(2,1)S(1)}, bf16[1,8,128]{2,1,0:T(8,128)(2,1)S(1)}) custom-call(f32[8,8,256]{2,1,0:T(8,128)S(1)} %get-tuple-element.20.mine, bf16[8,216,256]{2,1,0:T(8,128)(2,1)S(1)} %bitcast.2, bf16[64,216]{1,0:T(8,128)(2,1)S(1)} %get-tuple-element.21.comp_t.refs_3_, bf16[8,64,64]{2,1,0:T(8,128)(2,1)S(1)} %get-tuple-element.22.m2m.refs_4_), custom_call_target="tpu_custom_call" | custom-call | flops 2000000000 | tf_op jit(solution)/shard_map/pallas_call | solution.py:233
  1.9 0.1 collective-permute-start
  2.0 2.7 %collective-permute-start.1 = (bf16[9,8,256]{2,1,0:T(8,128)(2,1)S(1)}, bf16[9,8,256]{2,1,0:T(8,128)(2,1)S(1)}, u32[]{:S(2)}, u32[]{:S(2)}) collective-permute-start(bf16[9,8,256]{2,1,0:T(8,128)(2,1)S(1)} %get-tuple-element.25.refs_0_.packed), channel_id=1, source_target_pairs={{0,4},{1,5},{2,6},{3,7},{4,8},{5,9},{6,10},{7,11},{8,12},{9,13},{1... | collective-permute-start | bytes 110600 | tf_op jit(solution)/shard_map/ppermute | solution.py:207
  4.8 2.0 %collective-permute-start.2 = (bf16[9,8,256]{2,1,0:T(8,128)(2,1)S(1)}, bf16[9,8,256]{2,1,0:T(8,128)(2,1)S(1)}, u32[]{:S(2)}, u32[]{:S(2)}) collective-permute-start(bf16[9,8,256]{2,1,0:T(8,128)(2,1)S(1)} %get-tuple-element.25.refs_0_.packed), channel_id=1, source_target_pairs={{0,12},{1,13},{2,14},{3,15},{4,0},{5,1},{6,2},{7,3},{8,4},{9,5},{1... | collective-permute-start | bytes 110600 | tf_op jit(solution)/shard_map/ppermute | solution.py:207
  6.8 0.0 collective-permute-done
  6.8 0.9 %collective-permute-start.3 = (bf16[1,8,128]{2,1,0:T(8,128)(2,1)S(1)}, bf16[1,8,128]{2,1,0:T(8,128)(2,1)S(1)}, u32[]{:S(2)}, u32[]{:S(2)}) collective-permute-start(bf16[1,8,128]{2,1,0:T(8,128)(2,1)S(1)} %collective-permute-done), channel_id=1, source_target_pairs={{0,9},{1,8},{2,11},{3,10},{4,13},{5,12},{6,15},{7,14},{8,1},{9,0},... | collective-permute-start | bytes 6152 | tf_op jit(solution)/shard_map/ppermute | solution.py:207
  7.7 0.0 copy-done
  7.7 0.0 copy-done.1
  7.7 2.0 %shard_map.111 = (bf16[8,4,256,256]{3,2,1,0:T(8,128)(2,1)S(1)}, f32[8,8,256]{2,1,0:T(8,128)S(1)}, bf16[8,128,256]{2,1,0:T(8,128)(2,1)S(1)}, f32[8,256]{1,0:T(8,128)S(1)}, bf16[4,128,64]{2,1,0:T(8,128)(2,1)S(1)}) custom-call(bf16[9,8,256]{2,1,0:T(8,128)(2,1)S(1)} %get-tuple-element.25.refs_0_.packed, bf16[8,6,256,256]{3,2,1,0:T(8,128)(2,1)S(1)} %copy-done, ...), custom_call_target="tpu_custom_call" | custom-call | flops 2000000000 | tf_op jit(solution)/shard_map/pallas_call | solution.py:245
  9.7 0.0 collective-permute-done.1.low
  9.8 0.0 collective-permute-done.2.high
  9.8 1.3 %shard_map.112.near = f32[8,8,256]{2,1,0:T(8,128)S(1)} custom-call(s32[8,6]{1,0:T(8,128)S(1)} %get-tuple-element.29.places, bf16[9,8,256]{2,1,0:T(8,128)(2,1)S(1)} %get-tuple-element.25.refs_0_.packed, bf16[9,8,256]{2,1,0:T(8,128)(2,1)S(1)} %collective-permute-done.1.low, bf16[9,8,256]{2,1,0:T(8,128)(2,1)S(1)} %collective-permute-done.2.high, ...), custom_call_target="tpu_custom_call" | custom-call | flops 1000000 | tf_op jit(solution)/shard_map/pallas_call | solution.py:263
  11.1 0.0 collective-permute-done.3.refs_0_
  11.1 1.0 %shard_map.113 = f32[8,8,256]{2,1,0:T(8,128)} custom-call(bf16[4,128,64]{2,1,0:T(8,128)(2,1)S(1)} %get-tuple-element.28.sources, f32[8,8,256]{2,1,0:T(8,128)S(1)} %shard_map.112.near, f32[8,256]{1,0:T(8,128)S(1)} %get-tuple-element.32.live, f32[8,256]{1,0:T(8,128)S(1)} %get-tuple-element.33.back, bf16[8,128,256]{2,1,0:T(8,128)(2,1)S(1)} %get-tuple-element.34.apply, ...), custom_call_target="tpu_custom_call" | custom-call | flops 2000000000 | tf_op jit(solution)/shard_map/pallas_call | solution.py:266
Async XLA Ops:
  0.0 1.3 %copy-start.2 = (bf16[8,256,216]{1,2,0:T(8,128)(2,1)S(1)}, bf16[8,256,216]{1,2,0:T(8,128)(2,1)}, u32[]{:S(2)}) copy-start(bf16[8,256,216]{1,2,0:T(8,128)(2,1)} %param.16) | copy-start | bytes 2654212
  1.1 6.6 %copy-start = (bf16[8,6,256,256]{3,2,1,0:T(8,128)(2,1)S(1)}, bf16[8,6,256,256]{3,2,1,0:T(8,128)(2,1)}, u32[]{:S(2)}) copy-start(bf16[8,6,256,256]{3,2,1,0:T(8,128)(2,1)} %tiles.1) | copy-start | bytes 18874372
  1.1 6.6 %copy-start.1 = (bf16[8,256,256]{2,1,0:T(8,128)(2,1)S(1)}, bf16[8,256,256]{2,1,0:T(8,128)(2,1)}, u32[]{:S(2)}) copy-start(bf16[8,256,256]{2,1,0:T(8,128)(2,1)} %jacobi.1) | copy-start | bytes 3145732
  1.9 4.9 %collective-permute-start = (bf16[1,8,128]{2,1,0:T(8,128)(2,1)S(1)}, bf16[1,8,128]{2,1,0:T(8,128)(2,1)S(1)}, u32[]{:S(2)}, u32[]{:S(2)}) collective-permute-start(bf16[1,8,128]{2,1,0:T(8,128)(2,1)S(1)} %get-tuple-element.24.box), channel_id=1, source_target_pairs={{0,1},{1,0},{2,3},{3,2},{4,5},{5,4},{6,7},{7,6},{8,9},{9,8},{10,11... | collective-permute-start | bytes 6152 | tf_op jit(solution)/shard_map/ppermute | solution.py:207
  2.0 7.7 %collective-permute-start.1 = (bf16[9,8,256]{2,1,0:T(8,128)(2,1)S(1)}, bf16[9,8,256]{2,1,0:T(8,128)(2,1)S(1)}, u32[]{:S(2)}, u32[]{:S(2)}) collective-permute-start(bf16[9,8,256]{2,1,0:T(8,128)(2,1)S(1)} %get-tuple-element.25.refs_0_.packed), channel_id=1, source_target_pairs={{0,4},{1,5},{2,6},{3,7},{4,8},{5,9},{6,10},{7,11},{8,12},{9,13},{1... | collective-permute-start | bytes 110600 | tf_op jit(solution)/shard_map/ppermute | solution.py:207
  4.8 5.0 %collective-permute-start.2 = (bf16[9,8,256]{2,1,0:T(8,128)(2,1)S(1)}, bf16[9,8,256]{2,1,0:T(8,128)(2,1)S(1)}, u32[]{:S(2)}, u32[]{:S(2)}) collective-permute-start(bf16[9,8,256]{2,1,0:T(8,128)(2,1)S(1)} %get-tuple-element.25.refs_0_.packed), channel_id=1, source_target_pairs={{0,12},{1,13},{2,14},{3,15},{4,0},{5,1},{6,2},{7,3},{8,4},{9,5},{1... | collective-permute-start | bytes 110600 | tf_op jit(solution)/shard_map/ppermute | solution.py:207
  6.8 4.3 %collective-permute-start.3 = (bf16[1,8,128]{2,1,0:T(8,128)(2,1)S(1)}, bf16[1,8,128]{2,1,0:T(8,128)(2,1)S(1)}, u32[]{:S(2)}, u32[]{:S(2)}) collective-permute-start(bf16[1,8,128]{2,1,0:T(8,128)(2,1)S(1)} %collective-permute-done), channel_id=1, source_target_pairs={{0,9},{1,8},{2,11},{3,10},{4,13},{5,12},{6,15},{7,14},{8,1},{9,0},... | collective-permute-start | bytes 6152 | tf_op jit(solution)/shard_map/ppermute | solution.py:207

commit v8 on v7

--- a/solution.py
+++ b/solution.py
@@ -125,11 +125,12 @@
     for copy in copies:
         copy.start()
     comp = comp_t[...]
-    for leaf in range(leaves):
-        top = jnp.max(jnp.abs(jacobi[leaf]).astype(F32), axis=(0, 1), keepdims=True)
-        scale = jnp.where(top > 2.0**90, 2.0**-30, jnp.where(top < 2.0**-90, 2.0**30, 1.0))
-        back[leaf : leaf + 1] = jnp.broadcast_to(1.0 / scale, (1, back.shape[1]))
-        expand[leaf] = halves(nn(comp, interp_t[leaf]) * scale)
+    tops = [jnp.max(jnp.abs(jacobi[leaf]), axis=0, keepdims=True).astype(F32) for leaf in range(leaves)]
+    top = jnp.max(jnp.concatenate(tops, axis=0), axis=1, keepdims=True)
+    scale = jnp.where(top > 2.0**90, 2.0**-30, jnp.where(top < 2.0**-90, 2.0**30, 1.0))
+    back[...] = jnp.broadcast_to(1.0 / scale, back.shape)
+    for leaf in range(leaves):
+        expand[leaf] = halves(nn(comp, interp_t[leaf]) * scale[leaf : leaf + 1])
     for leaf in range(leaves):
         first[leaf] = nt(packed[leaf], tiles[leaf, 0])
         for k in range(turned.shape[1]):

time: 12.3 us -> 12.2 us (level)
  the two profiles are of different devices: /device:TPU:1 before, /device:TPU:0 now
where the time goes in v8:
time: 12.2 us; the launch traced here: 12 us
  Pallas kernels  6.03 us (49%)
  starting transfers between devices  5.65 us (46%)
  local copies, waits for them, and re-layouts  0.19 us (2%)
    ppermute x4, starting transfers between devices, permute(): return lax.ppermute(value, ('leaf', 'chan'), moves)  5.65 us
    pallas_call x1, Pallas kernels, body(): call(bound(prepare_kernel), (shape((leaves, AHEAD, unknowns, unknowns), B...  1.94 us
    pallas_call x1, Pallas kernels, body(): call(near_kernel, part, [VMEM] * 8, [pltpu.VMEM((3 * leaves, combos, unkn...  1.35 us
    pallas_call x1, Pallas kernels, body(): call(bound(load_kernel), (part, shape((leaves, unknowns), F32), shape((ra...  1.1 us
    pallas_call x1, Pallas kernels, body(): call(final_kernel, shape(currents.shape, F32), [VMEM] * (8 + len(further)))  1.01 us
    pallas_call x1, Pallas kernels, body(): call(box_kernel, (shape((leaves + 1, combos, unknowns), BF16), shape((1,...  0.63 us
  transfers between devices with their start and end apart: 4, of which 1 were waited for; matrix products, arithmetic and copies ran while one was open for 0% of the time, Pallas kernels for 27%

profile of v8, /device:TPU:0, one launch (start us, length us, event | category | flops | bytes accessed | tf_op | source)
XLA Modules:
  0.0 12.0 jit_solution(2385172667730156425)
XLA Ops:
  0.0 0.0 copy-start.2
  0.0 1.1 %shard_map.109 = (f32[8,8,256]{2,1,0:T(8,128)S(1)}, f32[8,256]{1,0:T(8,128)S(1)}, bf16[64,216]{1,0:T(8,128)(2,1)S(1)}, bf16[8,64,64]{2,1,0:T(8,128)(2,1)S(1)}, s...) custom-call(s32[8]{0:T(128)} %refs_0_.1, bf16[8,8,256]{2,1,0:T(8,128)(2,1)} %refs_1_.2, ...), custom_call_target="tpu_custom_call" | custom-call | flops 2000000000 | tf_op jit(solution)/shard_map/pallas_call | solution.py:214
  1.1 0.0 copy-start
  1.1 0.0 copy-start.1
  1.1 0.2 %copy-done.2 = bf16[8,256,216]{1,2,0:T(8,128)(2,1)S(1)} copy-done((bf16[8,256,216]{1,2,0:T(8,128)(2,1)S(1)}, bf16[8,256,216]{1,2,0:T(8,128)(2,1)}, u32[]{:S(2)}) %copy-start.2) | copy-done | bytes 884760
  1.3 0.6 %shard_map.110 = (bf16[9,8,256]{2,1,0:T(8,128)(2,1)S(1)}, bf16[1,8,128]{2,1,0:T(8,128)(2,1)S(1)}) custom-call(f32[8,8,256]{2,1,0:T(8,128)S(1)} %get-tuple-element.20.mine, bf16[8,216,256]{2,1,0:T(8,128)(2,1)S(1)} %bitcast.2, bf16[64,216]{1,0:T(8,128)(2,1)S(1)} %get-tuple-element.21.comp_t.refs_3_, bf16[8,64,64]{2,1,0:T(8,128)(2,1)S(1)} %get-tuple-element.22.m2m.refs_4_), custom_call_target="tpu_custom_call" | custom-call | flops 2000000000 | tf_op jit(solution)/shard_map/pallas_call | solution.py:234
  1.9 0.5 %collective-permute-start = (bf16[1,8,128]{2,1,0:T(8,128)(2,1)S(1)}, bf16[1,8,128]{2,1,0:T(8,128)(2,1)S(1)}, u32[]{:S(2)}, u32[]{:S(2)}) collective-permute-start(bf16[1,8,128]{2,1,0:T(8,128)(2,1)S(1)} %get-tuple-element.24.box), channel_id=1, source_target_pairs={{0,1},{1,0},{2,3},{3,2},{4,5},{5,4},{6,7},{7,6},{8,9},{9,8},{10,11... | collective-permute-start | bytes 6152 | tf_op jit(solution)/shard_map/ppermute | solution.py:208
  2.4 2.6 %collective-permute-start.1 = (bf16[9,8,256]{2,1,0:T(8,128)(2,1)S(1)}, bf16[9,8,256]{2,1,0:T(8,128)(2,1)S(1)}, u32[]{:S(2)}, u32[]{:S(2)}) collective-permute-start(bf16[9,8,256]{2,1,0:T(8,128)(2,1)S(1)} %get-tuple-element.25.refs_0_.packed), channel_id=1, source_target_pairs={{0,4},{1,5},{2,6},{3,7},{4,8},{5,9},{6,10},{7,11},{8,12},{9,13},{1... | collective-permute-start | bytes 110600 | tf_op jit(solution)/shard_map/ppermute | solution.py:208
  5.0 2.1 %collective-permute-start.2 = (bf16[9,8,256]{2,1,0:T(8,128)(2,1)S(1)}, bf16[9,8,256]{2,1,0:T(8,128)(2,1)S(1)}, u32[]{:S(2)}, u32[]{:S(2)}) collective-permute-start(bf16[9,8,256]{2,1,0:T(8,128)(2,1)S(1)} %get-tuple-element.25.refs_0_.packed), channel_id=1, source_target_pairs={{0,12},{1,13},{2,14},{3,15},{4,0},{5,1},{6,2},{7,3},{8,4},{9,5},{1... | collective-permute-start | bytes 110600 | tf_op jit(solution)/shard_map/ppermute | solution.py:208
  7.1 0.0 collective-permute-done
  7.1 0.5 %collective-permute-start.3 = (bf16[1,8,128]{2,1,0:T(8,128)(2,1)S(1)}, bf16[1,8,128]{2,1,0:T(8,128)(2,1)S(1)}, u32[]{:S(2)}, u32[]{:S(2)}) collective-permute-start(bf16[1,8,128]{2,1,0:T(8,128)(2,1)S(1)} %collective-permute-done), channel_id=1, source_target_pairs={{0,9},{1,8},{2,11},{3,10},{4,13},{5,12},{6,15},{7,14},{8,1},{9,0},... | collective-permute-start | bytes 6152 | tf_op jit(solution)/shard_map/ppermute | solution.py:208
  7.6 0.0 copy-done
  7.6 0.0 copy-done.1
  7.6 1.9 %shard_map.111 = (bf16[8,4,256,256]{3,2,1,0:T(8,128)(2,1)S(1)}, f32[8,8,256]{2,1,0:T(8,128)S(1)}, bf16[8,128,256]{2,1,0:T(8,128)(2,1)S(1)}, f32[8,256]{1,0:T(8,128)S(1)}, bf16[4,128,64]{2,1,0:T(8,128)(2,1)S(1)}) custom-call(bf16[9,8,256]{2,1,0:T(8,128)(2,1)S(1)} %get-tuple-element.25.refs_0_.packed, bf16[8,6,256,256]{3,2,1,0:T(8,128)(2,1)S(1)} %copy-done, ...), custom_call_target="tpu_custom_call" | custom-call | flops 2000000000 | tf_op jit(solution)/shard_map/pallas_call | solution.py:246
  9.6 0.0 collective-permute-done.1.low
  9.6 0.0 collective-permute-done.2.high
  9.6 1.3 %shard_map.112.near = f32[8,8,256]{2,1,0:T(8,128)S(1)} custom-call(s32[8,6]{1,0:T(8,128)S(1)} %get-tuple-element.29.places, bf16[9,8,256]{2,1,0:T(8,128)(2,1)S(1)} %get-tuple-element.25.refs_0_.packed, bf16[9,8,256]{2,1,0:T(8,128)(2,1)S(1)} %collective-permute-done.1.low, bf16[9,8,256]{2,1,0:T(8,128)(2,1)S(1)} %collective-permute-done.2.high, ...), custom_call_target="tpu_custom_call" | custom-call | flops 1000000 | tf_op jit(solution)/shard_map/pallas_call | solution.py:264
  10.9 0.1 collective-permute-done.3.refs_0_
  11.0 1.0 %shard_map.113 = f32[8,8,256]{2,1,0:T(8,128)} custom-call(bf16[4,128,64]{2,1,0:T(8,128)(2,1)S(1)} %get-tuple-element.28.sources, f32[8,8,256]{2,1,0:T(8,128)S(1)} %shard_map.112.near, f32[8,256]{1,0:T(8,128)S(1)} %get-tuple-element.32.live, f32[8,256]{1,0:T(8,128)S(1)} %get-tuple-element.33.back, bf16[8,128,256]{2,1,0:T(8,128)(2,1)S(1)} %get-tuple-element.34.apply, ...), custom_call_target="tpu_custom_call" | custom-call | flops 2000000000 | tf_op jit(solution)/shard_map/pallas_call | solution.py:267
Async XLA Ops:
  0.0 1.3 %copy-start.2 = (bf16[8,256,216]{1,2,0:T(8,128)(2,1)S(1)}, bf16[8,256,216]{1,2,0:T(8,128)(2,1)}, u32[]{:S(2)}) copy-start(bf16[8,256,216]{1,2,0:T(8,128)(2,1)} %param.16) | copy-start | bytes 2654212
  1.1 6.5 %copy-start = (bf16[8,6,256,256]{3,2,1,0:T(8,128)(2,1)S(1)}, bf16[8,6,256,256]{3,2,1,0:T(8,128)(2,1)}, u32[]{:S(2)}) copy-start(bf16[8,6,256,256]{3,2,1,0:T(8,128)(2,1)} %tiles.1) | copy-start | bytes 18874372
  1.1 6.5 %copy-start.1 = (bf16[8,256,256]{2,1,0:T(8,128)(2,1)S(1)}, bf16[8,256,256]{2,1,0:T(8,128)(2,1)}, u32[]{:S(2)}) copy-start(bf16[8,256,256]{2,1,0:T(8,128)(2,1)} %jacobi.1) | copy-start | bytes 3145732
  1.9 5.1 %collective-permute-start = (bf16[1,8,128]{2,1,0:T(8,128)(2,1)S(1)}, bf16[1,8,128]{2,1,0:T(8,128)(2,1)S(1)}, u32[]{:S(2)}, u32[]{:S(2)}) collective-permute-start(bf16[1,8,128]{2,1,0:T(8,128)(2,1)S(1)} %get-tuple-element.24.box), channel_id=1, source_target_pairs={{0,1},{1,0},{2,3},{3,2},{4,5},{5,4},{6,7},{7,6},{8,9},{9,8},{10,11... | collective-permute-start | bytes 6152 | tf_op jit(solution)/shard_map/ppermute | solution.py:208
  2.4 7.1 %collective-permute-start.1 = (bf16[9,8,256]{2,1,0:T(8,128)(2,1)S(1)}, bf16[9,8,256]{2,1,0:T(8,128)(2,1)S(1)}, u32[]{:S(2)}, u32[]{:S(2)}) collective-permute-start(bf16[9,8,256]{2,1,0:T(8,128)(2,1)S(1)} %get-tuple-element.25.refs_0_.packed), channel_id=1, source_target_pairs={{0,4},{1,5},{2,6},{3,7},{4,8},{5,9},{6,10},{7,11},{8,12},{9,13},{1... | collective-permute-start | bytes 110600 | tf_op jit(solution)/shard_map/ppermute | solution.py:208
  5.0 4.6 %collective-permute-start.2 = (bf16[9,8,256]{2,1,0:T(8,128)(2,1)S(1)}, bf16[9,8,256]{2,1,0:T(8,128)(2,1)S(1)}, u32[]{:S(2)}, u32[]{:S(2)}) collective-permute-start(bf16[9,8,256]{2,1,0:T(8,128)(2,1)S(1)} %get-tuple-element.25.refs_0_.packed), channel_id=1, source_target_pairs={{0,12},{1,13},{2,14},{3,15},{4,0},{5,1},{6,2},{7,3},{8,4},{9,5},{1... | collective-permute-start | bytes 110600 | tf_op jit(solution)/shard_map/ppermute | solution.py:208
  7.1 3.9 %collective-permute-start.3 = (bf16[1,8,128]{2,1,0:T(8,128)(2,1)S(1)}, bf16[1,8,128]{2,1,0:T(8,128)(2,1)S(1)}, u32[]{:S(2)}, u32[]{:S(2)}) collective-permute-start(bf16[1,8,128]{2,1,0:T(8,128)(2,1)S(1)} %collective-permute-done), channel_id=1, source_target_pairs={{0,9},{1,8},{2,11},{3,10},{4,13},{5,12},{6,15},{7,14},{8,1},{9,0},... | collective-permute-start | bytes 6152 | tf_op jit(solution)/shard_map/ppermute | solution.py:208

commit v9 on v8

--- a/solution.py
+++ b/solution.py
@@ -12,7 +12,7 @@
 HBM = pl.BlockSpec(memory_space=pltpu.HBM)
 INC = 8
 COST = 2 * 10**9
-AHEAD = 4
+AHEAD = 3
 KCOST = 2000000000
 PCOST = 2000000000
 NCOST = 1000000
@@ -164,7 +164,7 @@
             if k <= ahead:
                 total = total + nn(x, turned[leaf, k - 1])
             else:
-                total = total + nt(x, tiles[leaf, k])
+                total = total + nt(tiles[leaf, k], x).T
         sums.append(halves(total))
     for leaf in range(leaves):
         near[leaf] = halves_sum(nt(sums[leaf], jacobi[leaf]))

time: 12.2 us -> 12.1 us (level)
  waiting for transfers between devices: 0.07 us -> 0.5 us
  Pallas kernels: 6.03 us -> 5.61 us
    ppermute x4, waiting for transfers between devices: 0.07 us -> 0.5 us  [permute(): return lax.ppermute(value, ('leaf', 'chan'), moves)]
    pallas_call x1, Pallas kernels: 1.94 us -> 1.68 us  [body(): call(bound(prepare_kernel), (shape((leaves, AHEAD, unknowns, unknowns), B...]
    pallas_call x1, Pallas kernels: 1.35 us -> 1.19 us  [body(): call(near_kernel, part, [VMEM] * 8, [pltpu.VMEM((3 * leaves, combos, unkn...]
  transfers between devices with their start and end apart: 4 -> 4, of which waited for: 1 -> 2; matrix products, arithmetic and copies ran while one was open for 0% -> 0% of each run, Pallas kernels for 27% -> 24%
where the time goes in v9:
time: 12.1 us; the launch traced here: 12 us
  starting transfers between devices  5.65 us (47%)
  Pallas kernels  5.61 us (46%)
  waiting for transfers between devices  0.5 us (4%)
  local copies, waits for them, and re-layouts  0.19 us (2%)
    ppermute x4, starting transfers between devices, permute(): return lax.ppermute(value, ('leaf', 'chan'), moves)  5.65 us
    pallas_call x1, Pallas kernels, body(): call(bound(prepare_kernel), (shape((leaves, AHEAD, unknowns, unknowns), B...  1.68 us
    pallas_call x1, Pallas kernels, body(): call(near_kernel, part, [VMEM] * 8, [pltpu.VMEM((3 * leaves, combos, unkn...  1.19 us
    pallas_call x1, Pallas kernels, body(): call(bound(load_kernel), (part, shape((leaves, unknowns), F32), shape((ra...  1.1 us
    pallas_call x1, Pallas kernels, body(): call(final_kernel, shape(currents.shape, F32), [VMEM] * (8 + len(further)))  1.01 us
    pallas_call x1, Pallas kernels, body(): call(box_kernel, (shape((leaves + 1, combos, unknowns), BF16), shape((1,...  0.63 us
    ppermute x4, waiting for transfers between devices, permute(): return lax.ppermute(value, ('leaf', 'chan'), moves)  0.5 us
  transfers between devices with their start and end apart: 4, of which 2 were waited for; matrix products, arithmetic and copies ran while one was open for 0% of the time, Pallas kernels for 24%

profile of v9, /device:TPU:0, one launch (start us, length us, event | category | flops | bytes accessed | tf_op | source)
XLA Modules:
  0.0 12.0 jit_solution(4317031726004887573)
XLA Ops:
  0.0 0.0 copy-start.2
  0.0 1.1 %shard_map.109 = (f32[8,8,256]{2,1,0:T(8,128)S(1)}, f32[8,256]{1,0:T(8,128)S(1)}, bf16[64,216]{1,0:T(8,128)(2,1)S(1)}, bf16[8,64,64]{2,1,0:T(8,128)(2,1)S(1)}, s...) custom-call(s32[8]{0:T(128)} %refs_0_.1, bf16[8,8,256]{2,1,0:T(8,128)(2,1)} %refs_1_.2, ...), custom_call_target="tpu_custom_call" | custom-call | flops 2000000000 | tf_op jit(solution)/shard_map/pallas_call | solution.py:214
  1.1 0.0 copy-start
  1.1 0.0 copy-start.1
  1.1 0.2 %copy-done.2 = bf16[8,256,216]{1,2,0:T(8,128)(2,1)S(1)} copy-done((bf16[8,256,216]{1,2,0:T(8,128)(2,1)S(1)}, bf16[8,256,216]{1,2,0:T(8,128)(2,1)}, u32[]{:S(2)}) %copy-start.2) | copy-done | bytes 884760
  1.3 0.6 %shard_map.110 = (bf16[9,8,256]{2,1,0:T(8,128)(2,1)S(1)}, bf16[1,8,128]{2,1,0:T(8,128)(2,1)S(1)}) custom-call(f32[8,8,256]{2,1,0:T(8,128)S(1)} %get-tuple-element.20.mine, bf16[8,216,256]{2,1,0:T(8,128)(2,1)S(1)} %bitcast.2, bf16[64,216]{1,0:T(8,128)(2,1)S(1)} %get-tuple-element.21.comp_t.refs_3_, bf16[8,64,64]{2,1,0:T(8,128)(2,1)S(1)} %get-tuple-element.22.m2m.refs_4_), custom_call_target="tpu_custom_call" | custom-call | flops 2000000000 | tf_op jit(solution)/shard_map/pallas_call | solution.py:234
  1.9 0.5 %collective-permute-start = (bf16[1,8,128]{2,1,0:T(8,128)(2,1)S(1)}, bf16[1,8,128]{2,1,0:T(8,128)(2,1)S(1)}, u32[]{:S(2)}, u32[]{:S(2)}) collective-permute-start(bf16[1,8,128]{2,1,0:T(8,128)(2,1)S(1)} %get-tuple-element.24.box), channel_id=1, source_target_pairs={{0,1},{1,0},{2,3},{3,2},{4,5},{5,4},{6,7},{7,6},{8,9},{9,8},{10,11... | collective-permute-start | bytes 6152 | tf_op jit(solution)/shard_map/ppermute | solution.py:208
  2.4 2.6 %collective-permute-start.1 = (bf16[9,8,256]{2,1,0:T(8,128)(2,1)S(1)}, bf16[9,8,256]{2,1,0:T(8,128)(2,1)S(1)}, u32[]{:S(2)}, u32[]{:S(2)}) collective-permute-start(bf16[9,8,256]{2,1,0:T(8,128)(2,1)S(1)} %get-tuple-element.25.refs_0_.packed), channel_id=1, source_target_pairs={{0,4},{1,5},{2,6},{3,7},{4,8},{5,9},{6,10},{7,11},{8,12},{9,13},{1... | collective-permute-start | bytes 110600 | tf_op jit(solution)/shard_map/ppermute | solution.py:208
  5.0 2.1 %collective-permute-start.2 = (bf16[9,8,256]{2,1,0:T(8,128)(2,1)S(1)}, bf16[9,8,256]{2,1,0:T(8,128)(2,1)S(1)}, u32[]{:S(2)}, u32[]{:S(2)}) collective-permute-start(bf16[9,8,256]{2,1,0:T(8,128)(2,1)S(1)} %get-tuple-element.25.refs_0_.packed), channel_id=1, source_target_pairs={{0,12},{1,13},{2,14},{3,15},{4,0},{5,1},{6,2},{7,3},{8,4},{9,5},{1... | collective-permute-start | bytes 110600 | tf_op jit(solution)/shard_map/ppermute | solution.py:208
  7.1 0.0 collective-permute-done
  7.1 0.5 %collective-permute-start.3 = (bf16[1,8,128]{2,1,0:T(8,128)(2,1)S(1)}, bf16[1,8,128]{2,1,0:T(8,128)(2,1)S(1)}, u32[]{:S(2)}, u32[]{:S(2)}) collective-permute-start(bf16[1,8,128]{2,1,0:T(8,128)(2,1)S(1)} %collective-permute-done), channel_id=1, source_target_pairs={{0,9},{1,8},{2,11},{3,10},{4,13},{5,12},{6,15},{7,14},{8,1},{9,0},... | collective-permute-start | bytes 6152 | tf_op jit(solution)/shard_map/ppermute | solution.py:208
  7.6 0.0 copy-done
  7.6 0.0 copy-done.1
  7.6 1.7 %shard_map.111 = (bf16[8,3,256,256]{3,2,1,0:T(8,128)(2,1)S(1)}, f32[8,8,256]{2,1,0:T(8,128)S(1)}, bf16[8,128,256]{2,1,0:T(8,128)(2,1)S(1)}, f32[8,256]{1,0:T(8,128)S(1)}, bf16[4,128,64]{2,1,0:T(8,128)(2,1)S(1)}) custom-call(bf16[9,8,256]{2,1,0:T(8,128)(2,1)S(1)} %get-tuple-element.25.refs_0_.packed, bf16[8,6,256,256]{3,2,1,0:T(8,128)(2,1)S(1)} %copy-done, ...), custom_call_target="tpu_custom_call" | custom-call | flops 2000000000 | tf_op jit(solution)/shard_map/pallas_call | solution.py:246
  9.3 0.0 collective-permute-done.1.low
  9.3 0.3 %collective-permute-done.2.high = bf16[9,8,256]{2,1,0:T(8,128)(2,1)S(1)} collective-permute-done((bf16[9,8,256]{2,1,0:T(8,128)(2,1)S(1)}, bf16[9,8,256]{2,1,0:T(8,128)(2,1)S(1)}, u32[]{:S(2)}, u32[]{:S(2)}) %collective-permute-start.2) | collective-permute-done | bytes 36896 | tf_op jit(solution)/shard_map/ppermute | solution.py:208
  9.6 1.2 %shard_map.112.near = f32[8,8,256]{2,1,0:T(8,128)S(1)} custom-call(s32[8,6]{1,0:T(8,128)S(1)} %get-tuple-element.29.places, bf16[9,8,256]{2,1,0:T(8,128)(2,1)S(1)} %get-tuple-element.25.refs_0_.packed, bf16[9,8,256]{2,1,0:T(8,128)(2,1)S(1)} %collective-permute-done.1.low, bf16[9,8,256]{2,1,0:T(8,128)(2,1)S(1)} %collective-permute-done.2.high, ...), custom_call_target="tpu_custom_call" | custom-call | flops 1000000 | tf_op jit(solution)/shard_map/pallas_call | solution.py:264
  10.8 0.2 %collective-permute-done.3.refs_0_ = bf16[1,8,128]{2,1,0:T(8,128)(2,1)S(1)} collective-permute-done((bf16[1,8,128]{2,1,0:T(8,128)(2,1)S(1)}, bf16[1,8,128]{2,1,0:T(8,128)(2,1)S(1)}, u32[]{:S(2)}, u32[]{:S(2)}) %collective-permute-start.3) | collective-permute-done | bytes 2080 | tf_op jit(solution)/shard_map/ppermute | solution.py:208
  11.0 1.0 %shard_map.113 = f32[8,8,256]{2,1,0:T(8,128)} custom-call(bf16[4,128,64]{2,1,0:T(8,128)(2,1)S(1)} %get-tuple-element.28.sources, f32[8,8,256]{2,1,0:T(8,128)S(1)} %shard_map.112.near, f32[8,256]{1,0:T(8,128)S(1)} %get-tuple-element.32.live, f32[8,256]{1,0:T(8,128)S(1)} %get-tuple-element.33.back, bf16[8,128,256]{2,1,0:T(8,128)(2,1)S(1)} %get-tuple-element.34.apply, ...), custom_call_target="tpu_custom_call" | custom-call | flops 2000000000 | tf_op jit(solution)/shard_map/pallas_call | solution.py:267
Async XLA Ops:
  0.0 1.3 %copy-start.2 = (bf16[8,256,216]{1,2,0:T(8,128)(2,1)S(1)}, bf16[8,256,216]{1,2,0:T(8,128)(2,1)}, u32[]{:S(2)}) copy-start(bf16[8,256,216]{1,2,0:T(8,128)(2,1)} %param.16) | copy-start | bytes 2654212
  1.1 6.5 %copy-start = (bf16[8,6,256,256]{3,2,1,0:T(8,128)(2,1)S(1)}, bf16[8,6,256,256]{3,2,1,0:T(8,128)(2,1)}, u32[]{:S(2)}) copy-start(bf16[8,6,256,256]{3,2,1,0:T(8,128)(2,1)} %tiles.1) | copy-start | bytes 18874372
  1.1 6.5 %copy-start.1 = (bf16[8,256,256]{2,1,0:T(8,128)(2,1)S(1)}, bf16[8,256,256]{2,1,0:T(8,128)(2,1)}, u32[]{:S(2)}) copy-start(bf16[8,256,256]{2,1,0:T(8,128)(2,1)} %jacobi.1) | copy-start | bytes 3145732
  1.9 5.1 %collective-permute-start = (bf16[1,8,128]{2,1,0:T(8,128)(2,1)S(1)}, bf16[1,8,128]{2,1,0:T(8,128)(2,1)S(1)}, u32[]{:S(2)}, u32[]{:S(2)}) collective-permute-start(bf16[1,8,128]{2,1,0:T(8,128)(2,1)S(1)} %get-tuple-element.24.box), channel_id=1, source_target_pairs={{0,1},{1,0},{2,3},{3,2},{4,5},{5,4},{6,7},{7,6},{8,9},{9,8},{10,11... | collective-permute-start | bytes 6152 | tf_op jit(solution)/shard_map/ppermute | solution.py:208
  2.4 6.9 %collective-permute-start.1 = (bf16[9,8,256]{2,1,0:T(8,128)(2,1)S(1)}, bf16[9,8,256]{2,1,0:T(8,128)(2,1)S(1)}, u32[]{:S(2)}, u32[]{:S(2)}) collective-permute-start(bf16[9,8,256]{2,1,0:T(8,128)(2,1)S(1)} %get-tuple-element.25.refs_0_.packed), channel_id=1, source_target_pairs={{0,4},{1,5},{2,6},{3,7},{4,8},{5,9},{6,10},{7,11},{8,12},{9,13},{1... | collective-permute-start | bytes 110600 | tf_op jit(solution)/shard_map/ppermute | solution.py:208
  5.0 4.6 %collective-permute-start.2 = (bf16[9,8,256]{2,1,0:T(8,128)(2,1)S(1)}, bf16[9,8,256]{2,1,0:T(8,128)(2,1)S(1)}, u32[]{:S(2)}, u32[]{:S(2)}) collective-permute-start(bf16[9,8,256]{2,1,0:T(8,128)(2,1)S(1)} %get-tuple-element.25.refs_0_.packed), channel_id=1, source_target_pairs={{0,12},{1,13},{2,14},{3,15},{4,0},{5,1},{6,2},{7,3},{8,4},{9,5},{1... | collective-permute-start | bytes 110600 | tf_op jit(solution)/shard_map/ppermute | solution.py:208
  7.1 3.9 %collective-permute-start.3 = (bf16[1,8,128]{2,1,0:T(8,128)(2,1)S(1)}, bf16[1,8,128]{2,1,0:T(8,128)(2,1)S(1)}, u32[]{:S(2)}, u32[]{:S(2)}) collective-permute-start(bf16[1,8,128]{2,1,0:T(8,128)(2,1)S(1)} %collective-permute-done), channel_id=1, source_target_pairs={{0,9},{1,8},{2,11},{3,10},{4,13},{5,12},{6,15},{7,14},{8,1},{9,0},... | collective-permute-start | bytes 6152 | tf_op jit(solution)/shard_map/ppermute | solution.py:208
